TPU v7x, 32 devices: a whole 2x2x4 slice. The times are simulated.
32 devices in a mesh: groups: 2 (over x), layer: 8 (over z, y), loop: 2 (over core).
Axes of the slice: x: 2, y: 2, z: 4, core: 2. Of those that a mesh axis runs over, the one named last changes fastest.
Arguments:
- acts: bfloat16 [8, 1536, 2048], P('layer', ('groups', 'loop')), parts along dimension 1, may hold values from -6 to 6
- grads: bfloat16 [8, 1536, 7168], P('layer', ('groups', 'loop')), parts along dimension 1, may hold values from -6 to 6
- act_factors: bfloat16 [8, 2048, 512], P('layer', None, 'loop'), may hold values from -0.0008544922 to 0.0008544922
- grad_factors: bfloat16 [8, 7168, 512], P('layer', None, 'loop'), may hold values from -0.03125 to 0.03125
- lengths: int32 [16], P(('groups', 'loop')), parts along dimension 0, may hold values from 1 to 96, 480 in all
Outputs:
- scores: float32 [16, 16], P('groups'), parts along dimension 0
There are 2 independent parts, one for each index of `groups`. A program takes and returns all parts, laid end to end along the dimension named above; an argument that names none is the same for every part. Nothing has to cross between parts.
Inputs may be any that keep to these rules, and one draw needn't show every extreme that they name: The lengths of one group sum to 480, and the largest is 96.
All inputs are finite; a program needn't handle non-finite values.
Results may differ from a plain program's by a relative error of at most 0.0003.
Values may be sent and summed in bfloat16 or wider, within the bound.
No kernel may reach another device: no remote copies, remote signals or barrier semaphores. Data moves between devices by JAX's collectives and lax.ppermute only.
A program may use at most 64 MiB of HBM per device.

v0:
```python
import jax
import jax.numpy as jnp
from jax import lax
from jax.sharding import PartitionSpec as P

RANK = 32


def shifted(value, axis, by):
    length = lax.axis_size(axis)
    return lax.ppermute(value, axis, [(i, (i + by) % length) for i in range(length)])


def from_partner(value, axis, apart):
    mask = 2**apart
    pairs = [(source, source ^ mask) for source in range(lax.axis_size(axis))]
    return lax.ppermute(value, axis, pairs)


def project_rows(rows, factor):
    return lax.dot_general(
        factor, rows, (((0,), (1,)), ((), ())), preferred_element_type=jnp.float32
    )


def split_rank(projected, query_count):
    return projected.reshape(query_count, 2, 2, RANK // 4, projected.shape[1])


def pick_pair(shaped, bit_value, dim):
    mine = lax.dynamic_index_in_dim(shaped, bit_value, dim, keepdims=False)
    other = lax.dynamic_index_in_dim(shaped, 1 - bit_value, dim, keepdims=False)
    return (mine, other)


def on_device(acts, grads, act_factors, grad_factors, lengths):
    loop_count = lax.axis_size("loop")
    position = lax.axis_index("loop")
    layer_pos = lax.axis_index("layer")
    low_bit = layer_pos % 2
    high_bit = layer_pos // 2 % 2
    all_lengths = lax.all_gather(lengths, "loop", axis=0, tiled=True)
    seq_dev = lengths.shape[0]
    tok_rows = acts.shape[1]
    pad_rows = tok_rows // seq_dev
    query_cols = act_factors.shape[2]
    query_count = query_cols // RANK
    score_total = jnp.zeros((seq_dev * loop_count, query_count * loop_count), jnp.float32)
    span_pair = (acts[0], grads[0])
    factor_pair = (act_factors[0], grad_factors[0])
    offsets = jnp.arange(pad_rows, dtype=jnp.int32)
    for cycle_step in range(loop_count):
        source_index = (position - cycle_step) % loop_count
        if cycle_step > 0:
            span_pair = shifted((span_pair[0], span_pair[1]), "loop", 1)
        act_proj = split_rank(project_rows(span_pair[0], factor_pair[0]), query_count)
        grad_proj = split_rank(project_rows(span_pair[1], factor_pair[1]), query_count)
        act_keep, act_send = pick_pair(act_proj, low_bit, 2)
        grad_keep, grad_send = pick_pair(grad_proj, low_bit, 2)
        first = from_partner((act_send, grad_send), "layer", 0)
        act_keep = act_keep + first[0]
        grad_keep = grad_keep + first[1]
        act_last, act_out = pick_pair(act_keep, high_bit, 1)
        grad_last, grad_out = pick_pair(grad_keep, high_bit, 1)
        second = from_partner((act_out, grad_out), "layer", 1)
        act_full = act_last + second[0]
        grad_full = grad_last + second[1]
        token_score = jnp.sum(act_full * grad_full, axis=1)
        seq_lengths = lax.dynamic_slice_in_dim(all_lengths, source_index * seq_dev, seq_dev)
        valid_mask = (offsets[None, :] < seq_lengths[:, None]).astype(jnp.float32)
        per_seq = jnp.sum(
            token_score.reshape(query_count, seq_dev, pad_rows) * valid_mask[None], axis=2
        ).T
        placed = lax.dynamic_update_slice(
            jnp.zeros_like(score_total), per_seq, (source_index * seq_dev, position * query_count)
        )
        score_total = score_total + placed
    return lax.psum(score_total, ("layer", "loop"))


def solution(mesh):
    in_specs = (
        P("layer", ("groups", "loop"), None),
        P("layer", ("groups", "loop"), None),
        P("layer", None, "loop"),
        P("layer", None, "loop"),
        P(("groups", "loop")),
    )
    out_specs = P("groups", None)
    return jax.shard_map(
        on_device, mesh=mesh, in_specs=in_specs, out_specs=out_specs, check_vma=False
    )
```

profile of v0, /device:TPU:0, one launch (start us, length us, event | category | flops | bytes accessed | tf_op | source)
XLA Modules:
  0.0 81.0 jit_solution(13619313794098634771)
XLA Ops:
  0.0 0.5 collective-permute-start.7
  0.5 0.1 collective-permute-start.4
  0.5 1.5 %copy.14 = bf16[1,2048,256]{1,2,0:T(8,128)(2,1)S(1)} copy(bf16[1,2048,256]{2,1,0:T(8,128)(2,1)} %param.7) | data formatting | bytes 2097152 | tf_op args[2]
  2.0 2.1 %fusion.6 = f32[8,2,2,8,384]{4,3,2,1,0:T(8,128)S(1)} fusion(bf16[8,2,2,8,2048]{4,3,2,1,0:T(8,128)(2,1)S(1)} %bitcast.88, bf16[1,384,2048]{2,1,0:T(8,128)(2,1)} %param.5), kind=kOutput, calls=%fused_computation.6 | convolution fusion | flops 402653184 | bytes 3014656 | tf_op jit(solution)/shard_map/dot_general | solution.py:21
  4.2 3.0 %collective-permute-start = (f32[8,2,8,384]{3,2,1,0:T(8,128)S(1)}, f32[8,2,8,384]{3,2,1,0:T(8,128)S(1)}, u32[]{:S(2)}, u32[]{:S(2)}) collective-permute-start(f32[8,2,8,384]{3,2,1,0:T(8,128)S(1)} %dynamic-slice_bitcast_fusion.3), channel_id=1, source_target_pairs={{0,2},{2,0},{4,6},{6,4},{8,10},{10,8},{12,14},{14,12},{1,3},{3,1},... | collective-permute-start | bytes 589832 | tf_op jit(solution)/shard_map/ppermute | solution.py:17
  7.2 6.0 %copy.15 = bf16[1,7168,256]{1,2,0:T(8,128)(2,1)} copy(bf16[1,7168,256]{2,1,0:T(8,128)(2,1)} %param.8) | data formatting | bytes 7340032 | tf_op args[3]
  13.2 0.0 copy-start.2
  13.2 0.0 copy-start.1
  13.2 5.8 %fusion.2 = f32[8,2,2,8,384]{4,3,2,1,0:T(8,128)S(1)} fusion(bf16[8,2,2,8,7168]{4,3,2,1,0:T(8,128)(2,1)} %bitcast.86, bf16[1,384,7168]{2,1,0:T(8,128)(2,1)} %param.6), kind=kOutput, calls=%fused_computation.2 | convolution fusion | flops 1409286144 | bytes 9568256 | tf_op jit(solution)/shard_map/dot_general | solution.py:21
  19.0 0.0 copy-done.2
  19.0 0.6 dynamic-slice.1
  20.3 0.0 copy-done.1
  20.3 0.2 dynamic-update-slice.1
  20.5 0.1 collective-permute-start.2
  20.6 1.8 %all-reduce = s32[8]{0:T(128)S(1)} all-reduce(s32[8]{0:T(128)S(1)} %dynamic-update-slice.1), channel_id=1, replica_groups=mesh['groups'=2,'layer'=8,'loop'=2] {'loop'}, use_global_device_ids=true, to_apply=%add | all-reduce | flops 8 | bytes 64
  22.4 0.1 fusion.14
  22.5 0.1 fusion.13
  22.6 0.0 collective-permute-done
  22.6 2.1 %collective-permute-start.1 = (f32[8,8,384]{2,1,0:T(8,128)S(1)}, f32[8,8,384]{2,1,0:T(8,128)S(1)}, u32[]{:S(2)}, u32[]{:S(2)}) collective-permute-start(f32[8,8,384]{2,1,0:T(8,128)S(1)} %dynamic-slice_bitcast_fusion.7), channel_id=1, source_target_pairs={{0,4},{2,6},{4,0},{6,2},{8,12},{10,14},{12,8},{14,10},{1,5},{3,7},... | collective-permute-start | bytes 294920 | tf_op jit(solution)/shard_map/ppermute | solution.py:17
  24.8 2.4 %collective-permute-done.2 = f32[8,2,8,384]{3,2,1,0:T(8,128)S(1)} collective-permute-done((f32[8,2,8,384]{3,2,1,0:T(8,128)S(1)}, f32[8,2,8,384]{3,2,1,0:T(8,128)S(1)}, u32[]{:S(2)}, u32[]{:S(2)}) %collective-permute-start.2) | collective-permute-done | bytes 196640 | tf_op jit(solution)/shard_map/ppermute | solution.py:17
  27.2 1.6 %collective-permute-start.3 = (f32[8,8,384]{2,1,0:T(8,128)S(1)}, f32[8,8,384]{2,1,0:T(8,128)S(1)}, u32[]{:S(2)}, u32[]{:S(2)}) collective-permute-start(f32[8,8,384]{2,1,0:T(8,128)S(1)} %dynamic-slice_bitcast_fusion.6), channel_id=1, source_target_pairs={{0,4},{2,6},{4,0},{6,2},{8,12},{10,14},{12,8},{14,10},{1,5},{3,7},... | collective-permute-start | bytes 294920 | tf_op jit(solution)/shard_map/ppermute | solution.py:17
  28.8 0.1 fusion.12
  28.9 0.0 collective-permute-done.1
  28.9 3.0 %collective-permute-done.3 = f32[8,8,384]{2,1,0:T(8,128)S(1)} collective-permute-done((f32[8,8,384]{2,1,0:T(8,128)S(1)}, f32[8,8,384]{2,1,0:T(8,128)S(1)}, u32[]{:S(2)}, u32[]{:S(2)}) %collective-permute-start.3) | collective-permute-done | bytes 98336 | tf_op jit(solution)/shard_map/ppermute | solution.py:17
  31.9 0.1 reshape.52
  32.0 0.0 copy-start
  32.0 0.0 collective-permute-done.4
  32.0 2.3 %fusion.4 = f32[8,2,2,8,384]{4,3,2,1,0:T(8,128)S(1)} fusion(bf16[8,2,2,8,2048]{4,3,2,1,0:T(8,128)(2,1)S(1)} %bitcast.89, bf16[384,2048]{1,0:T(8,128)(2,1)} %collective-permute-done.4), kind=kOutput, calls=%fused_computation.4 | convolution fusion | flops 402653184 | bytes 3014656 | tf_op jit(solution)/shard_map/dot_general | solution.py:21
  34.3 0.4 collective-permute-start.5
  34.7 0.0 collective-permute-done.7
  34.7 0.0 copy-done
  34.7 4.9 %fusion = f32[8,2,2,8,384]{4,3,2,1,0:T(8,128)S(1)} fusion(bf16[8,2,2,8,7168]{4,3,2,1,0:T(8,128)(2,1)S(1)} %bitcast.87, bf16[384,7168]{1,0:T(8,128)(2,1)} %collective-permute-done.7), kind=kOutput, calls=%fused_computation | convolution fusion | flops 1409286144 | bytes 9568256 | tf_op jit(solution)/shard_map/dot_general | solution.py:21
  39.6 1.8 %collective-permute-start.8 = (f32[8,2,8,384]{3,2,1,0:T(8,128)S(1)}, f32[8,2,8,384]{3,2,1,0:T(8,128)S(1)}, u32[]{:S(2)}, u32[]{:S(2)}) collective-permute-start(f32[8,2,8,384]{3,2,1,0:T(8,128)S(1)} %dynamic-slice_bitcast_fusion), channel_id=1, source_target_pairs={{0,2},{2,0},{4,6},{6,4},{8,10},{10,8},{12,14},{14,12},{1,3},{3,1},... | collective-permute-start | bytes 589832 | tf_op jit(solution)/shard_map/ppermute | solution.py:17
  41.4 0.0 collective-permute-done.5
  41.4 1.6 %collective-permute-start.6 = (f32[8,8,384]{2,1,0:T(8,128)S(1)}, f32[8,8,384]{2,1,0:T(8,128)S(1)}, u32[]{:S(2)}, u32[]{:S(2)}) collective-permute-start(f32[8,8,384]{2,1,0:T(8,128)S(1)} %dynamic-slice_bitcast_fusion.5), channel_id=1, source_target_pairs={{0,4},{2,6},{4,0},{6,2},{8,12},{10,14},{12,8},{14,10},{1,5},{3,7},... | collective-permute-start | bytes 294920 | tf_op jit(solution)/shard_map/ppermute | solution.py:17
  43.1 2.2 %collective-permute-done.8 = f32[8,2,8,384]{3,2,1,0:T(8,128)S(1)} collective-permute-done((f32[8,2,8,384]{3,2,1,0:T(8,128)S(1)}, f32[8,2,8,384]{3,2,1,0:T(8,128)S(1)}, u32[]{:S(2)}, u32[]{:S(2)}) %collective-permute-start.8) | collective-permute-done | bytes 196640 | tf_op jit(solution)/shard_map/ppermute | solution.py:17
  45.4 1.9 %collective-permute-start.9 = (f32[8,8,384]{2,1,0:T(8,128)S(1)}, f32[8,8,384]{2,1,0:T(8,128)S(1)}, u32[]{:S(2)}, u32[]{:S(2)}) collective-permute-start(f32[8,8,384]{2,1,0:T(8,128)S(1)} %dynamic-slice_bitcast_fusion.4), channel_id=1, source_target_pairs={{0,4},{2,6},{4,0},{6,2},{8,12},{10,14},{12,8},{14,10},{1,5},{3,7},... | collective-permute-start | bytes 294920 | tf_op jit(solution)/shard_map/ppermute | solution.py:17
  47.2 0.1 multiply_reduce_fusion.1
  47.3 0.1 copy.22
  47.4 0.3 dynamic_update_slice.8
  47.6 0.0 collective-permute-done.6
  47.7 2.4 %collective-permute-done.9 = f32[8,8,384]{2,1,0:T(8,128)S(1)} collective-permute-done((f32[8,8,384]{2,1,0:T(8,128)S(1)}, f32[8,8,384]{2,1,0:T(8,128)S(1)}, u32[]{:S(2)}, u32[]{:S(2)}) %collective-permute-start.9) | collective-permute-done | bytes 98336 | tf_op jit(solution)/shard_map/ppermute | solution.py:17
  50.1 0.1 reshape.53
  50.2 0.1 multiply_reduce_fusion
  50.3 0.1 copy.23
  50.3 0.1 bitcast_add_fusion.8
  50.4 0.3 add.104
  50.7 30.3 %psum.7 = f32[8,16]{1,0:T(8,128)} all-reduce(f32[8,16]{1,0:T(8,128)S(1)} %add.104), channel_id=1, replica_groups=mesh['groups'=2,'layer'=8,'loop'=2] {'layer','loop'}, use_global_device_ids=true, to_apply=%region_4.5 | all-reduce | flops 128 | bytes 1024 | tf_op jit(solution)/shard_map/psum | solution.py:78
  (16 shorter events, 0.3 us)
Async XLA Ops:
  0.0 34.7 %collective-permute-start.7 = (bf16[384,7168]{1,0:T(8,128)(2,1)}, bf16[384,7168]{1,0:T(8,128)(2,1)}, u32[]{:S(2)}, u32[]{:S(2)}) collective-permute-start(bf16[384,7168]{1,0:T(8,128)(2,1)} %bitcast.91), channel_id=1, source_target_pairs={{0,1},{1,0},{2,3},{3,2},{4,5},{5,4},{6,7},{7,6},{8,9},{9,8},{10,11... | collective-permute-start | bytes 16515080 | tf_op jit(solution)/shard_map/ppermute | solution.py:11
  0.5 31.5 %collective-permute-start.4 = (bf16[384,2048]{1,0:T(8,128)(2,1)}, bf16[384,2048]{1,0:T(8,128)(2,1)}, u32[]{:S(2)}, u32[]{:S(2)}) collective-permute-start(bf16[384,2048]{1,0:T(8,128)(2,1)} %bitcast.92), channel_id=1, source_target_pairs={{0,1},{1,0},{2,3},{3,2},{4,5},{5,4},{6,7},{7,6},{8,9},{9,8},{10,11... | collective-permute-start | bytes 4718600 | tf_op jit(solution)/shard_map/ppermute | solution.py:11
  4.2 18.4 %collective-permute-start = (f32[8,2,8,384]{3,2,1,0:T(8,128)S(1)}, f32[8,2,8,384]{3,2,1,0:T(8,128)S(1)}, u32[]{:S(2)}, u32[]{:S(2)}) collective-permute-start(f32[8,2,8,384]{3,2,1,0:T(8,128)S(1)} %dynamic-slice_bitcast_fusion.3), channel_id=1, source_target_pairs={{0,2},{2,0},{4,6},{6,4},{8,10},{10,8},{12,14},{14,12},{1,3},{3,1},... | collective-permute-start | bytes 589832 | tf_op jit(solution)/shard_map/ppermute | solution.py:17
  13.2 5.8 %copy-start.2 = (u32[32]{0:T(128)S(1)}, u32[32]{0:T(128)}, u32[]{:S(2)}) copy-start(u32[32]{0:T(128)} %constant.101) | copy-start | bytes 388
  13.2 7.0 %copy-start.1 = (s32[4]{0:T(128)S(1)}, s32[4]{0:T(128)}, u32[]{:S(2)}) copy-start(s32[4]{0:T(128)} %param.9) | copy-start | bytes 52
  20.5 6.6 %collective-permute-start.2 = (f32[8,2,8,384]{3,2,1,0:T(8,128)S(1)}, f32[8,2,8,384]{3,2,1,0:T(8,128)S(1)}, u32[]{:S(2)}, u32[]{:S(2)}) collective-permute-start(f32[8,2,8,384]{3,2,1,0:T(8,128)S(1)} %dynamic-slice_bitcast_fusion.2), channel_id=1, source_target_pairs={{0,2},{2,0},{4,6},{6,4},{8,10},{10,8},{12,14},{14,12},{1,3},{3,1},... | collective-permute-start | bytes 589832 | tf_op jit(solution)/shard_map/ppermute | solution.py:17
  22.6 6.2 %collective-permute-start.1 = (f32[8,8,384]{2,1,0:T(8,128)S(1)}, f32[8,8,384]{2,1,0:T(8,128)S(1)}, u32[]{:S(2)}, u32[]{:S(2)}) collective-permute-start(f32[8,8,384]{2,1,0:T(8,128)S(1)} %dynamic-slice_bitcast_fusion.7), channel_id=1, source_target_pairs={{0,4},{2,6},{4,0},{6,2},{8,12},{10,14},{12,8},{14,10},{1,5},{3,7},... | collective-permute-start | bytes 294920 | tf_op jit(solution)/shard_map/ppermute | solution.py:17
  27.2 4.7 %collective-permute-start.3 = (f32[8,8,384]{2,1,0:T(8,128)S(1)}, f32[8,8,384]{2,1,0:T(8,128)S(1)}, u32[]{:S(2)}, u32[]{:S(2)}) collective-permute-start(f32[8,8,384]{2,1,0:T(8,128)S(1)} %dynamic-slice_bitcast_fusion.6), channel_id=1, source_target_pairs={{0,4},{2,6},{4,0},{6,2},{8,12},{10,14},{12,8},{14,10},{1,5},{3,7},... | collective-permute-start | bytes 294920 | tf_op jit(solution)/shard_map/ppermute | solution.py:17
  32.0 2.7 %copy-start = (bf16[1,7168,256]{1,2,0:T(8,128)(2,1)S(1)}, bf16[1,7168,256]{1,2,0:T(8,128)(2,1)}, u32[]{:S(2)}) copy-start(bf16[1,7168,256]{1,2,0:T(8,128)(2,1)} %copy.15) | copy-start | bytes 11010052
  34.3 7.1 %collective-permute-start.5 = (f32[8,2,8,384]{3,2,1,0:T(8,128)S(1)}, f32[8,2,8,384]{3,2,1,0:T(8,128)S(1)}, u32[]{:S(2)}, u32[]{:S(2)}) collective-permute-start(f32[8,2,8,384]{3,2,1,0:T(8,128)S(1)} %dynamic-slice_bitcast_fusion.1), channel_id=1, source_target_pairs={{0,2},{2,0},{4,6},{6,4},{8,10},{10,8},{12,14},{14,12},{1,3},{3,1},... | collective-permute-start | bytes 589832 | tf_op jit(solution)/shard_map/ppermute | solution.py:17
  39.6 5.7 %collective-permute-start.8 = (f32[8,2,8,384]{3,2,1,0:T(8,128)S(1)}, f32[8,2,8,384]{3,2,1,0:T(8,128)S(1)}, u32[]{:S(2)}, u32[]{:S(2)}) collective-permute-start(f32[8,2,8,384]{3,2,1,0:T(8,128)S(1)} %dynamic-slice_bitcast_fusion), channel_id=1, source_target_pairs={{0,2},{2,0},{4,6},{6,4},{8,10},{10,8},{12,14},{14,12},{1,3},{3,1},... | collective-permute-start | bytes 589832 | tf_op jit(solution)/shard_map/ppermute | solution.py:17
  41.4 6.2 %collective-permute-start.6 = (f32[8,8,384]{2,1,0:T(8,128)S(1)}, f32[8,8,384]{2,1,0:T(8,128)S(1)}, u32[]{:S(2)}, u32[]{:S(2)}) collective-permute-start(f32[8,8,384]{2,1,0:T(8,128)S(1)} %dynamic-slice_bitcast_fusion.5), channel_id=1, source_target_pairs={{0,4},{2,6},{4,0},{6,2},{8,12},{10,14},{12,8},{14,10},{1,5},{3,7},... | collective-permute-start | bytes 294920 | tf_op jit(solution)/shard_map/ppermute | solution.py:17
  45.4 4.7 %collective-permute-start.9 = (f32[8,8,384]{2,1,0:T(8,128)S(1)}, f32[8,8,384]{2,1,0:T(8,128)S(1)}, u32[]{:S(2)}, u32[]{:S(2)}) collective-permute-start(f32[8,8,384]{2,1,0:T(8,128)S(1)} %dynamic-slice_bitcast_fusion.4), channel_id=1, source_target_pairs={{0,4},{2,6},{4,0},{6,2},{8,12},{10,14},{12,8},{14,10},{1,5},{3,7},... | collective-permute-start | bytes 294920 | tf_op jit(solution)/shard_map/ppermute | solution.py:17
where the time goes:
time: 81.4 us; the launch traced here: 81 us
  blocking collectives  32.2 us (40%)
  matrix products  15 us (18%)
  starting transfers between devices  13 us (16%)
  waiting for transfers between devices  9.98 us (12%)
  local copies, waits for them, and re-layouts  9.39 us (12%)
  between operations  0.84 us (1%)
    psum x1, blocking collectives, on_device(): return lax.psum(score_total, ('layer', 'loop'))  30.3 us
    dot_general x4, matrix products, project_rows(): lax.dot_general(factor, rows, (((0,), (1,)), ((), ())), preferred_element...  15 us
    ppermute x8, starting transfers between devices, from_partner(): return lax.ppermute(value, axis, pairs)  12.5 us
    ppermute x8, waiting for transfers between devices, from_partner(): return lax.ppermute(value, axis, pairs)  9.98 us
    unnamed x13, local copies, waits for them, and re-layouts  8.49 us
    unnamed x1, blocking collectives  1.83 us
  transfers between devices with their start and end apart: 10, of which 4 were waited for; matrix products, arithmetic and copies ran while one was open for 30% of the time, Pallas kernels for 0%

commit v1 on v0

v1 whole, which is shorter than its diff:
```python
import jax
import jax.numpy as jnp
from jax import lax
from jax.sharding import PartitionSpec as P

RANK = 32
QUARTERS = 4


def from_partner(value, axis, mask):
    pairs = [(source, source ^ mask) for source in range(lax.axis_size(axis))]
    return lax.ppermute(value, axis, pairs)


def project(rows, factor):
    return jnp.dot(rows, factor, preferred_element_type=jnp.float32)


def sum_over_quarters(projected, quarter):
    parts = projected.reshape(QUARTERS, -1, projected.shape[1])
    total = lax.dynamic_index_in_dim(parts, quarter, 0, keepdims=False)
    for mask in range(1, QUARTERS):
        out = lax.dynamic_index_in_dim(parts, quarter ^ mask, 0, keepdims=False)
        total = total + from_partner(out, "layer", mask)
    return total


def on_device(acts, grads, act_factors, grad_factors, lengths):
    loop_count = lax.axis_size("loop")
    position = lax.axis_index("loop")
    layer_count = lax.axis_size("layer")
    quarter = lax.axis_index("layer") % QUARTERS
    seq_dev = lengths.shape[0]
    pad_rows = acts.shape[1] // seq_dev
    seq_part = seq_dev // QUARTERS
    other_grad = from_partner(grad_factors[0], "loop", 1)
    other_act = from_partner(act_factors[0], "loop", 1)
    mine = jnp.concatenate(
        [project(acts[0], act_factors[0]), project(grads[0], grad_factors[0])], axis=1
    )
    mine = sum_over_quarters(mine, quarter)
    other = jnp.concatenate(
        [project(acts[0], other_act), project(grads[0], other_grad)], axis=1
    )
    other = sum_over_quarters(other, quarter)
    my_lengths = lax.dynamic_slice_in_dim(lengths, quarter * seq_part, seq_part)
    offsets = jnp.arange(pad_rows, dtype=jnp.int32)
    live = (offsets[None, :] < my_lengths[:, None])[:, :, None]

    def score(both):
        act, grad = jnp.split(both, 2, axis=1)
        pair = jnp.where(live, (act * grad).reshape(seq_part, pad_rows, -1), 0)
        return jnp.sum(pair.reshape(seq_part, pad_rows, -1, RANK), axis=(1, 3))

    mine, other = score(mine), score(other)
    first = jnp.where(position == 0, mine, other)
    second = jnp.where(position == 0, other, mine)
    scores = jnp.concatenate([first, second], axis=1)
    total = jnp.zeros((seq_dev * loop_count, scores.shape[1]), jnp.float32)
    total = lax.dynamic_update_slice(
        total, scores, (position * seq_dev + quarter * seq_part, 0)
    )
    total = total + from_partner(total, "loop", 1)
    gathered = [from_partner(total, "layer", mask) for mask in range(1, QUARTERS)]
    total = total + gathered[0] + gathered[1] + gathered[2]
    mask = QUARTERS
    while mask < layer_count:
        total = total + from_partner(total, "layer", mask)
        mask *= 2
    return total


def solution(mesh):
    in_specs = (
        P("layer", ("groups", "loop"), None),
        P("layer", ("groups", "loop"), None),
        P("layer", None, "loop"),
        P("layer", None, "loop"),
        P(("groups", "loop")),
    )
    out_specs = P("groups", None)
    return jax.shard_map(
        on_device, mesh=mesh, in_specs=in_specs, out_specs=out_specs, check_vma=False
    )
```

time: 81.4 us -> 52.1 us (0.64)
  blocking collectives: 32.2 us -> 0 us
  local copies, waits for them, and re-layouts: 9.39 us -> 4.23 us
  other arithmetic: 0.58 us -> 3.87 us
  waiting for transfers between devices: 9.98 us -> 13.2 us
  starting transfers between devices: 13 us -> 14.8 us
    psum x1 -> x0, blocking collectives: 30.3 us -> none  [on_device(): return lax.psum(score_total, ('layer', 'loop'))]
    unnamed x13 -> x4, local copies, waits for them, and re-layouts: 8.49 us -> 0.89 us
    ppermute x8 -> x13, waiting for transfers between devices: 9.98 us -> 13.2 us  [from_partner(): return lax.ppermute(value, axis, pairs)]
    ppermute x8 -> x13, starting transfers between devices: 12.5 us -> 14.8 us  [from_partner(): return lax.ppermute(value, axis, pairs)]
    unnamed x1 -> x0, blocking collectives: 1.83 us -> none
    concatenate x0 -> x2, local copies, waits for them, and re-layouts: none -> 1.66 us  [the longest x1 1.39 us: on_device(): jnp.concatenate([project(acts[0], other_act), project(grads[0], other_gra...]
    add x4, other arithmetic: 0.1 us -> 1.74 us  [the longest x2 1.14 us: sum_over_quarters(): total = total + from_partner(out, 'layer', mask)]
    concatenate x0 -> x3, other arithmetic: none -> 1.06 us  [the longest x1 0.93 us: on_device(): jnp.concatenate([project(acts[0], other_act), project(grads[0], other_gra...]
  transfers between devices with their start and end apart: 10 -> 13, of which waited for: 4 -> 8; matrix products, arithmetic and copies ran while one was open for 30% -> 41% of each run, Pallas kernels for 0% -> 0%
where the time goes in v1:
time: 52.1 us; the launch traced here: 51.8 us
  matrix products  15.5 us (30%)
  starting transfers between devices  14.8 us (28%)
  waiting for transfers between devices  13.2 us (25%)
  local copies, waits for them, and re-layouts  4.23 us (8%)
  other arithmetic  3.87 us (7%)
    dot_general x4, matrix products, project(): return jnp.dot(rows, factor, preferred_element_type=jnp.float32)  15.5 us
    ppermute x13, starting transfers between devices, from_partner(): return lax.ppermute(value, axis, pairs)  14.8 us
    ppermute x13, waiting for transfers between devices, from_partner(): return lax.ppermute(value, axis, pairs)  13.2 us
    concatenate x1, local copies, waits for them, and re-layouts, on_device(): jnp.concatenate([project(acts[0], other_act), project(grads[0], other_gra...  1.39 us
    add x2, other arithmetic, sum_over_quarters(): total = total + from_partner(out, 'layer', mask)  1.14 us
  transfers between devices with their start and end apart: 13, of which 8 were waited for; matrix products, arithmetic and copies ran while one was open for 41% of the time, Pallas kernels for 0%

profile of v1, /device:TPU:0, one launch (start us, length us, event | category | flops | bytes accessed | tf_op | source)
XLA Modules:
  0.0 51.8 jit_solution(14835039217502851327)
XLA Ops:
  0.0 0.5 collective-permute-start.4
  0.5 0.1 collective-permute-start.3
  0.5 0.9 %copy-done = bf16[1,384,2048]{2,1,0:T(8,128)(2,1)S(1)} copy-done((bf16[1,384,2048]{2,1,0:T(8,128)(2,1)S(1)}, bf16[1,384,2048]{2,1,0:T(8,128)(2,1)}, u32[]{:S(2)}) %copy-start) | copy-done | bytes 1572888
  1.4 2.0 %fusion.6 = f32[384,256]{0,1:T(8,128)S(1)} fusion(bf16[1,384,2048]{2,1,0:T(8,128)(2,1)S(1)} %copy-done, bf16[1,2048,256]{2,1,0:T(8,128)(2,1)} %param.7), kind=kOutput, calls=%fused_computation.6 | convolution fusion | flops 402653184 | bytes 3014656 | tf_op jit(solution)/shard_map/dot_general | solution.py:16
  3.4 5.8 %fusion.2 = f32[384,256]{0,1:T(8,128)S(1)} fusion(bf16[1,384,7168]{2,1,0:T(8,128)(2,1)} %param.6, bf16[1,7168,256]{2,1,0:T(8,128)(2,1)} %param.8), kind=kOutput, calls=%fused_computation.2 | convolution fusion | flops 1409286144 | bytes 9568256 | tf_op jit(solution)/shard_map/dot_general | solution.py:16
  9.2 0.0 copy-start.1
  9.2 0.1 pad_maximum_fusion
  9.3 0.3 copy.8
  9.6 0.8 %dynamic-slice_bitcast_fusion.5 = (f32[96,512]{1,0:T(8,128)}, f32[96,512]{1,0:T(8,128)S(1)}, f32[96,512]{1,0:T(8,128)}) fusion(f32[4,96,512]{2,1,0:T(8,128)S(1)} %bitcast.49, s32[]{:T(128)S(6)} %select_n.74, s32[]{:T(128)S(6)} %select_n.76, s32[]{:T(128)S(6)} %select_n.75), kind=kLoop, calls=%fused_computation.21 | loop fusion | bytes 1179660 | tf_op jit(solution)/shard_map/jit(dynamic_index_in_dim)/squeeze | solution.py:23
  10.4 3.0 %collective-permute-start = (f32[96,512]{1,0:T(8,128)}, f32[96,512]{1,0:T(8,128)S(1)}, u32[]{:S(2)}, u32[]{:S(2)}) collective-permute-start(f32[96,512]{1,0:T(8,128)} %get-tuple-element.10), channel_id=1, source_target_pairs={{0,2},{2,0},{4,6},{6,4},{8,10},{10,8},{12,14},{14,12},{1,3},{3,1},... | collective-permute-start | bytes 589832 | tf_op jit(solution)/shard_map/ppermute | solution.py:12
  13.4 1.6 %collective-permute-start.1 = (f32[96,512]{1,0:T(8,128)}, f32[96,512]{1,0:T(8,128)}, u32[]{:S(2)}, u32[]{:S(2)}) collective-permute-start(f32[96,512]{1,0:T(8,128)} %get-tuple-element.12), channel_id=1, source_target_pairs={{0,4},{2,6},{4,0},{6,2},{8,12},{10,14},{12,8},{14,10},{1,5},{3,7},... | collective-permute-start | bytes 589832 | tf_op jit(solution)/shard_map/ppermute | solution.py:12
  14.9 0.0 collective-permute-start.2
  14.9 0.6 %dynamic_slice.28 = s32[1]{0:T(128)} dynamic-slice(s32[4]{0:T(128)S(1)} %copy-done.1, s32[]{:T(128)S(6)} %select_n.73), dynamic_slice_sizes={1} | dynamic-slice | bytes 12 | tf_op jit(solution)/shard_map/dynamic_slice | solution.py:46
  15.5 0.6 %iota_compare_fusion = pred[96]{0:T(512)(128)(4,1)S(1)} fusion(s32[]{:T(128)} %bitcast), kind=kLoop, calls=%fused_computation.36 | loop fusion | flops 96 | bytes 100 | tf_op jit(solution)/shard_map/lt | solution.py:48
  16.2 0.0 collective-permute-done.3
  16.2 2.0 %fusion.4 = f32[384,256]{0,1:T(8,128)S(1)} fusion(bf16[2048,256]{1,0:T(8,128)(2,1)} %collective-permute-done.3, bf16[1,384,2048]{2,1,0:T(8,128)(2,1)S(1)} %copy-done), kind=kOutput, calls=%fused_computation.4 | convolution fusion | flops 402653184 | bytes 3014656 | tf_op jit(solution)/shard_map/dot_general | solution.py:16
  18.2 0.0 collective-permute-done.4
  18.2 5.8 %fusion = f32[384,256]{0,1:T(8,128)S(1)} fusion(bf16[7168,256]{1,0:T(8,128)(2,1)} %collective-permute-done.4, bf16[1,384,7168]{2,1,0:T(8,128)(2,1)} %param.6), kind=kOutput, calls=%fused_computation | convolution fusion | flops 1409286144 | bytes 9568256 | tf_op jit(solution)/shard_map/dot_general | solution.py:16
  24.0 0.9 %pad_maximum_fusion.1 = f32[384,512]{0,1:T(8,128)} fusion(f32[384,256]{0,1:T(8,128)S(1)} %fusion, f32[384,256]{0,1:T(8,128)S(1)} %fusion.4), kind=kLoop, calls=%fused_computation.9 | loop fusion | flops 196608 | bytes 1572864 | tf_op jit(solution)/shard_map/concatenate | solution.py:42
  24.9 1.4 %copy.9 = f32[384,512]{1,0:T(8,128)S(1)} copy(f32[384,512]{0,1:T(8,128)} %pad_maximum_fusion.1) | data formatting | bytes 1572864 | tf_op jit(solution)/shard_map/concatenate | solution.py:42
  26.3 0.1 dynamic-slice_bitcast_fusion.2
  26.4 2.0 %collective-permute-start.5 = (f32[96,512]{1,0:T(8,128)S(1)}, f32[96,512]{1,0:T(8,128)S(1)}, u32[]{:S(2)}, u32[]{:S(2)}) collective-permute-start(f32[96,512]{1,0:T(8,128)S(1)} %get-tuple-element.7), channel_id=1, source_target_pairs={{0,2},{2,0},{4,6},{6,4},{8,10},{10,8},{12,14},{14,12},{1,3},{3,1},... | collective-permute-start | bytes 589832 | tf_op jit(solution)/shard_map/ppermute | solution.py:12
  28.3 1.6 %collective-permute-start.6 = (f32[96,512]{1,0:T(8,128)S(1)}, f32[96,512]{1,0:T(8,128)S(1)}, u32[]{:S(2)}, u32[]{:S(2)}) collective-permute-start(f32[96,512]{1,0:T(8,128)S(1)} %get-tuple-element.9), channel_id=1, source_target_pairs={{0,4},{2,6},{4,0},{6,2},{8,12},{10,14},{12,8},{14,10},{1,5},{3,7},... | collective-permute-start | bytes 589832 | tf_op jit(solution)/shard_map/ppermute | solution.py:12
  29.9 0.0 collective-permute-done
  29.9 0.0 collective-permute-done.2
  29.9 1.1 %fusion.11 = f32[96,512]{1,0:T(8,128)S(1)} fusion(f32[96,512]{1,0:T(8,128)} %collective-permute-done.2, f32[96,512]{1,0:T(8,128)} %collective-permute-done.1, f32[96,512]{1,0:T(8,128)S(1)} %collective-permute-done, f32[4,96,512]{2,1,0:T(8,128)S(1)} %bitcast.50, s32[]{:T(128)S(6)} %select_n.73), kind=kLoop, calls=%fused_computation.15 | loop fusion | flops 147456 | bytes 983044 | tf_op jit(solution)/shard_map/add | solution.py:24
  31.0 2.1 %collective-permute-done.5 = f32[96,512]{1,0:T(8,128)S(1)} collective-permute-done((f32[96,512]{1,0:T(8,128)S(1)}, f32[96,512]{1,0:T(8,128)S(1)}, u32[]{:S(2)}, u32[]{:S(2)}) %collective-permute-start.5) | collective-permute-done | bytes 196640 | tf_op jit(solution)/shard_map/ppermute | solution.py:12
  33.2 2.8 %collective-permute-done.6 = f32[96,512]{1,0:T(8,128)S(1)} collective-permute-done((f32[96,512]{1,0:T(8,128)S(1)}, f32[96,512]{1,0:T(8,128)S(1)}, u32[]{:S(2)}, u32[]{:S(2)}) %collective-permute-start.6) | collective-permute-done | bytes 196640 | tf_op jit(solution)/shard_map/ppermute | solution.py:12
  36.0 1.9 %collective-permute-done.7 = f32[96,512]{1,0:T(8,128)S(1)} collective-permute-done((f32[96,512]{1,0:T(8,128)S(1)}, f32[96,512]{1,0:T(8,128)S(1)}, u32[]{:S(2)}, u32[]{:S(2)}) %collective-permute-start.7) | collective-permute-done | bytes 196640 | tf_op jit(solution)/shard_map/ppermute | solution.py:12
  37.9 0.1 fusion.9
  38.0 0.1 fusion.15
  38.1 0.1 reduce_sum.24
  38.2 0.1 reduce_sum.36
  38.2 0.1 reduce_sum.25
  38.3 0.1 reduce_sum.37
  38.5 0.1 pad_maximum_fusion.2
  38.6 0.1 collective-permute-start.8
  38.7 1.2 %collective-permute-done.8 = f32[8,16]{1,0:T(8,128)S(1)} collective-permute-done((f32[8,16]{1,0:T(8,128)S(1)}, f32[8,16]{1,0:T(8,128)S(1)}, u32[]{:S(2)}, u32[]{:S(2)}) %collective-permute-start.8) | collective-permute-done | bytes 544 | tf_op jit(solution)/shard_map/ppermute | solution.py:12
  39.8 0.1 fusion.18
  39.9 1.7 %collective-permute-start.10 = (f32[8,16]{1,0:T(8,128)S(1)}, f32[8,16]{1,0:T(8,128)S(1)}, u32[]{:S(2)}, u32[]{:S(2)}) collective-permute-start(f32[8,16]{1,0:T(8,128)S(1)} %add.75), channel_id=1, source_target_pairs={{0,4},{2,6},{4,0},{6,2},{8,12},{10,14},{12,8},{14,10},{1,5},{3,7},... | collective-permute-start | bytes 1544 | tf_op jit(solution)/shard_map/ppermute | solution.py:12
  41.7 1.4 %collective-permute-start.11 = (f32[8,16]{1,0:T(8,128)S(1)}, f32[8,16]{1,0:T(8,128)S(1)}, u32[]{:S(2)}, u32[]{:S(2)}) collective-permute-start(f32[8,16]{1,0:T(8,128)S(1)} %add.75), channel_id=1, source_target_pairs={{0,6},{2,4},{4,2},{6,0},{8,14},{10,12},{12,10},{14,8},{1,7},{3,5},... | collective-permute-start | bytes 1544 | tf_op jit(solution)/shard_map/ppermute | solution.py:12
  43.1 0.4 collective-permute-start.9
  43.5 0.1 collective-permute-done.10
  43.6 2.6 %collective-permute-done.11 = f32[8,16]{1,0:T(8,128)S(1)} collective-permute-done((f32[8,16]{1,0:T(8,128)S(1)}, f32[8,16]{1,0:T(8,128)S(1)}, u32[]{:S(2)}, u32[]{:S(2)}) %collective-permute-start.11) | collective-permute-done | bytes 544 | tf_op jit(solution)/shard_map/ppermute | solution.py:12
  46.2 0.5 collective-permute-done.9
  46.7 2.6 %collective-permute-start.12 = (f32[8,16]{1,0:T(8,128)S(1)}, f32[8,16]{1,0:T(8,128)S(1)}, u32[]{:S(2)}, u32[]{:S(2)}) collective-permute-start(f32[8,16]{1,0:T(8,128)S(1)} %add_add_fusion), channel_id=1, source_target_pairs={{0,8},{2,10},{4,12},{6,14},{8,0},{10,2},{12,4},{14,6},{1,9},{3,11}... | collective-permute-start | bytes 1544 | tf_op jit(solution)/shard_map/ppermute | solution.py:12
  49.3 1.9 %collective-permute-done.12 = f32[8,16]{1,0:T(8,128)S(1)} collective-permute-done((f32[8,16]{1,0:T(8,128)S(1)}, f32[8,16]{1,0:T(8,128)S(1)}, u32[]{:S(2)}, u32[]{:S(2)}) %collective-permute-start.12) | collective-permute-done | bytes 544 | tf_op jit(solution)/shard_map/ppermute | solution.py:12
  51.2 0.6 %add.79 = f32[8,16]{1,0:T(8,128)} add(f32[8,16]{1,0:T(8,128)S(1)} %add_add_fusion, f32[8,16]{1,0:T(8,128)S(1)} %collective-permute-done.12) | non-fusion elementwise | flops 128 | bytes 1536 | tf_op jit(solution)/shard_map/add | solution.py:68
  (9 shorter events, 0.1 us)
Async XLA Ops:
  0.0 1.4 %copy-start = (bf16[1,384,2048]{2,1,0:T(8,128)(2,1)S(1)}, bf16[1,384,2048]{2,1,0:T(8,128)(2,1)}, u32[]{:S(2)}) copy-start(bf16[1,384,2048]{2,1,0:T(8,128)(2,1)} %param.5) | copy-start | bytes 4718596
  0.0 18.2 %collective-permute-start.4 = (bf16[7168,256]{1,0:T(8,128)(2,1)}, bf16[7168,256]{1,0:T(8,128)(2,1)}, u32[]{:S(2)}, u32[]{:S(2)}) collective-permute-start(bf16[7168,256]{1,0:T(8,128)(2,1)} %bitcast.54), channel_id=1, source_target_pairs={{0,1},{1,0},{2,3},{3,2},{4,5},{5,4},{6,7},{7,6},{8,9},{9,8},{10,11... | collective-permute-start | bytes 11010056 | tf_op jit(solution)/shard_map/ppermute | solution.py:12
  0.5 15.7 %collective-permute-start.3 = (bf16[2048,256]{1,0:T(8,128)(2,1)}, bf16[2048,256]{1,0:T(8,128)(2,1)}, u32[]{:S(2)}, u32[]{:S(2)}) collective-permute-start(bf16[2048,256]{1,0:T(8,128)(2,1)} %bitcast.53), channel_id=1, source_target_pairs={{0,1},{1,0},{2,3},{3,2},{4,5},{5,4},{6,7},{7,6},{8,9},{9,8},{10,11... | collective-permute-start | bytes 3145736 | tf_op jit(solution)/shard_map/ppermute | solution.py:12
  9.2 5.8 %copy-start.1 = (s32[4]{0:T(128)S(1)}, s32[4]{0:T(128)}, u32[]{:S(2)}) copy-start(s32[4]{0:T(128)} %param.9) | copy-start | bytes 52
  10.4 19.5 %collective-permute-start = (f32[96,512]{1,0:T(8,128)}, f32[96,512]{1,0:T(8,128)S(1)}, u32[]{:S(2)}, u32[]{:S(2)}) collective-permute-start(f32[96,512]{1,0:T(8,128)} %get-tuple-element.10), channel_id=1, source_target_pairs={{0,2},{2,0},{4,6},{6,4},{8,10},{10,8},{12,14},{14,12},{1,3},{3,1},... | collective-permute-start | bytes 589832 | tf_op jit(solution)/shard_map/ppermute | solution.py:12
  13.4 16.6 %collective-permute-start.1 = (f32[96,512]{1,0:T(8,128)}, f32[96,512]{1,0:T(8,128)}, u32[]{:S(2)}, u32[]{:S(2)}) collective-permute-start(f32[96,512]{1,0:T(8,128)} %get-tuple-element.12), channel_id=1, source_target_pairs={{0,4},{2,6},{4,0},{6,2},{8,12},{10,14},{12,8},{14,10},{1,5},{3,7},... | collective-permute-start | bytes 589832 | tf_op jit(solution)/shard_map/ppermute | solution.py:12
  14.9 15.0 %collective-permute-start.2 = (f32[96,512]{1,0:T(8,128)S(1)}, f32[96,512]{1,0:T(8,128)}, u32[]{:S(2)}, u32[]{:S(2)}) collective-permute-start(f32[96,512]{1,0:T(8,128)S(1)} %get-tuple-element.11), channel_id=1, source_target_pairs={{0,6},{2,4},{4,2},{6,0},{8,14},{10,12},{12,10},{14,8},{1,7},{3,5},... | collective-permute-start | bytes 589832 | tf_op jit(solution)/shard_map/ppermute | solution.py:12
  26.4 6.8 %collective-permute-start.5 = (f32[96,512]{1,0:T(8,128)S(1)}, f32[96,512]{1,0:T(8,128)S(1)}, u32[]{:S(2)}, u32[]{:S(2)}) collective-permute-start(f32[96,512]{1,0:T(8,128)S(1)} %get-tuple-element.7), channel_id=1, source_target_pairs={{0,2},{2,0},{4,6},{6,4},{8,10},{10,8},{12,14},{14,12},{1,3},{3,1},... | collective-permute-start | bytes 589832 | tf_op jit(solution)/shard_map/ppermute | solution.py:12
  28.3 7.6 %collective-permute-start.6 = (f32[96,512]{1,0:T(8,128)S(1)}, f32[96,512]{1,0:T(8,128)S(1)}, u32[]{:S(2)}, u32[]{:S(2)}) collective-permute-start(f32[96,512]{1,0:T(8,128)S(1)} %get-tuple-element.9), channel_id=1, source_target_pairs={{0,4},{2,6},{4,0},{6,2},{8,12},{10,14},{12,8},{14,10},{1,5},{3,7},... | collective-permute-start | bytes 589832 | tf_op jit(solution)/shard_map/ppermute | solution.py:12
  29.9 8.0 %collective-permute-start.7 = (f32[96,512]{1,0:T(8,128)S(1)}, f32[96,512]{1,0:T(8,128)S(1)}, u32[]{:S(2)}, u32[]{:S(2)}) collective-permute-start(f32[96,512]{1,0:T(8,128)S(1)} %get-tuple-element.8), channel_id=1, source_target_pairs={{0,6},{2,4},{4,2},{6,0},{8,14},{10,12},{12,10},{14,8},{1,7},{3,5},... | collective-permute-start | bytes 589832 | tf_op jit(solution)/shard_map/ppermute | solution.py:12
  38.6 1.2 %collective-permute-start.8 = (f32[8,16]{1,0:T(8,128)S(1)}, f32[8,16]{1,0:T(8,128)S(1)}, u32[]{:S(2)}, u32[]{:S(2)}) collective-permute-start(f32[8,16]{1,0:T(8,128)S(1)} %dynamic_update_slice.5), channel_id=1, source_target_pairs={{0,1},{1,0},{2,3},{3,2},{4,5},{5,4},{6,7},{7,6},{8,9},{9,8},{10,11... | collective-permute-start | bytes 1544 | tf_op jit(solution)/shard_map/ppermute | solution.py:12
  39.9 3.7 %collective-permute-start.10 = (f32[8,16]{1,0:T(8,128)S(1)}, f32[8,16]{1,0:T(8,128)S(1)}, u32[]{:S(2)}, u32[]{:S(2)}) collective-permute-start(f32[8,16]{1,0:T(8,128)S(1)} %add.75), channel_id=1, source_target_pairs={{0,4},{2,6},{4,0},{6,2},{8,12},{10,14},{12,8},{14,10},{1,5},{3,7},... | collective-permute-start | bytes 1544 | tf_op jit(solution)/shard_map/ppermute | solution.py:12
  41.7 4.5 %collective-permute-start.11 = (f32[8,16]{1,0:T(8,128)S(1)}, f32[8,16]{1,0:T(8,128)S(1)}, u32[]{:S(2)}, u32[]{:S(2)}) collective-permute-start(f32[8,16]{1,0:T(8,128)S(1)} %add.75), channel_id=1, source_target_pairs={{0,6},{2,4},{4,2},{6,0},{8,14},{10,12},{12,10},{14,8},{1,7},{3,5},... | collective-permute-start | bytes 1544 | tf_op jit(solution)/shard_map/ppermute | solution.py:12
  43.1 3.6 %collective-permute-start.9 = (f32[8,16]{1,0:T(8,128)S(1)}, f32[8,16]{1,0:T(8,128)S(1)}, u32[]{:S(2)}, u32[]{:S(2)}) collective-permute-start(f32[8,16]{1,0:T(8,128)S(1)} %add.75), channel_id=1, source_target_pairs={{0,2},{2,0},{4,6},{6,4},{8,10},{10,8},{12,14},{14,12},{1,3},{3,1},... | collective-permute-start | bytes 1544 | tf_op jit(solution)/shard_map/ppermute | solution.py:12
  46.7 4.5 %collective-permute-start.12 = (f32[8,16]{1,0:T(8,128)S(1)}, f32[8,16]{1,0:T(8,128)S(1)}, u32[]{:S(2)}, u32[]{:S(2)}) collective-permute-start(f32[8,16]{1,0:T(8,128)S(1)} %add_add_fusion), channel_id=1, source_target_pairs={{0,8},{2,10},{4,12},{6,14},{8,0},{10,2},{12,4},{14,6},{1,9},{3,11}... | collective-permute-start | bytes 1544 | tf_op jit(solution)/shard_map/ppermute | solution.py:12

commit v2 on v1

v2 whole, which is shorter than its diff:
```python
import functools

import jax
import jax.numpy as jnp
from jax import lax
from jax.experimental import pallas as pl
from jax.experimental.pallas import tpu as pltpu
from jax.sharding import PartitionSpec as P

RANK = 32
QUARTERS = 4
LANES = 128
CODE_ROWS = 16
TOP = 32000.0
STEPS = 256.0
FLOOR = 2.0**-112
CHUNK = 1024
MIB = 2**20

IN_VMEM = pl.BlockSpec(memory_space=pltpu.VMEM)
IN_HBM = pl.BlockSpec(memory_space=pltpu.HBM)
IN_SMEM = pl.BlockSpec(memory_space=pltpu.SMEM)


def from_partner(value, axis, mask):
    pairs = [(source, source ^ mask) for source in range(lax.axis_size(axis))]
    return lax.ppermute(value, axis, pairs)


def dot(rows, factor):
    return jnp.dot(rows, factor, preferred_element_type=jnp.float32)


def encode(part):
    peak = jnp.max(jnp.abs(part), axis=0, keepdims=True)
    code = jnp.ceil(jnp.log2(jnp.maximum(peak, FLOOR)) * STEPS) + 1.0
    fixed = jnp.round(part * (TOP * jnp.exp2(code * (-1.0 / STEPS))))
    code = jnp.broadcast_to(code, (CODE_ROWS, part.shape[1]))
    return fixed.astype(jnp.int32).astype(jnp.int16), code.astype(jnp.int32).astype(jnp.int16)


def decode(message, rows):
    fixed = message[:rows, :].astype(jnp.int32).astype(jnp.float32)
    code = message[rows:, :].astype(jnp.int32).astype(jnp.float32)[:1]
    return fixed * (jnp.exp2(code * (1.0 / STEPS)) * (1.0 / TOP))


def share(total, quarter, own_ref, out_refs, first):
    rows = own_ref.shape[0]
    columns = slice(first, first + total.shape[2])
    own_ref[:, columns] = total[quarter]
    for mask in range(1, QUARTERS):
        fixed, code = encode(total[quarter ^ mask])
        out_refs[mask - 1][:rows, columns] = fixed
        out_refs[mask - 1][rows:, columns] = code


def own_kernel(place, acts, grads, act_factors, grad_factors,
               act_rows, grad_rows, own, out1, out2, out3,
               act_held, grad_held, total, act_sems, grad_sems):
    quarter = place[0]
    rows = own.shape[0]
    copies = []
    for source, rows_ref, factor, held, sems in (
        (acts, act_rows, act_factors, act_held, act_sems),
        (grads, grad_rows, grad_factors, grad_held, grad_sems),
    ):
        mine = []
        for step in range(source.shape[1] // CHUNK):
            depth = pl.ds(step * CHUNK, CHUNK)
            pair = (
                pltpu.make_async_copy(source.at[:, depth], rows_ref.at[:, depth], sems.at[0, step]),
                pltpu.make_async_copy(factor.at[depth, :], held.at[depth, :], sems.at[1, step]),
            )
            for copy in pair:
                copy.start()
            mine.append(pair)
        copies.append(mine)
    first = 0
    for mine, rows_ref, held in ((copies[0], act_rows, act_held), (copies[1], grad_rows, grad_held)):
        for step, pair in enumerate(mine):
            for copy in pair:
                copy.wait()
            depth = slice(step * CHUNK, (step + 1) * CHUNK)
            part = dot(rows_ref[:, depth], held[depth, :])
            for quarter_at in range(QUARTERS):
                block = part[quarter_at * rows:(quarter_at + 1) * rows]
                if step == 0:
                    total[quarter_at] = block
                else:
                    total[quarter_at] += block
        share(total, quarter, own, (out1, out2, out3), first)
        first += held.shape[1]


def other_kernel(place, act_rows, grad_rows, act_factors, grad_factors, own, out1, out2, out3, total):
    quarter = place[0]
    rows = own.shape[0]
    first = 0
    for rows_ref, factor in ((grad_rows, grad_factors), (act_rows, act_factors)):
        part = dot(rows_ref[...], factor[...])
        for quarter_at in range(QUARTERS):
            total[quarter_at] = part[quarter_at * rows:(quarter_at + 1) * rows]
        share(total, quarter, own, (out1, out2, out3), first)
        first += factor.shape[1]


def score_kernel(place, lengths, mine, mine1, mine2, mine3, other, other1, other2, other3, out):
    quarter, position = place[0], place[1]
    rows, width = mine.shape[0], mine.shape[1] // 2
    seq_part = lengths.shape[0] // QUARTERS
    pad_rows = rows // seq_part
    queries = width // RANK
    column = lax.broadcasted_iota(jnp.int32, (width, LANES), 0) // RANK
    lane = lax.broadcasted_iota(jnp.int32, (width, LANES), 1)
    offsets = lax.broadcasted_iota(jnp.int32, (pad_rows, width), 0)
    line = lax.broadcasted_iota(jnp.int32, out.shape, 0)
    result = jnp.zeros(out.shape, jnp.float32)
    units = (
        (mine, (mine1, mine2, mine3), position),
        (other, (other1, other2, other3), 1 - position),
    )
    for own, received, half in units:
        full = own[...]
        for message in received:
            full = full + decode(message[...], rows)
        pair = full[:, :width] * full[:, width:]
        pick = (lane == column + half * queries).astype(jnp.float32)
        for seq in range(seq_part):
            live = offsets < lengths[quarter * seq_part + seq]
            sums = jnp.sum(
                jnp.where(live, pair[seq * pad_rows:(seq + 1) * pad_rows], 0.0), axis=0, keepdims=True
            )
            sums = jnp.broadcast_to(sums, (8, width))
            scores = jnp.dot(
                sums, pick, precision=lax.Precision.HIGHEST, preferred_element_type=jnp.float32
            )[:1]
            at = (position * QUARTERS + quarter) * seq_part + seq
            result = result + jnp.where(line == at, scores, 0.0)
    out[...] = result


def on_device(acts, grads, act_factors, grad_factors, lengths):
    loop_count = lax.axis_size("loop")
    layer_count = lax.axis_size("layer")
    quarter = lax.axis_index("layer") % QUARTERS
    place = jnp.stack([quarter, lax.axis_index("loop")]).astype(jnp.int32)
    acts, grads, act_factors, grad_factors = acts[0], grads[0], act_factors[0], grad_factors[0]
    seq_dev = lengths.shape[0]
    tok_rows, width = acts.shape[0], act_factors.shape[1]
    rows = tok_rows // QUARTERS
    queries = width * loop_count // RANK

    other_grad = from_partner(grad_factors, "loop", 1)
    other_act = from_partner(act_factors, "loop", 1)

    own_shape = pltpu.VMEM((rows, 2 * width), jnp.float32)
    out_shape = pltpu.VMEM((rows + CODE_ROWS, 2 * width), jnp.int16)
    total_shape = pltpu.VMEM((QUARTERS, rows, width), jnp.float32)
    act_rows, grad_rows, mine, *mine_out = pl.pallas_call(
        own_kernel,
        name="own_columns",
        out_shape=(
            pltpu.VMEM(acts.shape, acts.dtype), pltpu.VMEM(grads.shape, grads.dtype),
            own_shape, out_shape, out_shape, out_shape,
        ),
        in_specs=[IN_SMEM, IN_HBM, IN_HBM, IN_HBM, IN_HBM],
        out_specs=(IN_VMEM,) * 6,
        scratch_shapes=[
            pltpu.VMEM(act_factors.shape, act_factors.dtype),
            pltpu.VMEM(grad_factors.shape, grad_factors.dtype),
            total_shape,
            pltpu.SemaphoreType.DMA((2, acts.shape[1] // CHUNK)),
            pltpu.SemaphoreType.DMA((2, grads.shape[1] // CHUNK)),
        ],
        compiler_params=pltpu.CompilerParams(vmem_limit_bytes=24 * MIB),
        cost_estimate=pl.CostEstimate(flops=2 * tok_rows * width * 9216, bytes_accessed=12 * MIB, transcendentals=0),
    )(place, acts, grads, act_factors, grad_factors)
    mine_in = [from_partner(mine_out[mask - 1], "layer", mask) for mask in range(1, QUARTERS)]

    vmem = lambda x: pltpu.with_memory_space_constraint(x, pltpu.VMEM)
    other, *other_out = pl.pallas_call(
        other_kernel,
        name="other_columns",
        out_shape=(own_shape, out_shape, out_shape, out_shape),
        in_specs=[IN_SMEM] + [IN_VMEM] * 4,
        out_specs=(IN_VMEM,) * 4,
        scratch_shapes=[total_shape],
        compiler_params=pltpu.CompilerParams(vmem_limit_bytes=24 * MIB),
        cost_estimate=pl.CostEstimate(flops=2 * tok_rows * width * 9216, bytes_accessed=0, transcendentals=0),
    )(place, vmem(act_rows), vmem(grad_rows), vmem(other_act), vmem(other_grad))
    other_in = [from_partner(other_out[mask - 1], "layer", mask) for mask in range(1, QUARTERS)]

    total = pl.pallas_call(
        score_kernel,
        name="scores",
        out_shape=pltpu.VMEM((seq_dev * loop_count, LANES), jnp.float32),
        in_specs=[IN_SMEM, IN_SMEM] + [IN_VMEM] * 8,
        out_specs=IN_VMEM,
    )(place, lengths, vmem(mine), *map(vmem, mine_in), vmem(other), *map(vmem, other_in))

    total = total + from_partner(total, "loop", 1)
    gathered = [from_partner(total, "layer", mask) for mask in range(1, QUARTERS)]
    total = total + gathered[0] + gathered[1] + gathered[2]
    mask = QUARTERS
    while mask < layer_count:
        total = total + from_partner(total, "layer", mask)
        mask *= 2
    return total[:, :queries]


def solution(mesh):
    in_specs = (
        P("layer", ("groups", "loop"), None),
        P("layer", ("groups", "loop"), None),
        P("layer", None, "loop"),
        P("layer", None, "loop"),
        P(("groups", "loop")),
    )
    out_specs = P("groups", None)
    return jax.shard_map(
        on_device, mesh=mesh, in_specs=in_specs, out_specs=out_specs, check_vma=False
    )
```

time: 52.1 us -> 45.1 us (0.87)
  matrix products: 15.5 us -> 0 us
  Pallas kernels: 0 us -> 11.1 us
  other arithmetic: 3.87 us -> 0.68 us
  local copies, waits for them, and re-layouts: 4.23 us -> 7.24 us
  waiting for transfers between devices: 13.2 us -> 10.9 us
    dot_general x4 -> x0, matrix products: 15.5 us -> none  [project(): return jnp.dot(rows, factor, preferred_element_type=jnp.float32)]
    pallas_call x0 -> x3, Pallas kernels: none -> 11.1 us  [the longest x1 5.75 us: on_device(): pl.pallas_call(own_kernel, name='own_columns', out_shape=(pltpu.VMEM(acts...]
    unnamed x4 -> x10, local copies, waits for them, and re-layouts: 0.89 us -> 7.24 us
    ppermute x13, waiting for transfers between devices: 13.2 us -> 10.9 us  [from_partner(): return lax.ppermute(value, axis, pairs)]
    concatenate x2 -> x0, local copies, waits for them, and re-layouts: 1.66 us -> none  [the longest x1 1.39 us: on_device(): jnp.concatenate([project(acts[0], other_act), project(grads[0], other_gra...]
    add x2 -> x1, other arithmetic: 1.14 us -> 0.01 us  [on_device(): total = total + from_partner(total, 'loop', 1)]
    concatenate x3 -> x0, other arithmetic: 1.06 us -> none  [the longest x1 0.93 us: on_device(): jnp.concatenate([project(acts[0], other_act), project(grads[0], other_gra...]
    squeeze x2 -> x0, local copies, waits for them, and re-layouts: 0.89 us -> none  [sum_over_quarters(): out = lax.dynamic_index_in_dim(parts, quarter ^ mask, 0, keepdims=False)]
  transfers between devices with their start and end apart: 13 -> 13, of which waited for: 8 -> 8; matrix products, arithmetic and copies ran while one was open for 41% -> 0% of each run, Pallas kernels for 0% -> 22%
where the time goes in v2:
time: 45.1 us; the launch traced here: 44.8 us
  starting transfers between devices  14.8 us (33%)
  Pallas kernels  11.1 us (25%)
  waiting for transfers between devices  10.9 us (24%)
  local copies, waits for them, and re-layouts  7.24 us (16%)
  other arithmetic  0.68 us (2%)
    ppermute x13, starting transfers between devices, from_partner(): return lax.ppermute(value, axis, pairs)  14.8 us
    ppermute x13, waiting for transfers between devices, from_partner(): return lax.ppermute(value, axis, pairs)  10.9 us
    unnamed x10, local copies, waits for them, and re-layouts  7.24 us
    pallas_call x1, Pallas kernels, on_device(): pl.pallas_call(own_kernel, name='own_columns', out_shape=(pltpu.VMEM(acts...  5.75 us
    pallas_call x1, Pallas kernels, on_device(): pl.pallas_call(other_kernel, name='other_columns', out_shape=(own_shape,...  4.22 us
    pallas_call x1, Pallas kernels, on_device(): pl.pallas_call(score_kernel, name='scores', out_shape=pltpu.VMEM((seq_dev...  1.11 us
  transfers between devices with their start and end apart: 13, of which 8 were waited for; matrix products, arithmetic and copies ran while one was open for 0% of the time, Pallas kernels for 22%

profile of v2, /device:TPU:0, one launch (start us, length us, event | category | flops | bytes accessed | tf_op | source)
XLA Modules:
  0.0 44.8 jit_solution(7101657771831434922)
XLA Ops:
  0.0 0.5 %collective-permute-start.4 = (bf16[7168,256]{1,0:T(8,128)(2,1)}, bf16[7168,256]{1,0:T(8,128)(2,1)}, u32[]{:S(2)}, u32[]{:S(2)}) collective-permute-start(bf16[7168,256]{1,0:T(8,128)(2,1)} %bitcast.8), channel_id=1, source_target_pairs={{0,1},{1,0},{2,3},{3,2},{4,5},{5,4},{6,7},{7,6},{8,9},{9,8},{10,11... | collective-permute-start | bytes 11010056 | tf_op jit(solution)/shard_map/ppermute | solution.py:27
  0.5 0.1 collective-permute-start.3
  0.5 0.1 pad_add_fusion.place
  0.6 0.0 copy-start.4
  0.6 0.0 copy-start
  0.6 2.6 %copy-done = bf16[1,384,7168]{2,1,0:T(8,128)(2,1)S(1)} copy-done((bf16[1,384,7168]{2,1,0:T(8,128)(2,1)S(1)}, bf16[1,384,7168]{2,1,0:T(8,128)(2,1)}, u32[]{:S(2)}) %copy-start) | copy-done | bytes 5505048
  3.2 0.0 copy-start.1
  3.2 2.0 %copy-done.1 = bf16[1,7168,256]{2,1,0:T(8,128)(2,1)S(1)} copy-done((bf16[1,7168,256]{2,1,0:T(8,128)(2,1)S(1)}, bf16[1,7168,256]{2,1,0:T(8,128)(2,1)}, u32[]{:S(2)}) %copy-start.1) | copy-done | bytes 3670040
  5.2 0.0 copy-start.2
  5.2 1.4 %copy-done.2 = bf16[1,384,2048]{2,1,0:T(8,128)(2,1)S(1)} copy-done((bf16[1,384,2048]{2,1,0:T(8,128)(2,1)S(1)}, bf16[1,384,2048]{2,1,0:T(8,128)(2,1)}, u32[]{:S(2)}) %copy-start.2) | copy-done | bytes 1572888
  6.6 0.0 copy-start.3
  6.6 1.2 %copy-done.3 = bf16[1,2048,256]{2,1,0:T(8,128)(2,1)S(1)} copy-done((bf16[1,2048,256]{2,1,0:T(8,128)(2,1)S(1)}, bf16[1,2048,256]{2,1,0:T(8,128)(2,1)}, u32[]{:S(2)}) %copy-start.3) | copy-done | bytes 1048600
  7.8 5.8 %own_columns.1 = (bf16[384,2048]{1,0:T(8,128)(2,1)S(1)}, bf16[384,7168]{1,0:T(8,128)(2,1)S(1)}, f32[96,512]{1,0:T(8,128)S(1)}, s16[112,512]{1,0:T(8,128)(2,1)S(1...) custom-call(s32[2]{0:T(128)S(1)} %pad_add_fusion.place, bf16[384,2048]{1,0:T(8,128)(2,1)S(1)} %bitcast.10, ...), custom_call_target="tpu_custom_call" | custom-call | flops 1811939328 | bytes 12582912 | tf_op jit(solution)/shard_map/own_columns/pallas_call | solution.py:160
  13.6 3.0 %collective-permute-start = (s16[112,512]{1,0:T(8,128)(2,1)S(1)}, s16[112,512]{1,0:T(8,128)(2,1)S(1)}, u32[]{:S(2)}, u32[]{:S(2)}) collective-permute-start(s16[112,512]{1,0:T(8,128)(2,1)S(1)} %get-tuple-element.16), channel_id=1, source_target_pairs={{0,2},{2,0},{4,6},{6,4},{8,10},{10,8},{12,14},{14,12},{1,3},{3,1},... | collective-permute-start | bytes 344072 | tf_op jit(solution)/shard_map/ppermute | solution.py:27
  16.6 1.6 %collective-permute-start.1 = (s16[112,512]{1,0:T(8,128)(2,1)S(1)}, s16[112,512]{1,0:T(8,128)(2,1)S(1)}, u32[]{:S(2)}, u32[]{:S(2)}) collective-permute-start(s16[112,512]{1,0:T(8,128)(2,1)S(1)} %get-tuple-element.17), channel_id=1, source_target_pairs={{0,4},{2,6},{4,0},{6,2},{8,12},{10,14},{12,8},{14,10},{1,5},{3,7},... | collective-permute-start | bytes 344072 | tf_op jit(solution)/shard_map/ppermute | solution.py:27
  18.2 0.0 collective-permute-start.2
  18.2 0.0 collective-permute-done.3.act_factors
  18.2 0.0 collective-permute-done.4.grad_factors
  18.2 0.0 copy-done.4
  18.2 4.2 %other_columns.1 = (f32[96,512]{1,0:T(8,128)S(1)}, s16[112,512]{1,0:T(8,128)(2,1)S(1)}, s16[112,512]{1,0:T(8,128)(2,1)S(1)}, s16[112,512]{1,0:T(8,128)(2,1)S(1)}) custom-call(s32[2]{0:T(128)S(1)} %pad_add_fusion.place, bf16[384,2048]{1,0:T(8,128)(2,1)S(1)} %get-tuple-element.19.act_rows, bf16[384,7168]{1,0:T(8,128)(2,1)S(1)} %get-tuple-element.20.grad_rows, ...), custom_call_target="tpu_custom_call" | custom-call | flops 1811939328 | tf_op jit(solution)/shard_map/other_columns/pallas_call | solution.py:182
  22.4 2.0 %collective-permute-start.5 = (s16[112,512]{1,0:T(8,128)(2,1)S(1)}, s16[112,512]{1,0:T(8,128)(2,1)S(1)}, u32[]{:S(2)}, u32[]{:S(2)}) collective-permute-start(s16[112,512]{1,0:T(8,128)(2,1)S(1)} %get-tuple-element.22), channel_id=1, source_target_pairs={{0,2},{2,0},{4,6},{6,4},{8,10},{10,8},{12,14},{14,12},{1,3},{3,1},... | collective-permute-start | bytes 344072 | tf_op jit(solution)/shard_map/ppermute | solution.py:27
  24.4 1.6 %collective-permute-start.6 = (s16[112,512]{1,0:T(8,128)(2,1)S(1)}, s16[112,512]{1,0:T(8,128)(2,1)S(1)}, u32[]{:S(2)}, u32[]{:S(2)}) collective-permute-start(s16[112,512]{1,0:T(8,128)(2,1)S(1)} %get-tuple-element.23), channel_id=1, source_target_pairs={{0,4},{2,6},{4,0},{6,2},{8,12},{10,14},{12,8},{14,10},{1,5},{3,7},... | collective-permute-start | bytes 344072 | tf_op jit(solution)/shard_map/ppermute | solution.py:27
  26.0 0.0 collective-permute-done.mine1
  26.0 0.0 collective-permute-start.7
  26.0 0.0 collective-permute-done.1.mine2
  26.0 0.0 collective-permute-done.2.mine3
  26.0 2.0 %collective-permute-done.5.other1 = s16[112,512]{1,0:T(8,128)(2,1)S(1)} collective-permute-done((s16[112,512]{1,0:T(8,128)(2,1)S(1)}, s16[112,512]{1,0:T(8,128)(2,1)S(1)}, u32[]{:S(2)}, u32[]{:S(2)}) %collective-permute-start.5) | collective-permute-done | bytes 114720 | tf_op jit(solution)/shard_map/ppermute | solution.py:27
  28.0 1.6 %collective-permute-done.6.other2 = s16[112,512]{1,0:T(8,128)(2,1)S(1)} collective-permute-done((s16[112,512]{1,0:T(8,128)(2,1)S(1)}, s16[112,512]{1,0:T(8,128)(2,1)S(1)}, u32[]{:S(2)}, u32[]{:S(2)}) %collective-permute-start.6) | collective-permute-done | bytes 114720 | tf_op jit(solution)/shard_map/ppermute | solution.py:27
  29.6 2.1 %collective-permute-done.7.other3 = s16[112,512]{1,0:T(8,128)(2,1)S(1)} collective-permute-done((s16[112,512]{1,0:T(8,128)(2,1)S(1)}, s16[112,512]{1,0:T(8,128)(2,1)S(1)}, u32[]{:S(2)}, u32[]{:S(2)}) %collective-permute-start.7) | collective-permute-done | bytes 114720 | tf_op jit(solution)/shard_map/ppermute | solution.py:27
  31.7 1.1 %scores.1 = f32[8,128]{1,0:T(8,128)S(1)} custom-call(s32[2]{0:T(128)} %copy-done.4, s32[4]{0:T(128)} %lengths.1, f32[96,512]{1,0:T(8,128)S(1)} %get-tuple-element.15.mine, s16[112,512]{1,0:T(8,128)(2,1)S(1)} %collective-permute-done.mine1, s16[112,512]{1,0:T(8,128)(2,1)S(1)} %collective-permute-done.1.mine2, ...), custom_call_target="tpu_custom_call" | custom-call | tf_op jit(solution)/shard_map/scores/pallas_call | solution.py:194
  32.8 0.1 collective-permute-start.8
  32.9 1.2 %collective-permute-done.8 = f32[8,128]{1,0:T(8,128)S(1)} collective-permute-done((f32[8,128]{1,0:T(8,128)S(1)}, f32[8,128]{1,0:T(8,128)S(1)}, u32[]{:S(2)}, u32[]{:S(2)}) %collective-permute-start.8) | collective-permute-done | bytes 4128 | tf_op jit(solution)/shard_map/ppermute | solution.py:27
  34.0 1.6 %collective-permute-start.11 = (f32[8,128]{1,0:T(8,128)S(1)}, f32[8,128]{1,0:T(8,128)S(1)}, u32[]{:S(2)}, u32[]{:S(2)}) collective-permute-start(f32[8,128]{1,0:T(8,128)S(1)} %add.20), channel_id=1, source_target_pairs={{0,6},{2,4},{4,2},{6,0},{8,14},{10,12},{12,10},{14,8},{1,7},{3,5},... | collective-permute-start | bytes 12296 | tf_op jit(solution)/shard_map/ppermute | solution.py:27
  35.6 0.5 %collective-permute-start.10 = (f32[8,128]{1,0:T(8,128)S(1)}, f32[8,128]{1,0:T(8,128)S(1)}, u32[]{:S(2)}, u32[]{:S(2)}) collective-permute-start(f32[8,128]{1,0:T(8,128)S(1)} %add.20), channel_id=1, source_target_pairs={{0,4},{2,6},{4,0},{6,2},{8,12},{10,14},{12,8},{14,10},{1,5},{3,7},... | collective-permute-start | bytes 12296 | tf_op jit(solution)/shard_map/ppermute | solution.py:27
  36.1 1.4 %collective-permute-start.9 = (f32[8,128]{1,0:T(8,128)S(1)}, f32[8,128]{1,0:T(8,128)S(1)}, u32[]{:S(2)}, u32[]{:S(2)}) collective-permute-start(f32[8,128]{1,0:T(8,128)S(1)} %add.20), channel_id=1, source_target_pairs={{0,2},{2,0},{4,6},{6,4},{8,10},{10,8},{12,14},{14,12},{1,3},{3,1},... | collective-permute-start | bytes 12296 | tf_op jit(solution)/shard_map/ppermute | solution.py:27
  37.5 1.0 %collective-permute-done.11 = f32[8,128]{1,0:T(8,128)S(1)} collective-permute-done((f32[8,128]{1,0:T(8,128)S(1)}, f32[8,128]{1,0:T(8,128)S(1)}, u32[]{:S(2)}, u32[]{:S(2)}) %collective-permute-start.11) | collective-permute-done | bytes 4128 | tf_op jit(solution)/shard_map/ppermute | solution.py:27
  38.5 0.7 %collective-permute-done.10 = f32[8,128]{1,0:T(8,128)S(1)} collective-permute-done((f32[8,128]{1,0:T(8,128)S(1)}, f32[8,128]{1,0:T(8,128)S(1)}, u32[]{:S(2)}, u32[]{:S(2)}) %collective-permute-start.10) | collective-permute-done | bytes 4128 | tf_op jit(solution)/shard_map/ppermute | solution.py:27
  39.2 0.5 %collective-permute-done.9 = f32[8,128]{1,0:T(8,128)S(1)} collective-permute-done((f32[8,128]{1,0:T(8,128)S(1)}, f32[8,128]{1,0:T(8,128)S(1)}, u32[]{:S(2)}, u32[]{:S(2)}) %collective-permute-start.9) | collective-permute-done | bytes 4128 | tf_op jit(solution)/shard_map/ppermute | solution.py:27
  39.7 2.6 %collective-permute-start.12 = (f32[8,128]{1,0:T(8,128)S(1)}, f32[8,128]{1,0:T(8,128)S(1)}, u32[]{:S(2)}, u32[]{:S(2)}) collective-permute-start(f32[8,128]{1,0:T(8,128)S(1)} %add_add_fusion), channel_id=1, source_target_pairs={{0,8},{2,10},{4,12},{6,14},{8,0},{10,2},{12,4},{14,6},{1,9},{3,11}... | collective-permute-start | bytes 12296 | tf_op jit(solution)/shard_map/ppermute | solution.py:27
  42.3 1.9 %collective-permute-done.12 = f32[8,128]{1,0:T(8,128)S(1)} collective-permute-done((f32[8,128]{1,0:T(8,128)S(1)}, f32[8,128]{1,0:T(8,128)S(1)}, u32[]{:S(2)}, u32[]{:S(2)}) %collective-permute-start.12) | collective-permute-done | bytes 4128 | tf_op jit(solution)/shard_map/ppermute | solution.py:27
  44.2 0.6 %add.24 = f32[8,128]{1,0:T(8,128)} add(f32[8,128]{1,0:T(8,128)S(1)} %add_add_fusion, f32[8,128]{1,0:T(8,128)S(1)} %collective-permute-done.12) | non-fusion elementwise | flops 1024 | bytes 12288 | tf_op jit(solution)/shard_map/add | solution.py:207
  (2 shorter events, 0.0 us)
Async XLA Ops:
  0.0 18.2 %collective-permute-start.4 = (bf16[7168,256]{1,0:T(8,128)(2,1)}, bf16[7168,256]{1,0:T(8,128)(2,1)}, u32[]{:S(2)}, u32[]{:S(2)}) collective-permute-start(bf16[7168,256]{1,0:T(8,128)(2,1)} %bitcast.8), channel_id=1, source_target_pairs={{0,1},{1,0},{2,3},{3,2},{4,5},{5,4},{6,7},{7,6},{8,9},{9,8},{10,11... | collective-permute-start | bytes 11010056 | tf_op jit(solution)/shard_map/ppermute | solution.py:27
  0.5 17.7 %collective-permute-start.3 = (bf16[2048,256]{1,0:T(8,128)(2,1)}, bf16[2048,256]{1,0:T(8,128)(2,1)S(1)}, u32[]{:S(2)}, u32[]{:S(2)}) collective-permute-start(bf16[2048,256]{1,0:T(8,128)(2,1)} %bitcast.11), channel_id=1, source_target_pairs={{0,1},{1,0},{2,3},{3,2},{4,5},{5,4},{6,7},{7,6},{8,9},{9,8},{10,11... | collective-permute-start | bytes 3145736 | tf_op jit(solution)/shard_map/ppermute | solution.py:27
  0.6 17.6 %copy-start.4 = (s32[2]{0:T(128)}, s32[2]{0:T(128)S(1)}, u32[]{:S(2)}) copy-start(s32[2]{0:T(128)S(1)} %pad_add_fusion.place) | copy-start | bytes 28
  0.6 2.6 %copy-start = (bf16[1,384,7168]{2,1,0:T(8,128)(2,1)S(1)}, bf16[1,384,7168]{2,1,0:T(8,128)(2,1)}, u32[]{:S(2)}) copy-start(bf16[1,384,7168]{2,1,0:T(8,128)(2,1)} %param.6) | copy-start | bytes 16515076
  3.2 2.0 %copy-start.1 = (bf16[1,7168,256]{2,1,0:T(8,128)(2,1)S(1)}, bf16[1,7168,256]{2,1,0:T(8,128)(2,1)}, u32[]{:S(2)}) copy-start(bf16[1,7168,256]{2,1,0:T(8,128)(2,1)} %param.8) | copy-start | bytes 11010052
  5.2 1.4 %copy-start.2 = (bf16[1,384,2048]{2,1,0:T(8,128)(2,1)S(1)}, bf16[1,384,2048]{2,1,0:T(8,128)(2,1)}, u32[]{:S(2)}) copy-start(bf16[1,384,2048]{2,1,0:T(8,128)(2,1)} %param.5) | copy-start | bytes 4718596
  6.6 1.2 %copy-start.3 = (bf16[1,2048,256]{2,1,0:T(8,128)(2,1)S(1)}, bf16[1,2048,256]{2,1,0:T(8,128)(2,1)}, u32[]{:S(2)}) copy-start(bf16[1,2048,256]{2,1,0:T(8,128)(2,1)} %param.7) | copy-start | bytes 3145732
  13.6 12.4 %collective-permute-start = (s16[112,512]{1,0:T(8,128)(2,1)S(1)}, s16[112,512]{1,0:T(8,128)(2,1)S(1)}, u32[]{:S(2)}, u32[]{:S(2)}) collective-permute-start(s16[112,512]{1,0:T(8,128)(2,1)S(1)} %get-tuple-element.16), channel_id=1, source_target_pairs={{0,2},{2,0},{4,6},{6,4},{8,10},{10,8},{12,14},{14,12},{1,3},{3,1},... | collective-permute-start | bytes 344072 | tf_op jit(solution)/shard_map/ppermute | solution.py:27
  16.6 9.4 %collective-permute-start.1 = (s16[112,512]{1,0:T(8,128)(2,1)S(1)}, s16[112,512]{1,0:T(8,128)(2,1)S(1)}, u32[]{:S(2)}, u32[]{:S(2)}) collective-permute-start(s16[112,512]{1,0:T(8,128)(2,1)S(1)} %get-tuple-element.17), channel_id=1, source_target_pairs={{0,4},{2,6},{4,0},{6,2},{8,12},{10,14},{12,8},{14,10},{1,5},{3,7},... | collective-permute-start | bytes 344072 | tf_op jit(solution)/shard_map/ppermute | solution.py:27
  18.2 7.8 %collective-permute-start.2 = (s16[112,512]{1,0:T(8,128)(2,1)S(1)}, s16[112,512]{1,0:T(8,128)(2,1)S(1)}, u32[]{:S(2)}, u32[]{:S(2)}) collective-permute-start(s16[112,512]{1,0:T(8,128)(2,1)S(1)} %get-tuple-element.18), channel_id=1, source_target_pairs={{0,6},{2,4},{4,2},{6,0},{8,14},{10,12},{12,10},{14,8},{1,7},{3,5},... | collective-permute-start | bytes 344072 | tf_op jit(solution)/shard_map/ppermute | solution.py:27
  22.4 5.5 %collective-permute-start.5 = (s16[112,512]{1,0:T(8,128)(2,1)S(1)}, s16[112,512]{1,0:T(8,128)(2,1)S(1)}, u32[]{:S(2)}, u32[]{:S(2)}) collective-permute-start(s16[112,512]{1,0:T(8,128)(2,1)S(1)} %get-tuple-element.22), channel_id=1, source_target_pairs={{0,2},{2,0},{4,6},{6,4},{8,10},{10,8},{12,14},{14,12},{1,3},{3,1},... | collective-permute-start | bytes 344072 | tf_op jit(solution)/shard_map/ppermute | solution.py:27
  24.4 5.2 %collective-permute-start.6 = (s16[112,512]{1,0:T(8,128)(2,1)S(1)}, s16[112,512]{1,0:T(8,128)(2,1)S(1)}, u32[]{:S(2)}, u32[]{:S(2)}) collective-permute-start(s16[112,512]{1,0:T(8,128)(2,1)S(1)} %get-tuple-element.23), channel_id=1, source_target_pairs={{0,4},{2,6},{4,0},{6,2},{8,12},{10,14},{12,8},{14,10},{1,5},{3,7},... | collective-permute-start | bytes 344072 | tf_op jit(solution)/shard_map/ppermute | solution.py:27
  26.0 5.7 %collective-permute-start.7 = (s16[112,512]{1,0:T(8,128)(2,1)S(1)}, s16[112,512]{1,0:T(8,128)(2,1)S(1)}, u32[]{:S(2)}, u32[]{:S(2)}) collective-permute-start(s16[112,512]{1,0:T(8,128)(2,1)S(1)} %get-tuple-element.24), channel_id=1, source_target_pairs={{0,6},{2,4},{4,2},{6,0},{8,14},{10,12},{12,10},{14,8},{1,7},{3,5},... | collective-permute-start | bytes 344072 | tf_op jit(solution)/shard_map/ppermute | solution.py:27
  32.8 1.2 %collective-permute-start.8 = (f32[8,128]{1,0:T(8,128)S(1)}, f32[8,128]{1,0:T(8,128)S(1)}, u32[]{:S(2)}, u32[]{:S(2)}) collective-permute-start(f32[8,128]{1,0:T(8,128)S(1)} %scores.1), channel_id=1, source_target_pairs={{0,1},{1,0},{2,3},{3,2},{4,5},{5,4},{6,7},{7,6},{8,9},{9,8},{10,11... | collective-permute-start | bytes 12296 | tf_op jit(solution)/shard_map/ppermute | solution.py:27
  34.0 4.5 %collective-permute-start.11 = (f32[8,128]{1,0:T(8,128)S(1)}, f32[8,128]{1,0:T(8,128)S(1)}, u32[]{:S(2)}, u32[]{:S(2)}) collective-permute-start(f32[8,128]{1,0:T(8,128)S(1)} %add.20), channel_id=1, source_target_pairs={{0,6},{2,4},{4,2},{6,0},{8,14},{10,12},{12,10},{14,8},{1,7},{3,5},... | collective-permute-start | bytes 12296 | tf_op jit(solution)/shard_map/ppermute | solution.py:27
  35.6 3.6 %collective-permute-start.10 = (f32[8,128]{1,0:T(8,128)S(1)}, f32[8,128]{1,0:T(8,128)S(1)}, u32[]{:S(2)}, u32[]{:S(2)}) collective-permute-start(f32[8,128]{1,0:T(8,128)S(1)} %add.20), channel_id=1, source_target_pairs={{0,4},{2,6},{4,0},{6,2},{8,12},{10,14},{12,8},{14,10},{1,5},{3,7},... | collective-permute-start | bytes 12296 | tf_op jit(solution)/shard_map/ppermute | solution.py:27
  36.1 3.6 %collective-permute-start.9 = (f32[8,128]{1,0:T(8,128)S(1)}, f32[8,128]{1,0:T(8,128)S(1)}, u32[]{:S(2)}, u32[]{:S(2)}) collective-permute-start(f32[8,128]{1,0:T(8,128)S(1)} %add.20), channel_id=1, source_target_pairs={{0,2},{2,0},{4,6},{6,4},{8,10},{10,8},{12,14},{14,12},{1,3},{3,1},... | collective-permute-start | bytes 12296 | tf_op jit(solution)/shard_map/ppermute | solution.py:27
  39.7 4.5 %collective-permute-start.12 = (f32[8,128]{1,0:T(8,128)S(1)}, f32[8,128]{1,0:T(8,128)S(1)}, u32[]{:S(2)}, u32[]{:S(2)}) collective-permute-start(f32[8,128]{1,0:T(8,128)S(1)} %add_add_fusion), channel_id=1, source_target_pairs={{0,8},{2,10},{4,12},{6,14},{8,0},{10,2},{12,4},{14,6},{1,9},{3,11}... | collective-permute-start | bytes 12296 | tf_op jit(solution)/shard_map/ppermute | solution.py:27

commit v3 on v2

--- a/solution.py
+++ b/solution.py
@@ -175,7 +175,7 @@
         ],
         compiler_params=pltpu.CompilerParams(vmem_limit_bytes=24 * MIB),
         cost_estimate=pl.CostEstimate(flops=2 * tok_rows * width * 9216, bytes_accessed=12 * MIB, transcendentals=0),
-    )(place, acts, grads, act_factors, grad_factors)
+    )(place, *(pltpu.with_memory_space_constraint(x, pltpu.HBM) for x in (acts, grads, act_factors, grad_factors)))
     mine_in = [from_partner(mine_out[mask - 1], "layer", mask) for mask in range(1, QUARTERS)]
 
     vmem = lambda x: pltpu.with_memory_space_constraint(x, pltpu.VMEM)

time: 45.1 us -> 40.7 us (0.902)
  local copies, waits for them, and re-layouts: 7.24 us -> 0.01 us
  Pallas kernels: 11.1 us -> 14.1 us
    unnamed x10 -> x2, local copies, waits for them, and re-layouts: 7.24 us -> 0.01 us
    pallas_call x1, Pallas kernels: 5.75 us -> 8.72 us  [on_device(): pl.pallas_call(own_kernel, name='own_columns', out_shape=(pltpu.VMEM(acts...]
  transfers between devices with their start and end apart: 13 -> 13, of which waited for: 8 -> 8; matrix products, arithmetic and copies ran while one was open for 0% -> 0% of each run, Pallas kernels for 22% -> 32%
where the time goes in v3:
time: 40.7 us; the launch traced here: 40.6 us
  starting transfers between devices  14.8 us (36%)
  Pallas kernels  14.1 us (35%)
  waiting for transfers between devices  10.9 us (27%)
  other arithmetic  0.68 us (2%)
    ppermute x13, starting transfers between devices, from_partner(): return lax.ppermute(value, axis, pairs)  14.8 us
    ppermute x13, waiting for transfers between devices, from_partner(): return lax.ppermute(value, axis, pairs)  10.9 us
    pallas_call x1, Pallas kernels, on_device(): pl.pallas_call(own_kernel, name='own_columns', out_shape=(pltpu.VMEM(acts...  8.72 us
    pallas_call x1, Pallas kernels, on_device(): pl.pallas_call(other_kernel, name='other_columns', out_shape=(own_shape,...  4.22 us
    pallas_call x1, Pallas kernels, on_device(): pl.pallas_call(score_kernel, name='scores', out_shape=pltpu.VMEM((seq_dev...  1.11 us
  transfers between devices with their start and end apart: 13, of which 8 were waited for; matrix products, arithmetic and copies ran while one was open for 0% of the time, Pallas kernels for 32%

profile of v3, /device:TPU:0, one launch (start us, length us, event | category | flops | bytes accessed | tf_op | source)
XLA Modules:
  0.0 40.6 jit_solution(1369214428721648778)
XLA Ops:
  0.0 0.5 %collective-permute-start.4 = (bf16[7168,256]{1,0:T(8,128)(2,1)}, bf16[7168,256]{1,0:T(8,128)(2,1)}, u32[]{:S(2)}, u32[]{:S(2)}) collective-permute-start(bf16[7168,256]{1,0:T(8,128)(2,1)} %bitcast.8), channel_id=1, source_target_pairs={{0,1},{1,0},{2,3},{3,2},{4,5},{5,4},{6,7},{7,6},{8,9},{9,8},{10,11... | collective-permute-start | bytes 11010056 | tf_op jit(solution)/shard_map/ppermute | solution.py:27
  0.5 0.1 collective-permute-start.3
  0.5 0.1 pad_add_fusion.place
  0.6 0.0 copy-start
  0.6 8.7 %own_columns.1 = (bf16[384,2048]{1,0:T(8,128)(2,1)S(1)}, bf16[384,7168]{1,0:T(8,128)(2,1)S(1)}, f32[96,512]{1,0:T(8,128)S(1)}, s16[112,512]{1,0:T(8,128)(2,1)S(1...) custom-call(s32[2]{0:T(128)S(1)} %pad_add_fusion.place, bf16[384,2048]{1,0:T(8,128)(2,1)} %bitcast.10, ...), custom_call_target="tpu_custom_call" | custom-call | flops 1811939328 | bytes 12582912 | tf_op jit(solution)/shard_map/own_columns/pallas_call | solution.py:160
  9.3 3.0 %collective-permute-start = (s16[112,512]{1,0:T(8,128)(2,1)S(1)}, s16[112,512]{1,0:T(8,128)(2,1)S(1)}, u32[]{:S(2)}, u32[]{:S(2)}) collective-permute-start(s16[112,512]{1,0:T(8,128)(2,1)S(1)} %get-tuple-element.16), channel_id=1, source_target_pairs={{0,2},{2,0},{4,6},{6,4},{8,10},{10,8},{12,14},{14,12},{1,3},{3,1},... | collective-permute-start | bytes 344072 | tf_op jit(solution)/shard_map/ppermute | solution.py:27
  12.4 1.6 %collective-permute-start.1 = (s16[112,512]{1,0:T(8,128)(2,1)S(1)}, s16[112,512]{1,0:T(8,128)(2,1)S(1)}, u32[]{:S(2)}, u32[]{:S(2)}) collective-permute-start(s16[112,512]{1,0:T(8,128)(2,1)S(1)} %get-tuple-element.17), channel_id=1, source_target_pairs={{0,4},{2,6},{4,0},{6,2},{8,12},{10,14},{12,8},{14,10},{1,5},{3,7},... | collective-permute-start | bytes 344072 | tf_op jit(solution)/shard_map/ppermute | solution.py:27
  13.9 0.0 collective-permute-start.2
  13.9 0.0 collective-permute-done.3.act_factors
  13.9 0.0 collective-permute-done.4.grad_factors
  13.9 0.0 copy-done
  14.0 4.2 %other_columns.1 = (f32[96,512]{1,0:T(8,128)S(1)}, s16[112,512]{1,0:T(8,128)(2,1)S(1)}, s16[112,512]{1,0:T(8,128)(2,1)S(1)}, s16[112,512]{1,0:T(8,128)(2,1)S(1)}) custom-call(s32[2]{0:T(128)S(1)} %pad_add_fusion.place, bf16[384,2048]{1,0:T(8,128)(2,1)S(1)} %get-tuple-element.19.act_rows, bf16[384,7168]{1,0:T(8,128)(2,1)S(1)} %get-tuple-element.20.grad_rows, ...), custom_call_target="tpu_custom_call" | custom-call | flops 1811939328 | tf_op jit(solution)/shard_map/other_columns/pallas_call | solution.py:182
  18.2 2.0 %collective-permute-start.5 = (s16[112,512]{1,0:T(8,128)(2,1)S(1)}, s16[112,512]{1,0:T(8,128)(2,1)S(1)}, u32[]{:S(2)}, u32[]{:S(2)}) collective-permute-start(s16[112,512]{1,0:T(8,128)(2,1)S(1)} %get-tuple-element.22), channel_id=1, source_target_pairs={{0,2},{2,0},{4,6},{6,4},{8,10},{10,8},{12,14},{14,12},{1,3},{3,1},... | collective-permute-start | bytes 344072 | tf_op jit(solution)/shard_map/ppermute | solution.py:27
  20.1 1.6 %collective-permute-start.6 = (s16[112,512]{1,0:T(8,128)(2,1)S(1)}, s16[112,512]{1,0:T(8,128)(2,1)S(1)}, u32[]{:S(2)}, u32[]{:S(2)}) collective-permute-start(s16[112,512]{1,0:T(8,128)(2,1)S(1)} %get-tuple-element.23), channel_id=1, source_target_pairs={{0,4},{2,6},{4,0},{6,2},{8,12},{10,14},{12,8},{14,10},{1,5},{3,7},... | collective-permute-start | bytes 344072 | tf_op jit(solution)/shard_map/ppermute | solution.py:27
  21.7 0.0 collective-permute-done.mine1
  21.7 0.0 collective-permute-start.7
  21.7 0.0 collective-permute-done.1.mine2
  21.7 0.0 collective-permute-done.2.mine3
  21.7 2.0 %collective-permute-done.5.other1 = s16[112,512]{1,0:T(8,128)(2,1)S(1)} collective-permute-done((s16[112,512]{1,0:T(8,128)(2,1)S(1)}, s16[112,512]{1,0:T(8,128)(2,1)S(1)}, u32[]{:S(2)}, u32[]{:S(2)}) %collective-permute-start.5) | collective-permute-done | bytes 114720 | tf_op jit(solution)/shard_map/ppermute | solution.py:27
  23.7 1.6 %collective-permute-done.6.other2 = s16[112,512]{1,0:T(8,128)(2,1)S(1)} collective-permute-done((s16[112,512]{1,0:T(8,128)(2,1)S(1)}, s16[112,512]{1,0:T(8,128)(2,1)S(1)}, u32[]{:S(2)}, u32[]{:S(2)}) %collective-permute-start.6) | collective-permute-done | bytes 114720 | tf_op jit(solution)/shard_map/ppermute | solution.py:27
  25.3 2.1 %collective-permute-done.7.other3 = s16[112,512]{1,0:T(8,128)(2,1)S(1)} collective-permute-done((s16[112,512]{1,0:T(8,128)(2,1)S(1)}, s16[112,512]{1,0:T(8,128)(2,1)S(1)}, u32[]{:S(2)}, u32[]{:S(2)}) %collective-permute-start.7) | collective-permute-done | bytes 114720 | tf_op jit(solution)/shard_map/ppermute | solution.py:27
  27.4 1.1 %scores.1 = f32[8,128]{1,0:T(8,128)S(1)} custom-call(s32[2]{0:T(128)} %copy-done, s32[4]{0:T(128)} %lengths.1, f32[96,512]{1,0:T(8,128)S(1)} %get-tuple-element.15.mine, s16[112,512]{1,0:T(8,128)(2,1)S(1)} %collective-permute-done.mine1, s16[112,512]{1,0:T(8,128)(2,1)S(1)} %collective-permute-done.1.mine2, s16[112,512]{1,0:T(8,128)(2,1)S(1)} %collective-permute-done.2.mine3, ...), custom_call_target="tpu_custom_call" | custom-call | tf_op jit(solution)/shard_map/scores/pallas_call | solution.py:194
  28.5 0.1 collective-permute-start.8
  28.6 1.2 %collective-permute-done.8 = f32[8,128]{1,0:T(8,128)S(1)} collective-permute-done((f32[8,128]{1,0:T(8,128)S(1)}, f32[8,128]{1,0:T(8,128)S(1)}, u32[]{:S(2)}, u32[]{:S(2)}) %collective-permute-start.8) | collective-permute-done | bytes 4128 | tf_op jit(solution)/shard_map/ppermute | solution.py:27
  29.8 1.6 %collective-permute-start.11 = (f32[8,128]{1,0:T(8,128)S(1)}, f32[8,128]{1,0:T(8,128)S(1)}, u32[]{:S(2)}, u32[]{:S(2)}) collective-permute-start(f32[8,128]{1,0:T(8,128)S(1)} %add.20), channel_id=1, source_target_pairs={{0,6},{2,4},{4,2},{6,0},{8,14},{10,12},{12,10},{14,8},{1,7},{3,5},... | collective-permute-start | bytes 12296 | tf_op jit(solution)/shard_map/ppermute | solution.py:27
  31.4 0.5 %collective-permute-start.10 = (f32[8,128]{1,0:T(8,128)S(1)}, f32[8,128]{1,0:T(8,128)S(1)}, u32[]{:S(2)}, u32[]{:S(2)}) collective-permute-start(f32[8,128]{1,0:T(8,128)S(1)} %add.20), channel_id=1, source_target_pairs={{0,4},{2,6},{4,0},{6,2},{8,12},{10,14},{12,8},{14,10},{1,5},{3,7},... | collective-permute-start | bytes 12296 | tf_op jit(solution)/shard_map/ppermute | solution.py:27
  31.8 1.4 %collective-permute-start.9 = (f32[8,128]{1,0:T(8,128)S(1)}, f32[8,128]{1,0:T(8,128)S(1)}, u32[]{:S(2)}, u32[]{:S(2)}) collective-permute-start(f32[8,128]{1,0:T(8,128)S(1)} %add.20), channel_id=1, source_target_pairs={{0,2},{2,0},{4,6},{6,4},{8,10},{10,8},{12,14},{14,12},{1,3},{3,1},... | collective-permute-start | bytes 12296 | tf_op jit(solution)/shard_map/ppermute | solution.py:27
  33.3 1.0 %collective-permute-done.11 = f32[8,128]{1,0:T(8,128)S(1)} collective-permute-done((f32[8,128]{1,0:T(8,128)S(1)}, f32[8,128]{1,0:T(8,128)S(1)}, u32[]{:S(2)}, u32[]{:S(2)}) %collective-permute-start.11) | collective-permute-done | bytes 4128 | tf_op jit(solution)/shard_map/ppermute | solution.py:27
  34.3 0.7 %collective-permute-done.10 = f32[8,128]{1,0:T(8,128)S(1)} collective-permute-done((f32[8,128]{1,0:T(8,128)S(1)}, f32[8,128]{1,0:T(8,128)S(1)}, u32[]{:S(2)}, u32[]{:S(2)}) %collective-permute-start.10) | collective-permute-done | bytes 4128 | tf_op jit(solution)/shard_map/ppermute | solution.py:27
  35.0 0.5 %collective-permute-done.9 = f32[8,128]{1,0:T(8,128)S(1)} collective-permute-done((f32[8,128]{1,0:T(8,128)S(1)}, f32[8,128]{1,0:T(8,128)S(1)}, u32[]{:S(2)}, u32[]{:S(2)}) %collective-permute-start.9) | collective-permute-done | bytes 4128 | tf_op jit(solution)/shard_map/ppermute | solution.py:27
  35.4 2.6 %collective-permute-start.12 = (f32[8,128]{1,0:T(8,128)S(1)}, f32[8,128]{1,0:T(8,128)S(1)}, u32[]{:S(2)}, u32[]{:S(2)}) collective-permute-start(f32[8,128]{1,0:T(8,128)S(1)} %add_add_fusion), channel_id=1, source_target_pairs={{0,8},{2,10},{4,12},{6,14},{8,0},{10,2},{12,4},{14,6},{1,9},{3,11}... | collective-permute-start | bytes 12296 | tf_op jit(solution)/shard_map/ppermute | solution.py:27
  38.0 1.9 %collective-permute-done.12 = f32[8,128]{1,0:T(8,128)S(1)} collective-permute-done((f32[8,128]{1,0:T(8,128)S(1)}, f32[8,128]{1,0:T(8,128)S(1)}, u32[]{:S(2)}, u32[]{:S(2)}) %collective-permute-start.12) | collective-permute-done | bytes 4128 | tf_op jit(solution)/shard_map/ppermute | solution.py:27
  40.0 0.6 %add.24 = f32[8,128]{1,0:T(8,128)} add(f32[8,128]{1,0:T(8,128)S(1)} %add_add_fusion, f32[8,128]{1,0:T(8,128)S(1)} %collective-permute-done.12) | non-fusion elementwise | flops 1024 | bytes 12288 | tf_op jit(solution)/shard_map/add | solution.py:207
  (2 shorter events, 0.0 us)
Async XLA Ops:
  0.0 13.9 %collective-permute-start.4 = (bf16[7168,256]{1,0:T(8,128)(2,1)}, bf16[7168,256]{1,0:T(8,128)(2,1)}, u32[]{:S(2)}, u32[]{:S(2)}) collective-permute-start(bf16[7168,256]{1,0:T(8,128)(2,1)} %bitcast.8), channel_id=1, source_target_pairs={{0,1},{1,0},{2,3},{3,2},{4,5},{5,4},{6,7},{7,6},{8,9},{9,8},{10,11... | collective-permute-start | bytes 11010056 | tf_op jit(solution)/shard_map/ppermute | solution.py:27
  0.5 13.5 %collective-permute-start.3 = (bf16[2048,256]{1,0:T(8,128)(2,1)}, bf16[2048,256]{1,0:T(8,128)(2,1)S(1)}, u32[]{:S(2)}, u32[]{:S(2)}) collective-permute-start(bf16[2048,256]{1,0:T(8,128)(2,1)} %bitcast.11), channel_id=1, source_target_pairs={{0,1},{1,0},{2,3},{3,2},{4,5},{5,4},{6,7},{7,6},{8,9},{9,8},{10,11... | collective-permute-start | bytes 3145736 | tf_op jit(solution)/shard_map/ppermute | solution.py:27
  0.6 13.4 %copy-start = (s32[2]{0:T(128)}, s32[2]{0:T(128)S(1)}, u32[]{:S(2)}) copy-start(s32[2]{0:T(128)S(1)} %pad_add_fusion.place) | copy-start | bytes 28
  9.3 12.4 %collective-permute-start = (s16[112,512]{1,0:T(8,128)(2,1)S(1)}, s16[112,512]{1,0:T(8,128)(2,1)S(1)}, u32[]{:S(2)}, u32[]{:S(2)}) collective-permute-start(s16[112,512]{1,0:T(8,128)(2,1)S(1)} %get-tuple-element.16), channel_id=1, source_target_pairs={{0,2},{2,0},{4,6},{6,4},{8,10},{10,8},{12,14},{14,12},{1,3},{3,1},... | collective-permute-start | bytes 344072 | tf_op jit(solution)/shard_map/ppermute | solution.py:27
  12.4 9.4 %collective-permute-start.1 = (s16[112,512]{1,0:T(8,128)(2,1)S(1)}, s16[112,512]{1,0:T(8,128)(2,1)S(1)}, u32[]{:S(2)}, u32[]{:S(2)}) collective-permute-start(s16[112,512]{1,0:T(8,128)(2,1)S(1)} %get-tuple-element.17), channel_id=1, source_target_pairs={{0,4},{2,6},{4,0},{6,2},{8,12},{10,14},{12,8},{14,10},{1,5},{3,7},... | collective-permute-start | bytes 344072 | tf_op jit(solution)/shard_map/ppermute | solution.py:27
  13.9 7.8 %collective-permute-start.2 = (s16[112,512]{1,0:T(8,128)(2,1)S(1)}, s16[112,512]{1,0:T(8,128)(2,1)S(1)}, u32[]{:S(2)}, u32[]{:S(2)}) collective-permute-start(s16[112,512]{1,0:T(8,128)(2,1)S(1)} %get-tuple-element.18), channel_id=1, source_target_pairs={{0,6},{2,4},{4,2},{6,0},{8,14},{10,12},{12,10},{14,8},{1,7},{3,5},... | collective-permute-start | bytes 344072 | tf_op jit(solution)/shard_map/ppermute | solution.py:27
  18.2 5.5 %collective-permute-start.5 = (s16[112,512]{1,0:T(8,128)(2,1)S(1)}, s16[112,512]{1,0:T(8,128)(2,1)S(1)}, u32[]{:S(2)}, u32[]{:S(2)}) collective-permute-start(s16[112,512]{1,0:T(8,128)(2,1)S(1)} %get-tuple-element.22), channel_id=1, source_target_pairs={{0,2},{2,0},{4,6},{6,4},{8,10},{10,8},{12,14},{14,12},{1,3},{3,1},... | collective-permute-start | bytes 344072 | tf_op jit(solution)/shard_map/ppermute | solution.py:27
  20.1 5.2 %collective-permute-start.6 = (s16[112,512]{1,0:T(8,128)(2,1)S(1)}, s16[112,512]{1,0:T(8,128)(2,1)S(1)}, u32[]{:S(2)}, u32[]{:S(2)}) collective-permute-start(s16[112,512]{1,0:T(8,128)(2,1)S(1)} %get-tuple-element.23), channel_id=1, source_target_pairs={{0,4},{2,6},{4,0},{6,2},{8,12},{10,14},{12,8},{14,10},{1,5},{3,7},... | collective-permute-start | bytes 344072 | tf_op jit(solution)/shard_map/ppermute | solution.py:27
  21.7 5.7 %collective-permute-start.7 = (s16[112,512]{1,0:T(8,128)(2,1)S(1)}, s16[112,512]{1,0:T(8,128)(2,1)S(1)}, u32[]{:S(2)}, u32[]{:S(2)}) collective-permute-start(s16[112,512]{1,0:T(8,128)(2,1)S(1)} %get-tuple-element.24), channel_id=1, source_target_pairs={{0,6},{2,4},{4,2},{6,0},{8,14},{10,12},{12,10},{14,8},{1,7},{3,5},... | collective-permute-start | bytes 344072 | tf_op jit(solution)/shard_map/ppermute | solution.py:27
  28.5 1.2 %collective-permute-start.8 = (f32[8,128]{1,0:T(8,128)S(1)}, f32[8,128]{1,0:T(8,128)S(1)}, u32[]{:S(2)}, u32[]{:S(2)}) collective-permute-start(f32[8,128]{1,0:T(8,128)S(1)} %scores.1), channel_id=1, source_target_pairs={{0,1},{1,0},{2,3},{3,2},{4,5},{5,4},{6,7},{7,6},{8,9},{9,8},{10,11... | collective-permute-start | bytes 12296 | tf_op jit(solution)/shard_map/ppermute | solution.py:27
  29.8 4.5 %collective-permute-start.11 = (f32[8,128]{1,0:T(8,128)S(1)}, f32[8,128]{1,0:T(8,128)S(1)}, u32[]{:S(2)}, u32[]{:S(2)}) collective-permute-start(f32[8,128]{1,0:T(8,128)S(1)} %add.20), channel_id=1, source_target_pairs={{0,6},{2,4},{4,2},{6,0},{8,14},{10,12},{12,10},{14,8},{1,7},{3,5},... | collective-permute-start | bytes 12296 | tf_op jit(solution)/shard_map/ppermute | solution.py:27
  31.4 3.6 %collective-permute-start.10 = (f32[8,128]{1,0:T(8,128)S(1)}, f32[8,128]{1,0:T(8,128)S(1)}, u32[]{:S(2)}, u32[]{:S(2)}) collective-permute-start(f32[8,128]{1,0:T(8,128)S(1)} %add.20), channel_id=1, source_target_pairs={{0,4},{2,6},{4,0},{6,2},{8,12},{10,14},{12,8},{14,10},{1,5},{3,7},... | collective-permute-start | bytes 12296 | tf_op jit(solution)/shard_map/ppermute | solution.py:27
  31.8 3.6 %collective-permute-start.9 = (f32[8,128]{1,0:T(8,128)S(1)}, f32[8,128]{1,0:T(8,128)S(1)}, u32[]{:S(2)}, u32[]{:S(2)}) collective-permute-start(f32[8,128]{1,0:T(8,128)S(1)} %add.20), channel_id=1, source_target_pairs={{0,2},{2,0},{4,6},{6,4},{8,10},{10,8},{12,14},{14,12},{1,3},{3,1},... | collective-permute-start | bytes 12296 | tf_op jit(solution)/shard_map/ppermute | solution.py:27
  35.4 4.5 %collective-permute-start.12 = (f32[8,128]{1,0:T(8,128)S(1)}, f32[8,128]{1,0:T(8,128)S(1)}, u32[]{:S(2)}, u32[]{:S(2)}) collective-permute-start(f32[8,128]{1,0:T(8,128)S(1)} %add_add_fusion), channel_id=1, source_target_pairs={{0,8},{2,10},{4,12},{6,14},{8,0},{10,2},{12,4},{14,6},{1,9},{3,11}... | collective-permute-start | bytes 12296 | tf_op jit(solution)/shard_map/ppermute | solution.py:27

commit v4 on v1

v4 whole, which is shorter than its diff:
```python
import jax
import jax.numpy as jnp
from jax import lax
from jax.experimental import pallas as pl
from jax.experimental.pallas import tpu as pltpu
from jax.sharding import PartitionSpec as P

RANK = 32
QUARTERS = 4
LANES = 128
CODE_ROWS = 16
TOP = 32000.0
STEPS = 256.0
FLOOR = 2.0**-112
MIB = 2**20

IN_VMEM = pl.BlockSpec(memory_space=pltpu.VMEM)
IN_HBM = pl.BlockSpec(memory_space=pltpu.HBM)
IN_SMEM = pl.BlockSpec(memory_space=pltpu.SMEM)


def in_vmem(value):
    return pltpu.with_memory_space_constraint(value, pltpu.VMEM)


def in_hbm(value):
    return pltpu.with_memory_space_constraint(value, pltpu.HBM)


def from_partner(value, axis, mask):
    pairs = [(source, source ^ mask) for source in range(lax.axis_size(axis))]
    return lax.ppermute(value, axis, pairs)


def dot(rows, factor):
    return jnp.dot(rows, factor, preferred_element_type=jnp.float32)


def encode(part):
    peak = jnp.max(jnp.abs(part), axis=0, keepdims=True)
    code = jnp.ceil(jnp.log2(jnp.maximum(peak, FLOOR)) * STEPS) + 1.0
    fixed = jnp.round(part * (TOP * jnp.exp2(code * (-1.0 / STEPS))))
    code = jnp.broadcast_to(code, (CODE_ROWS, part.shape[1]))
    return fixed.astype(jnp.int32).astype(jnp.int16), code.astype(jnp.int32).astype(jnp.int16)


def decode(message, rows):
    fixed = message[:rows, :].astype(jnp.int32).astype(jnp.float32)
    code = message[rows:, :].astype(jnp.int32).astype(jnp.float32)[:1]
    return fixed * (jnp.exp2(code * (1.0 / STEPS)) * (1.0 / TOP))


def keep(part, total):
    rows = total.shape[1]
    for index in range(QUARTERS):
        total[index] = part[index * rows:(index + 1) * rows]


def share(total, quarter, own_ref, out_refs, first):
    rows = own_ref.shape[0]
    columns = slice(first, first + total.shape[2])
    own_ref[:, columns] = total[quarter]
    for mask in range(1, QUARTERS):
        fixed, code = encode(total[quarter ^ mask])
        out_refs[mask - 1][:rows, columns] = fixed
        out_refs[mask - 1][rows:, columns] = code


def act_own_kernel(acts, factor, total, rows_held, factor_held, sems):
    copies = (
        pltpu.make_async_copy(factor, factor_held, sems.at[0]),
        pltpu.make_async_copy(acts, rows_held, sems.at[1]),
    )
    for copy in copies:
        copy.start()
    for copy in copies:
        copy.wait()
    keep(dot(rows_held[...], factor_held[...]), total)


def grad_own_kernel(grads, factor, after, total):
    keep(dot(grads[...], factor[...]), total)


def other_kernel(*refs):
    *held, other_factor, mine, own, out1, out2, out3, total = refs
    quarter = lax.axis_index("layer") % QUARTERS
    outs = (out1, out2, out3)
    share(mine, quarter, own, outs, 0)
    first, part = 0, 0.0
    for rows_held in held:
        depth = rows_held.shape[1]
        part = part + dot(rows_held[...], other_factor[first:first + depth, :])
        first += depth
    keep(part, total)
    share(total, quarter, own, outs, total.shape[2])


def sum_kernel(own, in1, in2, in3, out):
    rows = own.shape[0]
    full = own[...]
    for message in (in1, in2, in3):
        full = full + decode(message[...], rows)
    out[...] = full


def score_kernel(lengths, acts, own, in1, in2, in3, out):
    quarter, position = lax.axis_index("layer") % QUARTERS, lax.axis_index("loop")
    rows, width = own.shape
    seq_part = lengths.shape[0] // QUARTERS
    pad_rows = rows // seq_part
    half = width // 2
    queries = half // RANK
    column = lax.broadcasted_iota(jnp.int32, (width, LANES), 0)
    lane = lax.broadcasted_iota(jnp.int32, (width, LANES), 1)
    holder = jnp.where(column < half, position, 1 - position)
    pick = (lane == (column % half) // RANK + holder * queries).astype(jnp.float32)
    offsets = lax.broadcasted_iota(jnp.int32, (pad_rows, width), 0)
    line = lax.broadcasted_iota(jnp.int32, out.shape, 0)
    full = own[...]
    for message in (in1, in2, in3):
        full = full + decode(message[...], rows)
    pair = acts[...] * full
    result = jnp.zeros(out.shape, jnp.float32)
    for seq in range(seq_part):
        live = offsets < lengths[quarter * seq_part + seq]
        sums = jnp.sum(
            jnp.where(live, pair[seq * pad_rows:(seq + 1) * pad_rows], 0.0), axis=0, keepdims=True
        )
        scores = jnp.dot(
            jnp.broadcast_to(sums, (8, width)), pick,
            precision=lax.Precision.HIGHEST, preferred_element_type=jnp.float32,
        )[:1]
        at = (position * QUARTERS + quarter) * seq_part + seq
        result = result + jnp.where(line == at, scores, 0.0)
    out[...] = result


def on_device(acts, grads, act_factors, grad_factors, lengths):
    loop_count = lax.axis_size("loop")
    layer_count = lax.axis_size("layer")
    acts, grads, act_factors, grad_factors = acts[0], grads[0], act_factors[0], grad_factors[0]
    seq_dev = lengths.shape[0]
    tok_rows, width = acts.shape[0], act_factors.shape[1]
    rows = tok_rows // QUARTERS
    queries = width * loop_count // RANK

    own_shape = pltpu.VMEM((rows, 2 * width), jnp.float32)
    out_shape = pltpu.VMEM((rows + CODE_ROWS, 2 * width), jnp.int16)
    total_shape = pltpu.VMEM((QUARTERS, rows, width), jnp.float32)

    def cost(depth, mib):
        return pl.CostEstimate(
            flops=2 * tok_rows * width * depth, bytes_accessed=mib * MIB, transcendentals=0
        )

    def limit(mib):
        return pltpu.CompilerParams(vmem_limit_bytes=mib * MIB)

    def other_columns(name, held, other_factor, mine, mib):
        own, *outs = pl.pallas_call(
            other_kernel,
            name=name,
            out_shape=(own_shape, out_shape, out_shape, out_shape),
            in_specs=[IN_VMEM] * (len(held) + 2),
            out_specs=(IN_VMEM,) * 4,
            scratch_shapes=[total_shape],
            compiler_params=limit(8),
            cost_estimate=cost(other_factor.shape[0], mib),
        )(*map(in_vmem, held), in_vmem(other_factor), in_vmem(mine))
        return own, [from_partner(outs[mask - 1], "layer", mask) for mask in range(1, QUARTERS)]

    other_act = from_partner(act_factors, "loop", 1)
    act_mine, act_rows = pl.pallas_call(
        act_own_kernel,
        name="act_own_columns",
        out_shape=(total_shape, pltpu.VMEM(acts.shape, acts.dtype)),
        in_specs=[IN_HBM] * 2,
        out_specs=(IN_VMEM,) * 2,
        scratch_shapes=[
            pltpu.VMEM(act_factors.shape, act_factors.dtype),
            pltpu.SemaphoreType.DMA((2,)),
        ],
        compiler_params=limit(8),
        cost_estimate=cost(acts.shape[1], 20),
    )(in_hbm(acts), in_hbm(act_factors))
    later_factors, other_act, act_mine = lax.optimization_barrier((grad_factors, other_act, act_mine))
    other_grad = from_partner(later_factors, "loop", 1)
    act_own, act_in = other_columns("act_other_columns", [act_rows], other_act, act_mine, 20)

    grad_mine = pl.pallas_call(
        grad_own_kernel,
        name="grad_own_columns",
        out_shape=total_shape,
        in_specs=[IN_VMEM] * 3,
        out_specs=IN_VMEM,
        compiler_params=limit(8),
        cost_estimate=cost(grads.shape[1], 10),
    )(in_vmem(grads), in_vmem(grad_factors), in_vmem(act_own))
    grad_own, grad_in = other_columns("grad_other_columns", [grads], other_grad, grad_mine, 10)

    act_full = pl.pallas_call(
        sum_kernel,
        name="act_sum",
        out_shape=own_shape,
        in_specs=[IN_VMEM] * 4,
        out_specs=IN_VMEM,
        compiler_params=limit(8),
    )(in_vmem(act_own), *map(in_vmem, act_in))
    total = pl.pallas_call(
        score_kernel,
        name="scores",
        out_shape=pltpu.VMEM((seq_dev * loop_count, LANES), jnp.float32),
        in_specs=[IN_SMEM] + [IN_VMEM] * 5,
        out_specs=IN_VMEM,
        compiler_params=limit(8),
    )(lengths, in_vmem(act_full), in_vmem(grad_own), *map(in_vmem, grad_in))

    total = total + from_partner(total, "loop", 1)
    gathered = [from_partner(total, "layer", mask) for mask in range(1, QUARTERS)]
    total = total + gathered[0] + gathered[1] + gathered[2]
    mask = QUARTERS
    while mask < layer_count:
        total = total + from_partner(total, "layer", mask)
        mask *= 2
    return total[:, :queries]


def solution(mesh):
    in_specs = (
        P("layer", ("groups", "loop"), None),
        P("layer", ("groups", "loop"), None),
        P("layer", None, "loop"),
        P("layer", None, "loop"),
        P(("groups", "loop")),
    )
    out_specs = P("groups", None)
    return jax.shard_map(
        on_device, mesh=mesh, in_specs=in_specs, out_specs=out_specs, check_vma=False
    )
```

time: 52.1 us -> 36.3 us (0.70)
  matrix products: 15.5 us -> 0 us
  Pallas kernels: 0 us -> 7.39 us
  other arithmetic: 3.87 us -> 0.6 us
  waiting for transfers between devices: 13.2 us -> 11 us
  local copies, waits for them, and re-layouts: 4.23 us -> 2.05 us
    dot_general x4 -> x0, matrix products: 15.5 us -> none  [project(): return jnp.dot(rows, factor, preferred_element_type=jnp.float32)]
    pallas_call x0 -> x6, Pallas kernels: none -> 7.39 us  [the longest x1 2.52 us: on_device(): pl.pallas_call(act_own_kernel, name='act_own_columns', out_shape=(total_s...]
    ppermute x13, waiting for transfers between devices: 13.2 us -> 11 us  [from_partner(): return lax.ppermute(value, axis, pairs)]
    concatenate x2 -> x0, local copies, waits for them, and re-layouts: 1.66 us -> none  [the longest x1 1.39 us: on_device(): jnp.concatenate([project(acts[0], other_act), project(grads[0], other_gra...]
    unnamed x4 -> x6, local copies, waits for them, and re-layouts: 0.89 us -> 2.05 us
    add x2 -> x1, other arithmetic: 1.14 us -> 0.01 us  [on_device(): total = total + from_partner(total, 'loop', 1)]
    concatenate x3 -> x0, other arithmetic: 1.06 us -> none  [the longest x1 0.93 us: on_device(): jnp.concatenate([project(acts[0], other_act), project(grads[0], other_gra...]
    squeeze x2 -> x0, local copies, waits for them, and re-layouts: 0.89 us -> none  [sum_over_quarters(): out = lax.dynamic_index_in_dim(parts, quarter ^ mask, 0, keepdims=False)]
  transfers between devices with their start and end apart: 13 -> 13, of which waited for: 8 -> 8; matrix products, arithmetic and copies ran while one was open for 41% -> 0% of each run, Pallas kernels for 0% -> 18%
where the time goes in v4:
time: 36.3 us; the launch traced here: 36.1 us
  starting transfers between devices  15 us (41%)
  waiting for transfers between devices  11 us (30%)
  Pallas kernels  7.39 us (20%)
  local copies, waits for them, and re-layouts  2.05 us (6%)
  other arithmetic  0.6 us (2%)
    ppermute x13, starting transfers between devices, from_partner(): return lax.ppermute(value, axis, pairs)  15 us
    ppermute x13, waiting for transfers between devices, from_partner(): return lax.ppermute(value, axis, pairs)  11 us
    pallas_call x1, Pallas kernels, on_device(): pl.pallas_call(act_own_kernel, name='act_own_columns', out_shape=(total_s...  2.52 us
    pallas_call x2, Pallas kernels, other_columns(): pl.pallas_call(other_kernel, name=name, out_shape=(own_shape, out_shape,...  2.29 us
    unnamed x6, local copies, waits for them, and re-layouts  2.05 us
    pallas_call x1, Pallas kernels, on_device(): pl.pallas_call(grad_own_kernel, name='grad_own_columns', out_shape=total_...  1.58 us
    pallas_call x1, Pallas kernels, on_device(): pl.pallas_call(score_kernel, name='scores', out_shape=pltpu.VMEM((seq_dev...  0.91 us
  transfers between devices with their start and end apart: 13, of which 8 were waited for; matrix products, arithmetic and copies ran while one was open for 0% of the time, Pallas kernels for 18%

profile of v4, /device:TPU:0, one launch (start us, length us, event | category | flops | bytes accessed | tf_op | source)
XLA Modules:
  0.0 36.1 jit_solution(17557554448247980769)
XLA Ops:
  0.0 0.0 copy-start
  0.0 0.5 %collective-permute-start = (bf16[2048,256]{1,0:T(8,128)(2,1)}, bf16[2048,256]{1,0:T(8,128)(2,1)S(1)}, u32[]{:S(2)}, u32[]{:S(2)}) collective-permute-start(bf16[2048,256]{1,0:T(8,128)(2,1)} %bitcast.10), channel_id=1, source_target_pairs={{0,1},{1,0},{2,3},{3,2},{4,5},{5,4},{6,7},{7,6},{8,9},{9,8},{10,11... | collective-permute-start | bytes 3145736 | tf_op jit(solution)/shard_map/ppermute | solution.py:32
  0.5 2.5 %act_own_columns.1 = (f32[4,96,256]{2,1,0:T(8,128)S(1)}, bf16[384,2048]{1,0:T(8,128)(2,1)S(1)}) custom-call(bf16[384,2048]{1,0:T(8,128)(2,1)} %bitcast.9, bf16[2048,256]{1,0:T(8,128)(2,1)} %bitcast.11), custom_call_target="tpu_custom_call" | custom-call | flops 402653184 | bytes 20971520 | tf_op jit(solution)/shard_map/act_own_columns/pallas_call | solution.py:174
  3.0 0.0 collective-permute-done.refs_1_
  3.0 0.3 collective-permute-start.4
  3.3 0.6 %act_other_columns.1 = (f32[96,512]{1,0:T(8,128)S(1)}, s16[112,512]{1,0:T(8,128)(2,1)S(1)}, s16[112,512]{1,0:T(8,128)(2,1)S(1)}, s16[112,512]{1,0:T(8,128)(2,1)S(1)}) custom-call(bf16[384,2048]{1,0:T(8,128)(2,1)S(1)} %get-tuple-element.18.refs_0_, bf16[2048,256]{1,0:T(8,128)(2,1)S(1)} %collective-permute-done.refs_1_, ...), custom_call_target="tpu_custom_call" | custom-call | flops 402653184 | bytes 20971520 | tf_op jit(solution)/shard_map/act_other_columns/pallas_call | solution.py:161
  4.0 2.9 %collective-permute-start.1 = (s16[112,512]{1,0:T(8,128)(2,1)S(1)}, s16[112,512]{1,0:T(8,128)(2,1)S(1)}, u32[]{:S(2)}, u32[]{:S(2)}) collective-permute-start(s16[112,512]{1,0:T(8,128)(2,1)S(1)} %get-tuple-element.23), channel_id=1, source_target_pairs={{0,2},{2,0},{4,6},{6,4},{8,10},{10,8},{12,14},{14,12},{1,3},{3,1},... | collective-permute-start | bytes 344072 | tf_op jit(solution)/shard_map/ppermute | solution.py:32
  6.9 1.6 %collective-permute-start.2 = (s16[112,512]{1,0:T(8,128)(2,1)S(1)}, s16[112,512]{1,0:T(8,128)(2,1)S(1)}, u32[]{:S(2)}, u32[]{:S(2)}) collective-permute-start(s16[112,512]{1,0:T(8,128)(2,1)S(1)} %get-tuple-element.24), channel_id=1, source_target_pairs={{0,4},{2,6},{4,0},{6,2},{8,12},{10,14},{12,8},{14,10},{1,5},{3,7},... | collective-permute-start | bytes 344072 | tf_op jit(solution)/shard_map/ppermute | solution.py:32
  8.5 0.0 collective-permute-start.3
  8.5 0.0 copy-done
  8.5 0.0 copy-start.1
  8.5 2.0 %copy-done.1 = bf16[1,7168,256]{2,1,0:T(8,128)(2,1)S(1)} copy-done((bf16[1,7168,256]{2,1,0:T(8,128)(2,1)S(1)}, bf16[1,7168,256]{2,1,0:T(8,128)(2,1)}, u32[]{:S(2)}) %copy-start.1) | copy-done | bytes 3670040
  10.5 1.6 %grad_own_columns.1.refs_2_ = f32[4,96,256]{2,1,0:T(8,128)S(1)} custom-call(bf16[384,7168]{1,0:T(8,128)(2,1)S(1)} %bitcast.5, bf16[7168,256]{1,0:T(8,128)(2,1)S(1)} %bitcast.8, f32[96,512]{1,0:T(8,128)S(1)} %get-tuple-element.22.own.after), custom_call_target="tpu_custom_call" | custom-call | flops 1409286144 | bytes 10485760 | tf_op jit(solution)/shard_map/grad_own_columns/pallas_call | solution.py:191
  12.1 0.0 copy-start.2
  12.1 0.0 collective-permute-done.4.refs_1_
  12.1 1.7 %grad_other_columns.1 = (f32[96,512]{1,0:T(8,128)S(1)}, s16[112,512]{1,0:T(8,128)(2,1)S(1)}, s16[112,512]{1,0:T(8,128)(2,1)S(1)}, s16[112,512]{1,0:T(8,128)(2,1)S(1)}) custom-call(bf16[384,7168]{1,0:T(8,128)(2,1)S(1)} %bitcast.6, bf16[7168,256]{1,0:T(8,128)(2,1)S(1)} %collective-permute-done.4.refs_1_, f32[4,96,256]{2,1,0:T(8,128)S(1)} %grad_own_columns.1.refs_2_), custom_call_target="tpu_custom_call" | custom-call | flops 1409286144 | bytes 10485760 | tf_op jit(solution)/shard_map/grad_other_columns/pallas_call | solution.py:161
  13.8 2.0 %collective-permute-start.5 = (s16[112,512]{1,0:T(8,128)(2,1)S(1)}, s16[112,512]{1,0:T(8,128)(2,1)S(1)}, u32[]{:S(2)}, u32[]{:S(2)}) collective-permute-start(s16[112,512]{1,0:T(8,128)(2,1)S(1)} %get-tuple-element.28), channel_id=1, source_target_pairs={{0,2},{2,0},{4,6},{6,4},{8,10},{10,8},{12,14},{14,12},{1,3},{3,1},... | collective-permute-start | bytes 344072 | tf_op jit(solution)/shard_map/ppermute | solution.py:32
  15.8 1.6 %collective-permute-start.6 = (s16[112,512]{1,0:T(8,128)(2,1)S(1)}, s16[112,512]{1,0:T(8,128)(2,1)S(1)}, u32[]{:S(2)}, u32[]{:S(2)}) collective-permute-start(s16[112,512]{1,0:T(8,128)(2,1)S(1)} %get-tuple-element.29), channel_id=1, source_target_pairs={{0,4},{2,6},{4,0},{6,2},{8,12},{10,14},{12,8},{14,10},{1,5},{3,7},... | collective-permute-start | bytes 344072 | tf_op jit(solution)/shard_map/ppermute | solution.py:32
  17.4 0.0 collective-permute-done.1.in1
  17.4 0.0 collective-permute-start.7
  17.4 0.0 collective-permute-done.2.in2
  17.4 0.0 collective-permute-done.3.in3
  17.4 0.1 act_sum.1.acts
  17.5 1.6 %collective-permute-done.5.in1 = s16[112,512]{1,0:T(8,128)(2,1)S(1)} collective-permute-done((s16[112,512]{1,0:T(8,128)(2,1)S(1)}, s16[112,512]{1,0:T(8,128)(2,1)S(1)}, u32[]{:S(2)}, u32[]{:S(2)}) %collective-permute-start.5) | collective-permute-done | bytes 114720 | tf_op jit(solution)/shard_map/ppermute | solution.py:32
  19.0 2.1 %collective-permute-done.6.in2 = s16[112,512]{1,0:T(8,128)(2,1)S(1)} collective-permute-done((s16[112,512]{1,0:T(8,128)(2,1)S(1)}, s16[112,512]{1,0:T(8,128)(2,1)S(1)}, u32[]{:S(2)}, u32[]{:S(2)}) %collective-permute-start.6) | collective-permute-done | bytes 114720 | tf_op jit(solution)/shard_map/ppermute | solution.py:32
  21.1 1.9 %collective-permute-done.7.in3 = s16[112,512]{1,0:T(8,128)(2,1)S(1)} collective-permute-done((s16[112,512]{1,0:T(8,128)(2,1)S(1)}, s16[112,512]{1,0:T(8,128)(2,1)S(1)}, u32[]{:S(2)}, u32[]{:S(2)}) %collective-permute-start.7) | collective-permute-done | bytes 114720 | tf_op jit(solution)/shard_map/ppermute | solution.py:32
  23.0 0.0 copy-done.2
  23.1 0.9 %scores.1 = f32[8,128]{1,0:T(8,128)S(1)} custom-call(s32[4]{0:T(128)S(1)} %copy-done.2, f32[96,512]{1,0:T(8,128)S(1)} %act_sum.1.acts, f32[96,512]{1,0:T(8,128)S(1)} %get-tuple-element.27.own, s16[112,512]{1,0:T(8,128)(2,1)S(1)} %collective-permute-done.5.in1, s16[112,512]{1,0:T(8,128)(2,1)S(1)} %collective-permute-done.6.in2, ...), custom_call_target="tpu_custom_call" | custom-call | tf_op jit(solution)/shard_map/scores/pallas_call | solution.py:210
  24.0 0.1 collective-permute-start.8
  24.0 1.2 %collective-permute-done.8 = f32[8,128]{1,0:T(8,128)S(1)} collective-permute-done((f32[8,128]{1,0:T(8,128)S(1)}, f32[8,128]{1,0:T(8,128)S(1)}, u32[]{:S(2)}, u32[]{:S(2)}) %collective-permute-start.8) | collective-permute-done | bytes 4128 | tf_op jit(solution)/shard_map/ppermute | solution.py:32
  25.2 1.8 %collective-permute-start.11 = (f32[8,128]{1,0:T(8,128)S(1)}, f32[8,128]{1,0:T(8,128)S(1)}, u32[]{:S(2)}, u32[]{:S(2)}) collective-permute-start(f32[8,128]{1,0:T(8,128)S(1)} %add.15), channel_id=1, source_target_pairs={{0,6},{2,4},{4,2},{6,0},{8,14},{10,12},{12,10},{14,8},{1,7},{3,5},... | collective-permute-start | bytes 12296 | tf_op jit(solution)/shard_map/ppermute | solution.py:32
  26.9 0.5 %collective-permute-start.10 = (f32[8,128]{1,0:T(8,128)S(1)}, f32[8,128]{1,0:T(8,128)S(1)}, u32[]{:S(2)}, u32[]{:S(2)}) collective-permute-start(f32[8,128]{1,0:T(8,128)S(1)} %add.15), channel_id=1, source_target_pairs={{0,4},{2,6},{4,0},{6,2},{8,12},{10,14},{12,8},{14,10},{1,5},{3,7},... | collective-permute-start | bytes 12296 | tf_op jit(solution)/shard_map/ppermute | solution.py:32
  27.4 1.3 %collective-permute-start.9 = (f32[8,128]{1,0:T(8,128)S(1)}, f32[8,128]{1,0:T(8,128)S(1)}, u32[]{:S(2)}, u32[]{:S(2)}) collective-permute-start(f32[8,128]{1,0:T(8,128)S(1)} %add.15), channel_id=1, source_target_pairs={{0,2},{2,0},{4,6},{6,4},{8,10},{10,8},{12,14},{14,12},{1,3},{3,1},... | collective-permute-start | bytes 12296 | tf_op jit(solution)/shard_map/ppermute | solution.py:32
  28.7 1.0 %collective-permute-done.11 = f32[8,128]{1,0:T(8,128)S(1)} collective-permute-done((f32[8,128]{1,0:T(8,128)S(1)}, f32[8,128]{1,0:T(8,128)S(1)}, u32[]{:S(2)}, u32[]{:S(2)}) %collective-permute-start.11) | collective-permute-done | bytes 4128 | tf_op jit(solution)/shard_map/ppermute | solution.py:32
  29.7 0.9 %collective-permute-done.10 = f32[8,128]{1,0:T(8,128)S(1)} collective-permute-done((f32[8,128]{1,0:T(8,128)S(1)}, f32[8,128]{1,0:T(8,128)S(1)}, u32[]{:S(2)}, u32[]{:S(2)}) %collective-permute-start.10) | collective-permute-done | bytes 4128 | tf_op jit(solution)/shard_map/ppermute | solution.py:32
  30.6 0.5 %collective-permute-done.9 = f32[8,128]{1,0:T(8,128)S(1)} collective-permute-done((f32[8,128]{1,0:T(8,128)S(1)}, f32[8,128]{1,0:T(8,128)S(1)}, u32[]{:S(2)}, u32[]{:S(2)}) %collective-permute-start.9) | collective-permute-done | bytes 4128 | tf_op jit(solution)/shard_map/ppermute | solution.py:32
  31.0 2.6 %collective-permute-start.12 = (f32[8,128]{1,0:T(8,128)S(1)}, f32[8,128]{1,0:T(8,128)S(1)}, u32[]{:S(2)}, u32[]{:S(2)}) collective-permute-start(f32[8,128]{1,0:T(8,128)S(1)} %add_add_fusion), channel_id=1, source_target_pairs={{0,8},{2,10},{4,12},{6,14},{8,0},{10,2},{12,4},{14,6},{1,9},{3,11}... | collective-permute-start | bytes 12296 | tf_op jit(solution)/shard_map/ppermute | solution.py:32
  33.6 1.9 %collective-permute-done.12 = f32[8,128]{1,0:T(8,128)S(1)} collective-permute-done((f32[8,128]{1,0:T(8,128)S(1)}, f32[8,128]{1,0:T(8,128)S(1)}, u32[]{:S(2)}, u32[]{:S(2)}) %collective-permute-start.12) | collective-permute-done | bytes 4128 | tf_op jit(solution)/shard_map/ppermute | solution.py:32
  35.5 0.6 %add.19 = f32[8,128]{1,0:T(8,128)} add(f32[8,128]{1,0:T(8,128)S(1)} %add_add_fusion, f32[8,128]{1,0:T(8,128)S(1)} %collective-permute-done.12) | non-fusion elementwise | flops 1024 | bytes 12288 | tf_op jit(solution)/shard_map/add | solution.py:224
  (2 shorter events, 0.0 us)
Async XLA Ops:
  0.0 8.5 %copy-start = (bf16[1,384,7168]{2,1,0:T(8,128)(2,1)S(1)}, bf16[1,384,7168]{2,1,0:T(8,128)(2,1)}, u32[]{:S(2)}) copy-start(bf16[1,384,7168]{2,1,0:T(8,128)(2,1)} %param.6) | copy-start | bytes 16515076
  0.0 3.0 %collective-permute-start = (bf16[2048,256]{1,0:T(8,128)(2,1)}, bf16[2048,256]{1,0:T(8,128)(2,1)S(1)}, u32[]{:S(2)}, u32[]{:S(2)}) collective-permute-start(bf16[2048,256]{1,0:T(8,128)(2,1)} %bitcast.10), channel_id=1, source_target_pairs={{0,1},{1,0},{2,3},{3,2},{4,5},{5,4},{6,7},{7,6},{8,9},{9,8},{10,11... | collective-permute-start | bytes 3145736 | tf_op jit(solution)/shard_map/ppermute | solution.py:32
  3.0 9.1 %collective-permute-start.4 = (bf16[7168,256]{1,0:T(8,128)(2,1)}, bf16[7168,256]{1,0:T(8,128)(2,1)S(1)}, u32[]{:S(2)}, u32[]{:S(2)}) collective-permute-start(bf16[7168,256]{1,0:T(8,128)(2,1)} %bitcast.7), channel_id=1, source_target_pairs={{0,1},{1,0},{2,3},{3,2},{4,5},{5,4},{6,7},{7,6},{8,9},{9,8},{10,11... | collective-permute-start | bytes 11010056 | tf_op jit(solution)/shard_map/ppermute | solution.py:32
  4.0 13.4 %collective-permute-start.1 = (s16[112,512]{1,0:T(8,128)(2,1)S(1)}, s16[112,512]{1,0:T(8,128)(2,1)S(1)}, u32[]{:S(2)}, u32[]{:S(2)}) collective-permute-start(s16[112,512]{1,0:T(8,128)(2,1)S(1)} %get-tuple-element.23), channel_id=1, source_target_pairs={{0,2},{2,0},{4,6},{6,4},{8,10},{10,8},{12,14},{14,12},{1,3},{3,1},... | collective-permute-start | bytes 344072 | tf_op jit(solution)/shard_map/ppermute | solution.py:32
  6.9 10.5 %collective-permute-start.2 = (s16[112,512]{1,0:T(8,128)(2,1)S(1)}, s16[112,512]{1,0:T(8,128)(2,1)S(1)}, u32[]{:S(2)}, u32[]{:S(2)}) collective-permute-start(s16[112,512]{1,0:T(8,128)(2,1)S(1)} %get-tuple-element.24), channel_id=1, source_target_pairs={{0,4},{2,6},{4,0},{6,2},{8,12},{10,14},{12,8},{14,10},{1,5},{3,7},... | collective-permute-start | bytes 344072 | tf_op jit(solution)/shard_map/ppermute | solution.py:32
  8.5 8.9 %collective-permute-start.3 = (s16[112,512]{1,0:T(8,128)(2,1)S(1)}, s16[112,512]{1,0:T(8,128)(2,1)S(1)}, u32[]{:S(2)}, u32[]{:S(2)}) collective-permute-start(s16[112,512]{1,0:T(8,128)(2,1)S(1)} %get-tuple-element.25), channel_id=1, source_target_pairs={{0,6},{2,4},{4,2},{6,0},{8,14},{10,12},{12,10},{14,8},{1,7},{3,5},... | collective-permute-start | bytes 344072 | tf_op jit(solution)/shard_map/ppermute | solution.py:32
  8.5 2.0 %copy-start.1 = (bf16[1,7168,256]{2,1,0:T(8,128)(2,1)S(1)}, bf16[1,7168,256]{2,1,0:T(8,128)(2,1)}, u32[]{:S(2)}) copy-start(bf16[1,7168,256]{2,1,0:T(8,128)(2,1)} %param.8) | copy-start | bytes 11010052
  12.1 10.9 %copy-start.2 = (s32[4]{0:T(128)S(1)}, s32[4]{0:T(128)}, u32[]{:S(2)}) copy-start(s32[4]{0:T(128)} %lengths.1) | copy-start | bytes 52
  13.8 5.2 %collective-permute-start.5 = (s16[112,512]{1,0:T(8,128)(2,1)S(1)}, s16[112,512]{1,0:T(8,128)(2,1)S(1)}, u32[]{:S(2)}, u32[]{:S(2)}) collective-permute-start(s16[112,512]{1,0:T(8,128)(2,1)S(1)} %get-tuple-element.28), channel_id=1, source_target_pairs={{0,2},{2,0},{4,6},{6,4},{8,10},{10,8},{12,14},{14,12},{1,3},{3,1},... | collective-permute-start | bytes 344072 | tf_op jit(solution)/shard_map/ppermute | solution.py:32
  15.8 5.3 %collective-permute-start.6 = (s16[112,512]{1,0:T(8,128)(2,1)S(1)}, s16[112,512]{1,0:T(8,128)(2,1)S(1)}, u32[]{:S(2)}, u32[]{:S(2)}) collective-permute-start(s16[112,512]{1,0:T(8,128)(2,1)S(1)} %get-tuple-element.29), channel_id=1, source_target_pairs={{0,4},{2,6},{4,0},{6,2},{8,12},{10,14},{12,8},{14,10},{1,5},{3,7},... | collective-permute-start | bytes 344072 | tf_op jit(solution)/shard_map/ppermute | solution.py:32
  17.4 5.7 %collective-permute-start.7 = (s16[112,512]{1,0:T(8,128)(2,1)S(1)}, s16[112,512]{1,0:T(8,128)(2,1)S(1)}, u32[]{:S(2)}, u32[]{:S(2)}) collective-permute-start(s16[112,512]{1,0:T(8,128)(2,1)S(1)} %get-tuple-element.30), channel_id=1, source_target_pairs={{0,6},{2,4},{4,2},{6,0},{8,14},{10,12},{12,10},{14,8},{1,7},{3,5},... | collective-permute-start | bytes 344072 | tf_op jit(solution)/shard_map/ppermute | solution.py:32
  24.0 1.2 %collective-permute-start.8 = (f32[8,128]{1,0:T(8,128)S(1)}, f32[8,128]{1,0:T(8,128)S(1)}, u32[]{:S(2)}, u32[]{:S(2)}) collective-permute-start(f32[8,128]{1,0:T(8,128)S(1)} %scores.1), channel_id=1, source_target_pairs={{0,1},{1,0},{2,3},{3,2},{4,5},{5,4},{6,7},{7,6},{8,9},{9,8},{10,11... | collective-permute-start | bytes 12296 | tf_op jit(solution)/shard_map/ppermute | solution.py:32
  25.2 4.5 %collective-permute-start.11 = (f32[8,128]{1,0:T(8,128)S(1)}, f32[8,128]{1,0:T(8,128)S(1)}, u32[]{:S(2)}, u32[]{:S(2)}) collective-permute-start(f32[8,128]{1,0:T(8,128)S(1)} %add.15), channel_id=1, source_target_pairs={{0,6},{2,4},{4,2},{6,0},{8,14},{10,12},{12,10},{14,8},{1,7},{3,5},... | collective-permute-start | bytes 12296 | tf_op jit(solution)/shard_map/ppermute | solution.py:32
  26.9 3.6 %collective-permute-start.10 = (f32[8,128]{1,0:T(8,128)S(1)}, f32[8,128]{1,0:T(8,128)S(1)}, u32[]{:S(2)}, u32[]{:S(2)}) collective-permute-start(f32[8,128]{1,0:T(8,128)S(1)} %add.15), channel_id=1, source_target_pairs={{0,4},{2,6},{4,0},{6,2},{8,12},{10,14},{12,8},{14,10},{1,5},{3,7},... | collective-permute-start | bytes 12296 | tf_op jit(solution)/shard_map/ppermute | solution.py:32
  27.4 3.6 %collective-permute-start.9 = (f32[8,128]{1,0:T(8,128)S(1)}, f32[8,128]{1,0:T(8,128)S(1)}, u32[]{:S(2)}, u32[]{:S(2)}) collective-permute-start(f32[8,128]{1,0:T(8,128)S(1)} %add.15), channel_id=1, source_target_pairs={{0,2},{2,0},{4,6},{6,4},{8,10},{10,8},{12,14},{14,12},{1,3},{3,1},... | collective-permute-start | bytes 12296 | tf_op jit(solution)/shard_map/ppermute | solution.py:32
  31.0 4.5 %collective-permute-start.12 = (f32[8,128]{1,0:T(8,128)S(1)}, f32[8,128]{1,0:T(8,128)S(1)}, u32[]{:S(2)}, u32[]{:S(2)}) collective-permute-start(f32[8,128]{1,0:T(8,128)S(1)} %add_add_fusion), channel_id=1, source_target_pairs={{0,8},{2,10},{4,12},{6,14},{8,0},{10,2},{12,4},{14,6},{1,9},{3,11}... | collective-permute-start | bytes 12296 | tf_op jit(solution)/shard_map/ppermute | solution.py:32

commit v5 on v4

v5 whole, which is shorter than its diff:
```python
import jax
import jax.numpy as jnp
from jax import lax
from jax.experimental import pallas as pl
from jax.experimental.pallas import tpu as pltpu
from jax.sharding import PartitionSpec as P

RANK = 32
QUARTERS = 4
LANES = 128
CODE_ROWS = 16
TOP = 32000.0
STEPS = 256.0
FLOOR = 2.0**-112
MIB = 2**20
ACT_OWN_MIB = 50

IN_VMEM = pl.BlockSpec(memory_space=pltpu.VMEM)
IN_HBM = pl.BlockSpec(memory_space=pltpu.HBM)
IN_SMEM = pl.BlockSpec(memory_space=pltpu.SMEM)


def in_vmem(value):
    return pltpu.with_memory_space_constraint(value, pltpu.VMEM)


def in_hbm(value):
    return pltpu.with_memory_space_constraint(value, pltpu.HBM)


def from_partner(value, axis, mask):
    pairs = [(source, source ^ mask) for source in range(lax.axis_size(axis))]
    return lax.ppermute(value, axis, pairs)


def dot(rows, factor):
    return jnp.dot(rows, factor, preferred_element_type=jnp.float32)


def encode(part):
    peak = jnp.max(jnp.abs(part), axis=0, keepdims=True)
    code = jnp.ceil(jnp.log2(jnp.maximum(peak, FLOOR)) * STEPS) + 1.0
    fixed = jnp.round(part * (TOP * jnp.exp2(code * (-1.0 / STEPS))))
    code = jnp.broadcast_to(code, (CODE_ROWS, part.shape[1]))
    return fixed.astype(jnp.int32).astype(jnp.int16), code.astype(jnp.int32).astype(jnp.int16)


def decode(message, rows):
    fixed = message[:rows, :].astype(jnp.int32).astype(jnp.float32)
    code = message[rows:, :].astype(jnp.int32).astype(jnp.float32)[:1]
    return fixed * (jnp.exp2(code * (1.0 / STEPS)) * (1.0 / TOP))


def keep(part, total):
    rows = total.shape[1]
    for index in range(QUARTERS):
        total[index] = part[index * rows:(index + 1) * rows]


def share(total, quarter, own_ref, out_refs, first):
    rows = own_ref.shape[0]
    columns = slice(first, first + total.shape[2])
    own_ref[:, columns] = total[quarter]
    for mask in range(1, QUARTERS):
        fixed, code = encode(total[quarter ^ mask])
        out_refs[mask - 1][:rows, columns] = fixed
        out_refs[mask - 1][rows:, columns] = code


def act_own_kernel(acts, factor, grad_factor, total, rows_held, grad_factor_held, factor_held, sems):
    copies = (
        pltpu.make_async_copy(factor, factor_held, sems.at[0]),
        pltpu.make_async_copy(acts, rows_held, sems.at[1]),
        pltpu.make_async_copy(grad_factor, grad_factor_held, sems.at[2]),
    )
    for copy in copies:
        copy.start()
    copies[0].wait()
    copies[1].wait()
    keep(dot(rows_held[...], factor_held[...]), total)
    copies[2].wait()


def grad_own_kernel(grads, factor, total):
    keep(dot(grads[...], factor[...]), total)


def act_other_kernel(act_held, other_factor, act_total, grad_total, own, out1, out2, out3, total):
    quarter = lax.axis_index("layer") % QUARTERS
    outs = (out1, out2, out3)
    width = total.shape[2]
    keep(dot(act_held[...], other_factor[...]), total)
    for index, part in enumerate((act_total, grad_total, total)):
        share(part, quarter, own, outs, index * width)


def grad_other_kernel(grads, other_factor, own, out1, out2, out3, total):
    quarter = lax.axis_index("layer") % QUARTERS
    keep(dot(grads[...], other_factor[...]), total)
    share(total, quarter, own, (out1, out2, out3), 0)


def received(own, messages):
    full = own[...]
    for message in messages:
        full = full + decode(message[...], own.shape[0])
    return full


def score(pair, lengths, holder, out):
    quarter, position = lax.axis_index("layer") % QUARTERS, lax.axis_index("loop")
    rows, width = pair.shape
    seq_part = lengths.shape[0] // QUARTERS
    pad_rows = rows // seq_part
    column = lax.broadcasted_iota(jnp.int32, (width, LANES), 0)
    lane = lax.broadcasted_iota(jnp.int32, (width, LANES), 1)
    pick = (lane == column // RANK + holder * (width // RANK)).astype(jnp.float32)
    offsets = lax.broadcasted_iota(jnp.int32, (pad_rows, width), 0)
    line = lax.broadcasted_iota(jnp.int32, out.shape, 0)
    result = jnp.zeros(out.shape, jnp.float32)
    for seq in range(seq_part):
        live = offsets < lengths[quarter * seq_part + seq]
        sums = jnp.sum(
            jnp.where(live, pair[seq * pad_rows:(seq + 1) * pad_rows], 0.0), axis=0, keepdims=True
        )
        scores = jnp.dot(
            jnp.broadcast_to(sums, (8, width)), pick,
            precision=lax.Precision.HIGHEST, preferred_element_type=jnp.float32,
        )[:1]
        at = (position * QUARTERS + quarter) * seq_part + seq
        result = result + jnp.where(line == at, scores, 0.0)
    return result


def own_score_kernel(lengths, own, in1, in2, in3, out, act_other):
    width = act_other.shape[1]
    full = received(own, (in1, in2, in3))
    act_other[...] = full[:, 2 * width:]
    out[...] = score(full[:, :width] * full[:, width:2 * width], lengths, lax.axis_index("loop"), out)


def other_score_kernel(lengths, act_other, before, own, in1, in2, in3, out):
    pair = act_other[...] * received(own, (in1, in2, in3))
    out[...] = before[...] + score(pair, lengths, 1 - lax.axis_index("loop"), out)


def on_device(acts, grads, act_factors, grad_factors, lengths):
    loop_count = lax.axis_size("loop")
    layer_count = lax.axis_size("layer")
    acts, grads, act_factors, grad_factors = acts[0], grads[0], act_factors[0], grad_factors[0]
    seq_dev = lengths.shape[0]
    tok_rows, width = acts.shape[0], act_factors.shape[1]
    rows = tok_rows // QUARTERS
    queries = width * loop_count // RANK

    depth = grads.shape[1]

    def kernel(body, name, outs, specs, scratch, mib, work):
        return pl.pallas_call(
            body,
            name=name,
            out_shape=tuple(outs),
            in_specs=specs,
            out_specs=(IN_VMEM,) * len(outs),
            scratch_shapes=scratch,
            compiler_params=pltpu.CompilerParams(vmem_limit_bytes=mib * MIB),
            cost_estimate=pl.CostEstimate(
                flops=2 * tok_rows * width * work, bytes_accessed=mib * MIB, transcendentals=0
            ),
        )

    def own_shape(parts):
        return pltpu.VMEM((rows, parts * width), jnp.float32)

    def out_shapes(parts):
        return [pltpu.VMEM((rows + CODE_ROWS, parts * width), jnp.int16)] * (QUARTERS - 1)

    def to_quarters(outs):
        return [in_vmem(from_partner(outs[mask - 1], "layer", mask)) for mask in range(1, QUARTERS)]

    total_shape = pltpu.VMEM((QUARTERS, rows, width), jnp.float32)
    score_shape = pltpu.VMEM((seq_dev * loop_count, LANES), jnp.float32)

    other_act = from_partner(act_factors, "loop", 1)
    act_total, act_held, factor_held = kernel(
        act_own_kernel, "act_own_columns",
        (total_shape, pltpu.VMEM(acts.shape, acts.dtype), pltpu.VMEM(grad_factors.shape, grad_factors.dtype)),
        [IN_HBM] * 3,
        [pltpu.VMEM(act_factors.shape, act_factors.dtype), pltpu.SemaphoreType.DMA((3,))],
        ACT_OWN_MIB, acts.shape[1],
    )(in_hbm(acts), in_hbm(act_factors), in_hbm(grad_factors))
    later_factors, other_act, act_total = lax.optimization_barrier((grad_factors, other_act, act_total))
    other_grad = from_partner(later_factors, "loop", 1)
    (grad_total,) = kernel(
        grad_own_kernel, "grad_own_columns", (total_shape,), [IN_VMEM] * 2, [], 8, depth,
    )(in_vmem(grads), in_vmem(factor_held))
    own, *outs = kernel(
        act_other_kernel, "act_other_columns", (own_shape(3), *out_shapes(3)), [IN_VMEM] * 4, [total_shape],
        8, acts.shape[1],
    )(in_vmem(act_held), in_vmem(other_act), in_vmem(act_total), in_vmem(grad_total))
    own_in = to_quarters(outs)
    other, *outs = kernel(
        grad_other_kernel, "grad_other_columns", (own_shape(1), *out_shapes(1)), [IN_VMEM] * 2, [total_shape],
        8, depth,
    )(in_vmem(grads), in_vmem(other_grad))
    other_in = to_quarters(outs)
    before, act_other = kernel(
        own_score_kernel, "own_scores", (score_shape, own_shape(1)), [IN_SMEM] + [IN_VMEM] * 4, [], 8, 0,
    )(lengths, in_vmem(own), *own_in)
    (total,) = kernel(
        other_score_kernel, "other_scores", (score_shape,), [IN_SMEM] + [IN_VMEM] * 6, [], 8, 0,
    )(lengths, in_vmem(act_other), in_vmem(before), in_vmem(other), *other_in)

    total = total + from_partner(total, "loop", 1)
    gathered = [from_partner(total, "layer", mask) for mask in range(1, QUARTERS)]
    total = total + gathered[0] + gathered[1] + gathered[2]
    mask = QUARTERS
    while mask < layer_count:
        total = total + from_partner(total, "layer", mask)
        mask *= 2
    return total[:, :queries]


def solution(mesh):
    in_specs = (
        P("layer", ("groups", "loop"), None),
        P("layer", ("groups", "loop"), None),
        P("layer", None, "loop"),
        P("layer", None, "loop"),
        P(("groups", "loop")),
    )
    out_specs = P("groups", None)
    return jax.shard_map(
        on_device, mesh=mesh, in_specs=in_specs, out_specs=out_specs, check_vma=False
    )
```

time: 36.3 us -> 35.5 us (0.978)
  local copies, waits for them, and re-layouts: 2.05 us -> 0.8 us
  Pallas kernels: 7.39 us -> 8.63 us
  waiting for transfers between devices: 11 us -> 9.8 us
  starting transfers between devices: 15 us -> 15.4 us
    unnamed x6 -> x4, local copies, waits for them, and re-layouts: 2.05 us -> 0.8 us
    pallas_call x6, Pallas kernels: 7.39 us -> 8.63 us  [the longest x1 3.06 us: on_device(): kernel(act_own_kernel, 'act_own_columns', (total_shape, pltpu.VMEM(acts.s...]
    ppermute x13, waiting for transfers between devices: 11 us -> 9.8 us  [from_partner(): return lax.ppermute(value, axis, pairs)]
    ppermute x13, starting transfers between devices: 15 us -> 15.4 us  [from_partner(): return lax.ppermute(value, axis, pairs)]
  transfers between devices with their start and end apart: 13 -> 13, of which waited for: 8 -> 8; matrix products, arithmetic and copies ran while one was open for 0% -> 0% of each run, Pallas kernels for 18% -> 22%
where the time goes in v5:
time: 35.5 us; the launch traced here: 35.4 us
  starting transfers between devices  15.4 us (43%)
  waiting for transfers between devices  9.8 us (28%)
  Pallas kernels  8.63 us (24%)
  local copies, waits for them, and re-layouts  0.8 us (2%)
  other arithmetic  0.6 us (2%)
    ppermute x13, starting transfers between devices, from_partner(): return lax.ppermute(value, axis, pairs)  15.4 us
    ppermute x13, waiting for transfers between devices, from_partner(): return lax.ppermute(value, axis, pairs)  9.8 us
    pallas_call x1, Pallas kernels, on_device(): kernel(act_own_kernel, 'act_own_columns', (total_shape, pltpu.VMEM(acts.s...  3.06 us
    pallas_call x1, Pallas kernels, on_device(): kernel(grad_other_kernel, 'grad_other_columns', (own_shape(1), *out_shape...  1.66 us
    pallas_call x1, Pallas kernels, on_device(): kernel(grad_own_kernel, 'grad_own_columns', (total_shape,), [IN_VMEM] * 2...  1.58 us
    pallas_call x1, Pallas kernels, on_device(): kernel(own_score_kernel, 'own_scores', (score_shape, own_shape(1)), [IN_S...  0.87 us
    unnamed x4, local copies, waits for them, and re-layouts  0.8 us
    pallas_call x1, Pallas kernels, on_device(): kernel(other_score_kernel, 'other_scores', (score_shape,), [IN_SMEM] + [I...  0.78 us
  transfers between devices with their start and end apart: 13, of which 8 were waited for; matrix products, arithmetic and copies ran while one was open for 0% of the time, Pallas kernels for 22%

profile of v5, /device:TPU:0, one launch (start us, length us, event | category | flops | bytes accessed | tf_op | source)
XLA Modules:
  0.0 35.4 jit_solution(5295450368415941414)
XLA Ops:
  0.0 0.0 copy-start
  0.0 0.5 %collective-permute-start = (bf16[2048,256]{1,0:T(8,128)(2,1)}, bf16[2048,256]{1,0:T(8,128)(2,1)S(1)}, u32[]{:S(2)}, u32[]{:S(2)}) collective-permute-start(bf16[2048,256]{1,0:T(8,128)(2,1)} %bitcast.10), channel_id=1, source_target_pairs={{0,1},{1,0},{2,3},{3,2},{4,5},{5,4},{6,7},{7,6},{8,9},{9,8},{10,11... | collective-permute-start | bytes 3145736 | tf_op jit(solution)/shard_map/ppermute | solution.py:33
  0.5 3.1 %act_own_columns.1 = (f32[4,96,256]{2,1,0:T(8,128)S(1)}, bf16[384,2048]{1,0:T(8,128)(2,1)S(1)}, bf16[7168,256]{1,0:T(8,128)(2,1)S(1)}) custom-call(bf16[384,2048]{1,0:T(8,128)(2,1)} %bitcast.9, bf16[2048,256]{1,0:T(8,128)(2,1)} %bitcast.11, bf16[7168,256]{1,0:T(8,128)(2,1)} %bitcast.7), custom_call_target="tpu_custom_call" | custom-call | flops 402653184 | bytes 52428800 | tf_op jit(solution)/shard_map/act_own_columns/pallas_call | solution.py:185
  3.5 0.0 collective-permute-done.other_factor
  3.5 0.1 collective-permute-start.4
  3.6 0.8 %copy-done = bf16[1,384,7168]{2,1,0:T(8,128)(2,1)S(1)} copy-done((bf16[1,384,7168]{2,1,0:T(8,128)(2,1)S(1)}, bf16[1,384,7168]{2,1,0:T(8,128)(2,1)}, u32[]{:S(2)}) %copy-start) | copy-done | bytes 5505048
  4.4 1.6 %grad_own_columns.1.grad_total = f32[4,96,256]{2,1,0:T(8,128)S(1)} custom-call(bf16[384,7168]{1,0:T(8,128)(2,1)S(1)} %bitcast.5, bf16[7168,256]{1,0:T(8,128)(2,1)S(1)} %get-tuple-element.25.factor), custom_call_target="tpu_custom_call" | custom-call | flops 1409286144 | bytes 8388608 | tf_op jit(solution)/shard_map/grad_own_columns/pallas_call | solution.py:194
  6.0 0.7 %act_other_columns.1 = (f32[96,768]{1,0:T(8,128)S(1)}, s16[112,768]{1,0:T(8,128)(2,1)S(1)}, s16[112,768]{1,0:T(8,128)(2,1)S(1)}, s16[112,768]{1,0:T(8,128)(2,1)S(1)}) custom-call(bf16[384,2048]{1,0:T(8,128)(2,1)S(1)} %get-tuple-element.21.act_held, bf16[2048,256]{1,0:T(8,128)(2,1)S(1)} %collective-permute-done.other_factor, ...), custom_call_target="tpu_custom_call" | custom-call | flops 402653184 | bytes 8388608 | tf_op jit(solution)/shard_map/act_other_columns/pallas_call | solution.py:197
  6.7 3.0 %collective-permute-start.1 = (s16[112,768]{1,0:T(8,128)(2,1)S(1)}, s16[112,768]{1,0:T(8,128)(2,1)S(1)}, u32[]{:S(2)}, u32[]{:S(2)}) collective-permute-start(s16[112,768]{1,0:T(8,128)(2,1)S(1)} %get-tuple-element.27), channel_id=1, source_target_pairs={{0,2},{2,0},{4,6},{6,4},{8,10},{10,8},{12,14},{14,12},{1,3},{3,1},... | collective-permute-start | bytes 516104 | tf_op jit(solution)/shard_map/ppermute | solution.py:33
  9.7 1.6 %collective-permute-start.2 = (s16[112,768]{1,0:T(8,128)(2,1)S(1)}, s16[112,768]{1,0:T(8,128)(2,1)S(1)}, u32[]{:S(2)}, u32[]{:S(2)}) collective-permute-start(s16[112,768]{1,0:T(8,128)(2,1)S(1)} %get-tuple-element.28), channel_id=1, source_target_pairs={{0,4},{2,6},{4,0},{6,2},{8,12},{10,14},{12,8},{14,10},{1,5},{3,7},... | collective-permute-start | bytes 516104 | tf_op jit(solution)/shard_map/ppermute | solution.py:33
  11.3 0.0 copy-start.1
  11.3 0.0 collective-permute-start.3
  11.3 0.0 collective-permute-done.4.other_factor
  11.3 1.7 %grad_other_columns.1 = (f32[96,256]{1,0:T(8,128)S(1)}, s16[112,256]{1,0:T(8,128)(2,1)S(1)}, s16[112,256]{1,0:T(8,128)(2,1)S(1)}, s16[112,256]{1,0:T(8,128)(2,1)S(1)}) custom-call(bf16[384,7168]{1,0:T(8,128)(2,1)S(1)} %bitcast.6, bf16[7168,256]{1,0:T(8,128)(2,1)S(1)} %collective-permute-done.4.other_factor), custom_call_target="tpu_custom_call" | custom-call | flops 1409286144 | bytes 8388608 | tf_op jit(solution)/shard_map/grad_other_columns/pallas_call | solution.py:202
  13.0 2.0 %collective-permute-start.5 = (s16[112,256]{1,0:T(8,128)(2,1)S(1)}, s16[112,256]{1,0:T(8,128)(2,1)S(1)}, u32[]{:S(2)}, u32[]{:S(2)}) collective-permute-start(s16[112,256]{1,0:T(8,128)(2,1)S(1)} %get-tuple-element.34), channel_id=1, source_target_pairs={{0,2},{2,0},{4,6},{6,4},{8,10},{10,8},{12,14},{14,12},{1,3},{3,1},... | collective-permute-start | bytes 172040 | tf_op jit(solution)/shard_map/ppermute | solution.py:33
  14.9 1.6 %collective-permute-start.6 = (s16[112,256]{1,0:T(8,128)(2,1)S(1)}, s16[112,256]{1,0:T(8,128)(2,1)S(1)}, u32[]{:S(2)}, u32[]{:S(2)}) collective-permute-start(s16[112,256]{1,0:T(8,128)(2,1)S(1)} %get-tuple-element.35), channel_id=1, source_target_pairs={{0,4},{2,6},{4,0},{6,2},{8,12},{10,14},{12,8},{14,10},{1,5},{3,7},... | collective-permute-start | bytes 172040 | tf_op jit(solution)/shard_map/ppermute | solution.py:33
  16.5 0.0 collective-permute-done.1.in1
  16.5 0.6 %collective-permute-start.7 = (s16[112,256]{1,0:T(8,128)(2,1)S(1)}, s16[112,256]{1,0:T(8,128)(2,1)S(1)}, u32[]{:S(2)}, u32[]{:S(2)}) collective-permute-start(s16[112,256]{1,0:T(8,128)(2,1)S(1)} %get-tuple-element.36), channel_id=1, source_target_pairs={{0,6},{2,4},{4,2},{6,0},{8,14},{10,12},{12,10},{14,8},{1,7},{3,5},... | collective-permute-start | bytes 172040 | tf_op jit(solution)/shard_map/ppermute | solution.py:33
  17.1 0.0 collective-permute-done.2.in2
  17.1 2.6 %collective-permute-done.3.in3 = s16[112,768]{1,0:T(8,128)(2,1)S(1)} collective-permute-done((s16[112,768]{1,0:T(8,128)(2,1)S(1)}, s16[112,768]{1,0:T(8,128)(2,1)S(1)}, u32[]{:S(2)}, u32[]{:S(2)}) %collective-permute-start.3) | collective-permute-done | bytes 172064 | tf_op jit(solution)/shard_map/ppermute | solution.py:33
  19.8 0.0 copy-done.1
  19.8 0.9 %own_scores.1 = (f32[8,128]{1,0:T(8,128)S(1)}, f32[96,256]{1,0:T(8,128)S(1)}) custom-call(s32[4]{0:T(128)S(1)} %copy-done.1, f32[96,768]{1,0:T(8,128)S(1)} %get-tuple-element.26.own, s16[112,768]{1,0:T(8,128)(2,1)S(1)} %collective-permute-done.1.in1, s16[112,768]{1,0:T(8,128)(2,1)S(1)} %collective-permute-done.2.in2, ...), custom_call_target="tpu_custom_call" | custom-call | bytes 8388608 | tf_op jit(solution)/shard_map/own_scores/pallas_call | solution.py:207
  20.6 0.0 collective-permute-done.5.in1
  20.6 0.4 %collective-permute-done.6.in2 = s16[112,256]{1,0:T(8,128)(2,1)S(1)} collective-permute-done((s16[112,256]{1,0:T(8,128)(2,1)S(1)}, s16[112,256]{1,0:T(8,128)(2,1)S(1)}, u32[]{:S(2)}, u32[]{:S(2)}) %collective-permute-start.6) | collective-permute-done | bytes 57376 | tf_op jit(solution)/shard_map/ppermute | solution.py:33
  21.1 0.5 %collective-permute-done.7.in3 = s16[112,256]{1,0:T(8,128)(2,1)S(1)} collective-permute-done((s16[112,256]{1,0:T(8,128)(2,1)S(1)}, s16[112,256]{1,0:T(8,128)(2,1)S(1)}, u32[]{:S(2)}, u32[]{:S(2)}) %collective-permute-start.7) | collective-permute-done | bytes 57376 | tf_op jit(solution)/shard_map/ppermute | solution.py:33
  21.6 0.8 %other_scores.1 = f32[8,128]{1,0:T(8,128)S(1)} custom-call(s32[4]{0:T(128)S(1)} %copy-done.1, f32[96,256]{1,0:T(8,128)S(1)} %get-tuple-element.30.act_other, f32[8,128]{1,0:T(8,128)S(1)} %get-tuple-element.31.before, f32[96,256]{1,0:T(8,128)S(1)} %get-tuple-element.33.own, s16[112,256]{1,0:T(8,128)(2,1)S(1)} %collective-permute-done.5.in1, ...), custom_call_target="tpu_custom_call" | custom-call | bytes 8388608 | tf_op jit(solution)/shard_map/other_scores/pallas_call | solution.py:210
  22.4 0.1 collective-permute-start.8
  22.5 1.2 %collective-permute-done.8 = f32[8,128]{1,0:T(8,128)S(1)} collective-permute-done((f32[8,128]{1,0:T(8,128)S(1)}, f32[8,128]{1,0:T(8,128)S(1)}, u32[]{:S(2)}, u32[]{:S(2)}) %collective-permute-start.8) | collective-permute-done | bytes 4128 | tf_op jit(solution)/shard_map/ppermute | solution.py:33
  23.6 2.6 %collective-permute-start.11 = (f32[8,128]{1,0:T(8,128)S(1)}, f32[8,128]{1,0:T(8,128)S(1)}, u32[]{:S(2)}, u32[]{:S(2)}) collective-permute-start(f32[8,128]{1,0:T(8,128)S(1)} %add.15), channel_id=1, source_target_pairs={{0,6},{2,4},{4,2},{6,0},{8,14},{10,12},{12,10},{14,8},{1,7},{3,5},... | collective-permute-start | bytes 12296 | tf_op jit(solution)/shard_map/ppermute | solution.py:33
  26.2 0.4 %collective-permute-start.10 = (f32[8,128]{1,0:T(8,128)S(1)}, f32[8,128]{1,0:T(8,128)S(1)}, u32[]{:S(2)}, u32[]{:S(2)}) collective-permute-start(f32[8,128]{1,0:T(8,128)S(1)} %add.15), channel_id=1, source_target_pairs={{0,4},{2,6},{4,0},{6,2},{8,12},{10,14},{12,8},{14,10},{1,5},{3,7},... | collective-permute-start | bytes 12296 | tf_op jit(solution)/shard_map/ppermute | solution.py:33
  26.6 0.5 %collective-permute-start.9 = (f32[8,128]{1,0:T(8,128)S(1)}, f32[8,128]{1,0:T(8,128)S(1)}, u32[]{:S(2)}, u32[]{:S(2)}) collective-permute-start(f32[8,128]{1,0:T(8,128)S(1)} %add.15), channel_id=1, source_target_pairs={{0,2},{2,0},{4,6},{6,4},{8,10},{10,8},{12,14},{14,12},{1,3},{3,1},... | collective-permute-start | bytes 12296 | tf_op jit(solution)/shard_map/ppermute | solution.py:33
  27.1 1.0 %collective-permute-done.11 = f32[8,128]{1,0:T(8,128)S(1)} collective-permute-done((f32[8,128]{1,0:T(8,128)S(1)}, f32[8,128]{1,0:T(8,128)S(1)}, u32[]{:S(2)}, u32[]{:S(2)}) %collective-permute-start.11) | collective-permute-done | bytes 4128 | tf_op jit(solution)/shard_map/ppermute | solution.py:33
  28.1 1.7 %collective-permute-done.10 = f32[8,128]{1,0:T(8,128)S(1)} collective-permute-done((f32[8,128]{1,0:T(8,128)S(1)}, f32[8,128]{1,0:T(8,128)S(1)}, u32[]{:S(2)}, u32[]{:S(2)}) %collective-permute-start.10) | collective-permute-done | bytes 4128 | tf_op jit(solution)/shard_map/ppermute | solution.py:33
  29.8 0.4 %collective-permute-done.9 = f32[8,128]{1,0:T(8,128)S(1)} collective-permute-done((f32[8,128]{1,0:T(8,128)S(1)}, f32[8,128]{1,0:T(8,128)S(1)}, u32[]{:S(2)}, u32[]{:S(2)}) %collective-permute-start.9) | collective-permute-done | bytes 4128 | tf_op jit(solution)/shard_map/ppermute | solution.py:33
  30.3 2.6 %collective-permute-start.12 = (f32[8,128]{1,0:T(8,128)S(1)}, f32[8,128]{1,0:T(8,128)S(1)}, u32[]{:S(2)}, u32[]{:S(2)}) collective-permute-start(f32[8,128]{1,0:T(8,128)S(1)} %add_add_fusion), channel_id=1, source_target_pairs={{0,8},{2,10},{4,12},{6,14},{8,0},{10,2},{12,4},{14,6},{1,9},{3,11}... | collective-permute-start | bytes 12296 | tf_op jit(solution)/shard_map/ppermute | solution.py:33
  32.8 1.9 %collective-permute-done.12 = f32[8,128]{1,0:T(8,128)S(1)} collective-permute-done((f32[8,128]{1,0:T(8,128)S(1)}, f32[8,128]{1,0:T(8,128)S(1)}, u32[]{:S(2)}, u32[]{:S(2)}) %collective-permute-start.12) | collective-permute-done | bytes 4128 | tf_op jit(solution)/shard_map/ppermute | solution.py:33
  34.8 0.6 %add.19 = f32[8,128]{1,0:T(8,128)} add(f32[8,128]{1,0:T(8,128)S(1)} %add_add_fusion, f32[8,128]{1,0:T(8,128)S(1)} %collective-permute-done.12) | non-fusion elementwise | flops 1024 | bytes 12288 | tf_op jit(solution)/shard_map/add | solution.py:219
  (2 shorter events, 0.0 us)
Async XLA Ops:
  0.0 4.4 %copy-start = (bf16[1,384,7168]{2,1,0:T(8,128)(2,1)S(1)}, bf16[1,384,7168]{2,1,0:T(8,128)(2,1)}, u32[]{:S(2)}) copy-start(bf16[1,384,7168]{2,1,0:T(8,128)(2,1)} %param.6) | copy-start | bytes 16515076
  0.0 3.5 %collective-permute-start = (bf16[2048,256]{1,0:T(8,128)(2,1)}, bf16[2048,256]{1,0:T(8,128)(2,1)S(1)}, u32[]{:S(2)}, u32[]{:S(2)}) collective-permute-start(bf16[2048,256]{1,0:T(8,128)(2,1)} %bitcast.10), channel_id=1, source_target_pairs={{0,1},{1,0},{2,3},{3,2},{4,5},{5,4},{6,7},{7,6},{8,9},{9,8},{10,11... | collective-permute-start | bytes 3145736 | tf_op jit(solution)/shard_map/ppermute | solution.py:33
  3.5 7.8 %collective-permute-start.4 = (bf16[7168,256]{1,0:T(8,128)(2,1)}, bf16[7168,256]{1,0:T(8,128)(2,1)S(1)}, u32[]{:S(2)}, u32[]{:S(2)}) collective-permute-start(bf16[7168,256]{1,0:T(8,128)(2,1)} %bitcast.8), channel_id=1, source_target_pairs={{0,1},{1,0},{2,3},{3,2},{4,5},{5,4},{6,7},{7,6},{8,9},{9,8},{10,11... | collective-permute-start | bytes 11010056 | tf_op jit(solution)/shard_map/ppermute | solution.py:33
  6.7 9.8 %collective-permute-start.1 = (s16[112,768]{1,0:T(8,128)(2,1)S(1)}, s16[112,768]{1,0:T(8,128)(2,1)S(1)}, u32[]{:S(2)}, u32[]{:S(2)}) collective-permute-start(s16[112,768]{1,0:T(8,128)(2,1)S(1)} %get-tuple-element.27), channel_id=1, source_target_pairs={{0,2},{2,0},{4,6},{6,4},{8,10},{10,8},{12,14},{14,12},{1,3},{3,1},... | collective-permute-start | bytes 516104 | tf_op jit(solution)/shard_map/ppermute | solution.py:33
  9.7 7.4 %collective-permute-start.2 = (s16[112,768]{1,0:T(8,128)(2,1)S(1)}, s16[112,768]{1,0:T(8,128)(2,1)S(1)}, u32[]{:S(2)}, u32[]{:S(2)}) collective-permute-start(s16[112,768]{1,0:T(8,128)(2,1)S(1)} %get-tuple-element.28), channel_id=1, source_target_pairs={{0,4},{2,6},{4,0},{6,2},{8,12},{10,14},{12,8},{14,10},{1,5},{3,7},... | collective-permute-start | bytes 516104 | tf_op jit(solution)/shard_map/ppermute | solution.py:33
  11.3 8.5 %copy-start.1 = (s32[4]{0:T(128)S(1)}, s32[4]{0:T(128)}, u32[]{:S(2)}) copy-start(s32[4]{0:T(128)} %lengths.3) | copy-start | bytes 52
  11.3 8.5 %collective-permute-start.3 = (s16[112,768]{1,0:T(8,128)(2,1)S(1)}, s16[112,768]{1,0:T(8,128)(2,1)S(1)}, u32[]{:S(2)}, u32[]{:S(2)}) collective-permute-start(s16[112,768]{1,0:T(8,128)(2,1)S(1)} %get-tuple-element.29), channel_id=1, source_target_pairs={{0,6},{2,4},{4,2},{6,0},{8,14},{10,12},{12,10},{14,8},{1,7},{3,5},... | collective-permute-start | bytes 516104 | tf_op jit(solution)/shard_map/ppermute | solution.py:33
  13.0 7.7 %collective-permute-start.5 = (s16[112,256]{1,0:T(8,128)(2,1)S(1)}, s16[112,256]{1,0:T(8,128)(2,1)S(1)}, u32[]{:S(2)}, u32[]{:S(2)}) collective-permute-start(s16[112,256]{1,0:T(8,128)(2,1)S(1)} %get-tuple-element.34), channel_id=1, source_target_pairs={{0,2},{2,0},{4,6},{6,4},{8,10},{10,8},{12,14},{14,12},{1,3},{3,1},... | collective-permute-start | bytes 172040 | tf_op jit(solution)/shard_map/ppermute | solution.py:33
  14.9 6.1 %collective-permute-start.6 = (s16[112,256]{1,0:T(8,128)(2,1)S(1)}, s16[112,256]{1,0:T(8,128)(2,1)S(1)}, u32[]{:S(2)}, u32[]{:S(2)}) collective-permute-start(s16[112,256]{1,0:T(8,128)(2,1)S(1)} %get-tuple-element.35), channel_id=1, source_target_pairs={{0,4},{2,6},{4,0},{6,2},{8,12},{10,14},{12,8},{14,10},{1,5},{3,7},... | collective-permute-start | bytes 172040 | tf_op jit(solution)/shard_map/ppermute | solution.py:33
  16.5 5.1 %collective-permute-start.7 = (s16[112,256]{1,0:T(8,128)(2,1)S(1)}, s16[112,256]{1,0:T(8,128)(2,1)S(1)}, u32[]{:S(2)}, u32[]{:S(2)}) collective-permute-start(s16[112,256]{1,0:T(8,128)(2,1)S(1)} %get-tuple-element.36), channel_id=1, source_target_pairs={{0,6},{2,4},{4,2},{6,0},{8,14},{10,12},{12,10},{14,8},{1,7},{3,5},... | collective-permute-start | bytes 172040 | tf_op jit(solution)/shard_map/ppermute | solution.py:33
  22.4 1.2 %collective-permute-start.8 = (f32[8,128]{1,0:T(8,128)S(1)}, f32[8,128]{1,0:T(8,128)S(1)}, u32[]{:S(2)}, u32[]{:S(2)}) collective-permute-start(f32[8,128]{1,0:T(8,128)S(1)} %other_scores.1), channel_id=1, source_target_pairs={{0,1},{1,0},{2,3},{3,2},{4,5},{5,4},{6,7},{7,6},{8,9},{9,8},{10,11... | collective-permute-start | bytes 12296 | tf_op jit(solution)/shard_map/ppermute | solution.py:33
  23.6 4.5 %collective-permute-start.11 = (f32[8,128]{1,0:T(8,128)S(1)}, f32[8,128]{1,0:T(8,128)S(1)}, u32[]{:S(2)}, u32[]{:S(2)}) collective-permute-start(f32[8,128]{1,0:T(8,128)S(1)} %add.15), channel_id=1, source_target_pairs={{0,6},{2,4},{4,2},{6,0},{8,14},{10,12},{12,10},{14,8},{1,7},{3,5},... | collective-permute-start | bytes 12296 | tf_op jit(solution)/shard_map/ppermute | solution.py:33
  26.2 3.6 %collective-permute-start.10 = (f32[8,128]{1,0:T(8,128)S(1)}, f32[8,128]{1,0:T(8,128)S(1)}, u32[]{:S(2)}, u32[]{:S(2)}) collective-permute-start(f32[8,128]{1,0:T(8,128)S(1)} %add.15), channel_id=1, source_target_pairs={{0,4},{2,6},{4,0},{6,2},{8,12},{10,14},{12,8},{14,10},{1,5},{3,7},... | collective-permute-start | bytes 12296 | tf_op jit(solution)/shard_map/ppermute | solution.py:33
  26.6 3.6 %collective-permute-start.9 = (f32[8,128]{1,0:T(8,128)S(1)}, f32[8,128]{1,0:T(8,128)S(1)}, u32[]{:S(2)}, u32[]{:S(2)}) collective-permute-start(f32[8,128]{1,0:T(8,128)S(1)} %add.15), channel_id=1, source_target_pairs={{0,2},{2,0},{4,6},{6,4},{8,10},{10,8},{12,14},{14,12},{1,3},{3,1},... | collective-permute-start | bytes 12296 | tf_op jit(solution)/shard_map/ppermute | solution.py:33
  30.3 4.5 %collective-permute-start.12 = (f32[8,128]{1,0:T(8,128)S(1)}, f32[8,128]{1,0:T(8,128)S(1)}, u32[]{:S(2)}, u32[]{:S(2)}) collective-permute-start(f32[8,128]{1,0:T(8,128)S(1)} %add_add_fusion), channel_id=1, source_target_pairs={{0,8},{2,10},{4,12},{6,14},{8,0},{10,2},{12,4},{14,6},{1,9},{3,11}... | collective-permute-start | bytes 12296 | tf_op jit(solution)/shard_map/ppermute | solution.py:33

commit v6 on v5

--- a/solution.py
+++ b/solution.py
@@ -212,11 +212,12 @@
     )(lengths, in_vmem(act_other), in_vmem(before), in_vmem(other), *other_in)
 
     total = total + from_partner(total, "loop", 1)
-    gathered = [from_partner(total, "layer", mask) for mask in range(1, QUARTERS)]
+    both = ("layer", "loop")
+    gathered = [from_partner(total, both, (mask + 1) * loop_count - 1) for mask in range(1, QUARTERS)]
     total = total + gathered[0] + gathered[1] + gathered[2]
     mask = QUARTERS
     while mask < layer_count:
-        total = total + from_partner(total, "layer", mask)
+        total = total + from_partner(total, both, (mask + 1) * loop_count - 1)
         mask *= 2
     return total[:, :queries]
 

time: 35.5 us -> 34.1 us (0.961)
  waiting for transfers between devices: 9.8 us -> 9.09 us
  starting transfers between devices: 15.4 us -> 14.7 us
    ppermute x13, starting transfers between devices: 15.4 us -> 14.7 us  [from_partner(): return lax.ppermute(value, axis, pairs)]
    ppermute x13, waiting for transfers between devices: 9.8 us -> 9.09 us  [from_partner(): return lax.ppermute(value, axis, pairs)]
  transfers between devices with their start and end apart: 13 -> 13, of which waited for: 8 -> 8; matrix products, arithmetic and copies ran while one was open for 0% -> 0% of each run, Pallas kernels for 22% -> 23%
where the time goes in v6:
time: 34.1 us; the launch traced here: 33.9 us
  starting transfers between devices  14.7 us (43%)
  waiting for transfers between devices  9.09 us (27%)
  Pallas kernels  8.63 us (25%)
  local copies, waits for them, and re-layouts  0.8 us (2%)
  other arithmetic  0.6 us (2%)
    ppermute x13, starting transfers between devices, from_partner(): return lax.ppermute(value, axis, pairs)  14.7 us
    ppermute x13, waiting for transfers between devices, from_partner(): return lax.ppermute(value, axis, pairs)  9.09 us
    pallas_call x1, Pallas kernels, on_device(): kernel(act_own_kernel, 'act_own_columns', (total_shape, pltpu.VMEM(acts.s...  3.06 us
    pallas_call x1, Pallas kernels, on_device(): kernel(grad_other_kernel, 'grad_other_columns', (own_shape(1), *out_shape...  1.66 us
    pallas_call x1, Pallas kernels, on_device(): kernel(grad_own_kernel, 'grad_own_columns', (total_shape,), [IN_VMEM] * 2...  1.58 us
    pallas_call x1, Pallas kernels, on_device(): kernel(own_score_kernel, 'own_scores', (score_shape, own_shape(1)), [IN_S...  0.87 us
    unnamed x4, local copies, waits for them, and re-layouts  0.8 us
    pallas_call x1, Pallas kernels, on_device(): kernel(other_score_kernel, 'other_scores', (score_shape,), [IN_SMEM] + [I...  0.78 us
  transfers between devices with their start and end apart: 13, of which 8 were waited for; matrix products, arithmetic and copies ran while one was open for 0% of the time, Pallas kernels for 23%

profile of v6, /device:TPU:0, one launch (start us, length us, event | category | flops | bytes accessed | tf_op | source)
XLA Modules:
  0.0 33.9 jit_solution(14280142473828604592)
XLA Ops:
  0.0 0.0 copy-start
  0.0 0.5 %collective-permute-start = (bf16[2048,256]{1,0:T(8,128)(2,1)}, bf16[2048,256]{1,0:T(8,128)(2,1)S(1)}, u32[]{:S(2)}, u32[]{:S(2)}) collective-permute-start(bf16[2048,256]{1,0:T(8,128)(2,1)} %bitcast.10), channel_id=1, source_target_pairs={{0,1},{1,0},{2,3},{3,2},{4,5},{5,4},{6,7},{7,6},{8,9},{9,8},{10,11... | collective-permute-start | bytes 3145736 | tf_op jit(solution)/shard_map/ppermute | solution.py:33
  0.5 3.1 %act_own_columns.1 = (f32[4,96,256]{2,1,0:T(8,128)S(1)}, bf16[384,2048]{1,0:T(8,128)(2,1)S(1)}, bf16[7168,256]{1,0:T(8,128)(2,1)S(1)}) custom-call(bf16[384,2048]{1,0:T(8,128)(2,1)} %bitcast.9, bf16[2048,256]{1,0:T(8,128)(2,1)} %bitcast.11, bf16[7168,256]{1,0:T(8,128)(2,1)} %bitcast.7), custom_call_target="tpu_custom_call" | custom-call | flops 402653184 | bytes 52428800 | tf_op jit(solution)/shard_map/act_own_columns/pallas_call | solution.py:185
  3.5 0.0 collective-permute-done.other_factor
  3.5 0.1 collective-permute-start.4
  3.6 0.8 %copy-done = bf16[1,384,7168]{2,1,0:T(8,128)(2,1)S(1)} copy-done((bf16[1,384,7168]{2,1,0:T(8,128)(2,1)S(1)}, bf16[1,384,7168]{2,1,0:T(8,128)(2,1)}, u32[]{:S(2)}) %copy-start) | copy-done | bytes 5505048
  4.4 1.6 %grad_own_columns.1.grad_total = f32[4,96,256]{2,1,0:T(8,128)S(1)} custom-call(bf16[384,7168]{1,0:T(8,128)(2,1)S(1)} %bitcast.5, bf16[7168,256]{1,0:T(8,128)(2,1)S(1)} %get-tuple-element.25.factor), custom_call_target="tpu_custom_call" | custom-call | flops 1409286144 | bytes 8388608 | tf_op jit(solution)/shard_map/grad_own_columns/pallas_call | solution.py:194
  6.0 0.7 %act_other_columns.1 = (f32[96,768]{1,0:T(8,128)S(1)}, s16[112,768]{1,0:T(8,128)(2,1)S(1)}, s16[112,768]{1,0:T(8,128)(2,1)S(1)}, s16[112,768]{1,0:T(8,128)(2,1)S(1)}) custom-call(bf16[384,2048]{1,0:T(8,128)(2,1)S(1)} %get-tuple-element.21.act_held, bf16[2048,256]{1,0:T(8,128)(2,1)S(1)} %collective-permute-done.other_factor, ...), custom_call_target="tpu_custom_call" | custom-call | flops 402653184 | bytes 8388608 | tf_op jit(solution)/shard_map/act_other_columns/pallas_call | solution.py:197
  6.7 3.0 %collective-permute-start.1 = (s16[112,768]{1,0:T(8,128)(2,1)S(1)}, s16[112,768]{1,0:T(8,128)(2,1)S(1)}, u32[]{:S(2)}, u32[]{:S(2)}) collective-permute-start(s16[112,768]{1,0:T(8,128)(2,1)S(1)} %get-tuple-element.27), channel_id=1, source_target_pairs={{0,2},{2,0},{4,6},{6,4},{8,10},{10,8},{12,14},{14,12},{1,3},{3,1},... | collective-permute-start | bytes 516104 | tf_op jit(solution)/shard_map/ppermute | solution.py:33
  9.7 1.6 %collective-permute-start.2 = (s16[112,768]{1,0:T(8,128)(2,1)S(1)}, s16[112,768]{1,0:T(8,128)(2,1)S(1)}, u32[]{:S(2)}, u32[]{:S(2)}) collective-permute-start(s16[112,768]{1,0:T(8,128)(2,1)S(1)} %get-tuple-element.28), channel_id=1, source_target_pairs={{0,4},{2,6},{4,0},{6,2},{8,12},{10,14},{12,8},{14,10},{1,5},{3,7},... | collective-permute-start | bytes 516104 | tf_op jit(solution)/shard_map/ppermute | solution.py:33
  11.3 0.0 copy-start.1
  11.3 0.0 collective-permute-start.3
  11.3 0.0 collective-permute-done.4.other_factor
  11.3 1.7 %grad_other_columns.1 = (f32[96,256]{1,0:T(8,128)S(1)}, s16[112,256]{1,0:T(8,128)(2,1)S(1)}, s16[112,256]{1,0:T(8,128)(2,1)S(1)}, s16[112,256]{1,0:T(8,128)(2,1)S(1)}) custom-call(bf16[384,7168]{1,0:T(8,128)(2,1)S(1)} %bitcast.6, bf16[7168,256]{1,0:T(8,128)(2,1)S(1)} %collective-permute-done.4.other_factor), custom_call_target="tpu_custom_call" | custom-call | flops 1409286144 | bytes 8388608 | tf_op jit(solution)/shard_map/grad_other_columns/pallas_call | solution.py:202
  13.0 2.0 %collective-permute-start.5 = (s16[112,256]{1,0:T(8,128)(2,1)S(1)}, s16[112,256]{1,0:T(8,128)(2,1)S(1)}, u32[]{:S(2)}, u32[]{:S(2)}) collective-permute-start(s16[112,256]{1,0:T(8,128)(2,1)S(1)} %get-tuple-element.34), channel_id=1, source_target_pairs={{0,2},{2,0},{4,6},{6,4},{8,10},{10,8},{12,14},{14,12},{1,3},{3,1},... | collective-permute-start | bytes 172040 | tf_op jit(solution)/shard_map/ppermute | solution.py:33
  14.9 1.6 %collective-permute-start.6 = (s16[112,256]{1,0:T(8,128)(2,1)S(1)}, s16[112,256]{1,0:T(8,128)(2,1)S(1)}, u32[]{:S(2)}, u32[]{:S(2)}) collective-permute-start(s16[112,256]{1,0:T(8,128)(2,1)S(1)} %get-tuple-element.35), channel_id=1, source_target_pairs={{0,4},{2,6},{4,0},{6,2},{8,12},{10,14},{12,8},{14,10},{1,5},{3,7},... | collective-permute-start | bytes 172040 | tf_op jit(solution)/shard_map/ppermute | solution.py:33
  16.5 0.0 collective-permute-done.1.in1
  16.5 0.6 %collective-permute-start.7 = (s16[112,256]{1,0:T(8,128)(2,1)S(1)}, s16[112,256]{1,0:T(8,128)(2,1)S(1)}, u32[]{:S(2)}, u32[]{:S(2)}) collective-permute-start(s16[112,256]{1,0:T(8,128)(2,1)S(1)} %get-tuple-element.36), channel_id=1, source_target_pairs={{0,6},{2,4},{4,2},{6,0},{8,14},{10,12},{12,10},{14,8},{1,7},{3,5},... | collective-permute-start | bytes 172040 | tf_op jit(solution)/shard_map/ppermute | solution.py:33
  17.1 0.0 collective-permute-done.2.in2
  17.1 2.6 %collective-permute-done.3.in3 = s16[112,768]{1,0:T(8,128)(2,1)S(1)} collective-permute-done((s16[112,768]{1,0:T(8,128)(2,1)S(1)}, s16[112,768]{1,0:T(8,128)(2,1)S(1)}, u32[]{:S(2)}, u32[]{:S(2)}) %collective-permute-start.3) | collective-permute-done | bytes 172064 | tf_op jit(solution)/shard_map/ppermute | solution.py:33
  19.8 0.0 copy-done.1
  19.8 0.9 %own_scores.1 = (f32[8,128]{1,0:T(8,128)S(1)}, f32[96,256]{1,0:T(8,128)S(1)}) custom-call(s32[4]{0:T(128)S(1)} %copy-done.1, f32[96,768]{1,0:T(8,128)S(1)} %get-tuple-element.26.own, s16[112,768]{1,0:T(8,128)(2,1)S(1)} %collective-permute-done.1.in1, s16[112,768]{1,0:T(8,128)(2,1)S(1)} %collective-permute-done.2.in2, ...), custom_call_target="tpu_custom_call" | custom-call | bytes 8388608 | tf_op jit(solution)/shard_map/own_scores/pallas_call | solution.py:207
  20.6 0.0 collective-permute-done.5.in1
  20.6 0.4 %collective-permute-done.6.in2 = s16[112,256]{1,0:T(8,128)(2,1)S(1)} collective-permute-done((s16[112,256]{1,0:T(8,128)(2,1)S(1)}, s16[112,256]{1,0:T(8,128)(2,1)S(1)}, u32[]{:S(2)}, u32[]{:S(2)}) %collective-permute-start.6) | collective-permute-done | bytes 57376 | tf_op jit(solution)/shard_map/ppermute | solution.py:33
  21.1 0.5 %collective-permute-done.7.in3 = s16[112,256]{1,0:T(8,128)(2,1)S(1)} collective-permute-done((s16[112,256]{1,0:T(8,128)(2,1)S(1)}, s16[112,256]{1,0:T(8,128)(2,1)S(1)}, u32[]{:S(2)}, u32[]{:S(2)}) %collective-permute-start.7) | collective-permute-done | bytes 57376 | tf_op jit(solution)/shard_map/ppermute | solution.py:33
  21.6 0.8 %other_scores.1 = f32[8,128]{1,0:T(8,128)S(1)} custom-call(s32[4]{0:T(128)S(1)} %copy-done.1, f32[96,256]{1,0:T(8,128)S(1)} %get-tuple-element.30.act_other, f32[8,128]{1,0:T(8,128)S(1)} %get-tuple-element.31.before, f32[96,256]{1,0:T(8,128)S(1)} %get-tuple-element.33.own, s16[112,256]{1,0:T(8,128)(2,1)S(1)} %collective-permute-done.5.in1, ...), custom_call_target="tpu_custom_call" | custom-call | bytes 8388608 | tf_op jit(solution)/shard_map/other_scores/pallas_call | solution.py:210
  22.4 0.1 collective-permute-start.8
  22.5 1.2 %collective-permute-done.8 = f32[8,128]{1,0:T(8,128)S(1)} collective-permute-done((f32[8,128]{1,0:T(8,128)S(1)}, f32[8,128]{1,0:T(8,128)S(1)}, u32[]{:S(2)}, u32[]{:S(2)}) %collective-permute-start.8) | collective-permute-done | bytes 4128 | tf_op jit(solution)/shard_map/ppermute | solution.py:33
  23.6 2.3 %collective-permute-start.11 = (f32[8,128]{1,0:T(8,128)S(1)}, f32[8,128]{1,0:T(8,128)S(1)}, u32[]{:S(2)}, u32[]{:S(2)}) collective-permute-start(f32[8,128]{1,0:T(8,128)S(1)} %add.15), channel_id=1, source_target_pairs={{0,7},{1,6},{2,5},{3,4},{4,3},{5,2},{6,1},{7,0},{8,15},{9,14},{10,... | collective-permute-start | bytes 12296 | tf_op jit(solution)/shard_map/ppermute | solution.py:33
  26.0 0.4 %collective-permute-start.10 = (f32[8,128]{1,0:T(8,128)S(1)}, f32[8,128]{1,0:T(8,128)S(1)}, u32[]{:S(2)}, u32[]{:S(2)}) collective-permute-start(f32[8,128]{1,0:T(8,128)S(1)} %add.15), channel_id=1, source_target_pairs={{0,5},{1,4},{2,7},{3,6},{4,1},{5,0},{6,3},{7,2},{8,13},{9,12},{10,... | collective-permute-start | bytes 12296 | tf_op jit(solution)/shard_map/ppermute | solution.py:33
  26.4 0.2 collective-permute-start.9
  26.6 0.9 %collective-permute-done.11 = f32[8,128]{1,0:T(8,128)S(1)} collective-permute-done((f32[8,128]{1,0:T(8,128)S(1)}, f32[8,128]{1,0:T(8,128)S(1)}, u32[]{:S(2)}, u32[]{:S(2)}) %collective-permute-start.11) | collective-permute-done | bytes 4128 | tf_op jit(solution)/shard_map/ppermute | solution.py:33
  27.5 1.4 %collective-permute-done.10 = f32[8,128]{1,0:T(8,128)S(1)} collective-permute-done((f32[8,128]{1,0:T(8,128)S(1)}, f32[8,128]{1,0:T(8,128)S(1)}, u32[]{:S(2)}, u32[]{:S(2)}) %collective-permute-start.10) | collective-permute-done | bytes 4128 | tf_op jit(solution)/shard_map/ppermute | solution.py:33
  29.0 0.4 %collective-permute-done.9 = f32[8,128]{1,0:T(8,128)S(1)} collective-permute-done((f32[8,128]{1,0:T(8,128)S(1)}, f32[8,128]{1,0:T(8,128)S(1)}, u32[]{:S(2)}, u32[]{:S(2)}) %collective-permute-start.9) | collective-permute-done | bytes 4128 | tf_op jit(solution)/shard_map/ppermute | solution.py:33
  29.4 2.4 %collective-permute-start.12 = (f32[8,128]{1,0:T(8,128)S(1)}, f32[8,128]{1,0:T(8,128)S(1)}, u32[]{:S(2)}, u32[]{:S(2)}) collective-permute-start(f32[8,128]{1,0:T(8,128)S(1)} %add_add_fusion), channel_id=1, source_target_pairs={{0,9},{1,8},{2,11},{3,10},{4,13},{5,12},{6,15},{7,14},{8,1},{9,0},... | collective-permute-start | bytes 12296 | tf_op jit(solution)/shard_map/ppermute | solution.py:33
  31.8 1.6 %collective-permute-done.12 = f32[8,128]{1,0:T(8,128)S(1)} collective-permute-done((f32[8,128]{1,0:T(8,128)S(1)}, f32[8,128]{1,0:T(8,128)S(1)}, u32[]{:S(2)}, u32[]{:S(2)}) %collective-permute-start.12) | collective-permute-done | bytes 4128 | tf_op jit(solution)/shard_map/ppermute | solution.py:33
  33.3 0.6 %add.19 = f32[8,128]{1,0:T(8,128)} add(f32[8,128]{1,0:T(8,128)S(1)} %add_add_fusion, f32[8,128]{1,0:T(8,128)S(1)} %collective-permute-done.12) | non-fusion elementwise | flops 1024 | bytes 12288 | tf_op jit(solution)/shard_map/add | solution.py:220
  (2 shorter events, 0.0 us)
Async XLA Ops:
  0.0 4.4 %copy-start = (bf16[1,384,7168]{2,1,0:T(8,128)(2,1)S(1)}, bf16[1,384,7168]{2,1,0:T(8,128)(2,1)}, u32[]{:S(2)}) copy-start(bf16[1,384,7168]{2,1,0:T(8,128)(2,1)} %param.6) | copy-start | bytes 16515076
  0.0 3.5 %collective-permute-start = (bf16[2048,256]{1,0:T(8,128)(2,1)}, bf16[2048,256]{1,0:T(8,128)(2,1)S(1)}, u32[]{:S(2)}, u32[]{:S(2)}) collective-permute-start(bf16[2048,256]{1,0:T(8,128)(2,1)} %bitcast.10), channel_id=1, source_target_pairs={{0,1},{1,0},{2,3},{3,2},{4,5},{5,4},{6,7},{7,6},{8,9},{9,8},{10,11... | collective-permute-start | bytes 3145736 | tf_op jit(solution)/shard_map/ppermute | solution.py:33
  3.5 7.8 %collective-permute-start.4 = (bf16[7168,256]{1,0:T(8,128)(2,1)}, bf16[7168,256]{1,0:T(8,128)(2,1)S(1)}, u32[]{:S(2)}, u32[]{:S(2)}) collective-permute-start(bf16[7168,256]{1,0:T(8,128)(2,1)} %bitcast.8), channel_id=1, source_target_pairs={{0,1},{1,0},{2,3},{3,2},{4,5},{5,4},{6,7},{7,6},{8,9},{9,8},{10,11... | collective-permute-start | bytes 11010056 | tf_op jit(solution)/shard_map/ppermute | solution.py:33
  6.7 9.8 %collective-permute-start.1 = (s16[112,768]{1,0:T(8,128)(2,1)S(1)}, s16[112,768]{1,0:T(8,128)(2,1)S(1)}, u32[]{:S(2)}, u32[]{:S(2)}) collective-permute-start(s16[112,768]{1,0:T(8,128)(2,1)S(1)} %get-tuple-element.27), channel_id=1, source_target_pairs={{0,2},{2,0},{4,6},{6,4},{8,10},{10,8},{12,14},{14,12},{1,3},{3,1},... | collective-permute-start | bytes 516104 | tf_op jit(solution)/shard_map/ppermute | solution.py:33
  9.7 7.4 %collective-permute-start.2 = (s16[112,768]{1,0:T(8,128)(2,1)S(1)}, s16[112,768]{1,0:T(8,128)(2,1)S(1)}, u32[]{:S(2)}, u32[]{:S(2)}) collective-permute-start(s16[112,768]{1,0:T(8,128)(2,1)S(1)} %get-tuple-element.28), channel_id=1, source_target_pairs={{0,4},{2,6},{4,0},{6,2},{8,12},{10,14},{12,8},{14,10},{1,5},{3,7},... | collective-permute-start | bytes 516104 | tf_op jit(solution)/shard_map/ppermute | solution.py:33
  11.3 8.5 %copy-start.1 = (s32[4]{0:T(128)S(1)}, s32[4]{0:T(128)}, u32[]{:S(2)}) copy-start(s32[4]{0:T(128)} %lengths.3) | copy-start | bytes 52
  11.3 8.5 %collective-permute-start.3 = (s16[112,768]{1,0:T(8,128)(2,1)S(1)}, s16[112,768]{1,0:T(8,128)(2,1)S(1)}, u32[]{:S(2)}, u32[]{:S(2)}) collective-permute-start(s16[112,768]{1,0:T(8,128)(2,1)S(1)} %get-tuple-element.29), channel_id=1, source_target_pairs={{0,6},{2,4},{4,2},{6,0},{8,14},{10,12},{12,10},{14,8},{1,7},{3,5},... | collective-permute-start | bytes 516104 | tf_op jit(solution)/shard_map/ppermute | solution.py:33
  13.0 7.7 %collective-permute-start.5 = (s16[112,256]{1,0:T(8,128)(2,1)S(1)}, s16[112,256]{1,0:T(8,128)(2,1)S(1)}, u32[]{:S(2)}, u32[]{:S(2)}) collective-permute-start(s16[112,256]{1,0:T(8,128)(2,1)S(1)} %get-tuple-element.34), channel_id=1, source_target_pairs={{0,2},{2,0},{4,6},{6,4},{8,10},{10,8},{12,14},{14,12},{1,3},{3,1},... | collective-permute-start | bytes 172040 | tf_op jit(solution)/shard_map/ppermute | solution.py:33
  14.9 6.1 %collective-permute-start.6 = (s16[112,256]{1,0:T(8,128)(2,1)S(1)}, s16[112,256]{1,0:T(8,128)(2,1)S(1)}, u32[]{:S(2)}, u32[]{:S(2)}) collective-permute-start(s16[112,256]{1,0:T(8,128)(2,1)S(1)} %get-tuple-element.35), channel_id=1, source_target_pairs={{0,4},{2,6},{4,0},{6,2},{8,12},{10,14},{12,8},{14,10},{1,5},{3,7},... | collective-permute-start | bytes 172040 | tf_op jit(solution)/shard_map/ppermute | solution.py:33
  16.5 5.1 %collective-permute-start.7 = (s16[112,256]{1,0:T(8,128)(2,1)S(1)}, s16[112,256]{1,0:T(8,128)(2,1)S(1)}, u32[]{:S(2)}, u32[]{:S(2)}) collective-permute-start(s16[112,256]{1,0:T(8,128)(2,1)S(1)} %get-tuple-element.36), channel_id=1, source_target_pairs={{0,6},{2,4},{4,2},{6,0},{8,14},{10,12},{12,10},{14,8},{1,7},{3,5},... | collective-permute-start | bytes 172040 | tf_op jit(solution)/shard_map/ppermute | solution.py:33
  22.4 1.2 %collective-permute-start.8 = (f32[8,128]{1,0:T(8,128)S(1)}, f32[8,128]{1,0:T(8,128)S(1)}, u32[]{:S(2)}, u32[]{:S(2)}) collective-permute-start(f32[8,128]{1,0:T(8,128)S(1)} %other_scores.1), channel_id=1, source_target_pairs={{0,1},{1,0},{2,3},{3,2},{4,5},{5,4},{6,7},{7,6},{8,9},{9,8},{10,11... | collective-permute-start | bytes 12296 | tf_op jit(solution)/shard_map/ppermute | solution.py:33
  23.6 3.9 %collective-permute-start.11 = (f32[8,128]{1,0:T(8,128)S(1)}, f32[8,128]{1,0:T(8,128)S(1)}, u32[]{:S(2)}, u32[]{:S(2)}) collective-permute-start(f32[8,128]{1,0:T(8,128)S(1)} %add.15), channel_id=1, source_target_pairs={{0,7},{1,6},{2,5},{3,4},{4,3},{5,2},{6,1},{7,0},{8,15},{9,14},{10,... | collective-permute-start | bytes 12296 | tf_op jit(solution)/shard_map/ppermute | solution.py:33
  26.0 3.0 %collective-permute-start.10 = (f32[8,128]{1,0:T(8,128)S(1)}, f32[8,128]{1,0:T(8,128)S(1)}, u32[]{:S(2)}, u32[]{:S(2)}) collective-permute-start(f32[8,128]{1,0:T(8,128)S(1)} %add.15), channel_id=1, source_target_pairs={{0,5},{1,4},{2,7},{3,6},{4,1},{5,0},{6,3},{7,2},{8,13},{9,12},{10,... | collective-permute-start | bytes 12296 | tf_op jit(solution)/shard_map/ppermute | solution.py:33
  26.4 3.0 %collective-permute-start.9 = (f32[8,128]{1,0:T(8,128)S(1)}, f32[8,128]{1,0:T(8,128)S(1)}, u32[]{:S(2)}, u32[]{:S(2)}) collective-permute-start(f32[8,128]{1,0:T(8,128)S(1)} %add.15), channel_id=1, source_target_pairs={{0,3},{1,2},{2,1},{3,0},{4,7},{5,6},{6,5},{7,4},{8,11},{9,10},{10,... | collective-permute-start | bytes 12296 | tf_op jit(solution)/shard_map/ppermute | solution.py:33
  29.4 3.9 %collective-permute-start.12 = (f32[8,128]{1,0:T(8,128)S(1)}, f32[8,128]{1,0:T(8,128)S(1)}, u32[]{:S(2)}, u32[]{:S(2)}) collective-permute-start(f32[8,128]{1,0:T(8,128)S(1)} %add_add_fusion), channel_id=1, source_target_pairs={{0,9},{1,8},{2,11},{3,10},{4,13},{5,12},{6,15},{7,14},{8,1},{9,0},... | collective-permute-start | bytes 12296 | tf_op jit(solution)/shard_map/ppermute | solution.py:33

commit v7 on v5

--- a/solution.py
+++ b/solution.py
@@ -1,3 +1,5 @@
+import functools
+
 import jax
 import jax.numpy as jnp
 from jax import lax
@@ -107,44 +109,51 @@
     return full
 
 
-def score(pair, lengths, holder, out):
+def score(pair, seq_part, holder, out):
     quarter, position = lax.axis_index("layer") % QUARTERS, lax.axis_index("loop")
     rows, width = pair.shape
-    seq_part = lengths.shape[0] // QUARTERS
     pad_rows = rows // seq_part
     column = lax.broadcasted_iota(jnp.int32, (width, LANES), 0)
     lane = lax.broadcasted_iota(jnp.int32, (width, LANES), 1)
-    pick = (lane == column // RANK + holder * (width // RANK)).astype(jnp.float32)
-    offsets = lax.broadcasted_iota(jnp.int32, (pad_rows, width), 0)
+    pick = (lane == column // RANK + holder * (width // RANK)).astype(jnp.float32).astype(jnp.bfloat16)
     line = lax.broadcasted_iota(jnp.int32, out.shape, 0)
     result = jnp.zeros(out.shape, jnp.float32)
     for seq in range(seq_part):
-        live = offsets < lengths[quarter * seq_part + seq]
-        sums = jnp.sum(
-            jnp.where(live, pair[seq * pad_rows:(seq + 1) * pad_rows], 0.0), axis=0, keepdims=True
-        )
-        scores = jnp.dot(
-            jnp.broadcast_to(sums, (8, width)), pick,
-            precision=lax.Precision.HIGHEST, preferred_element_type=jnp.float32,
-        )[:1]
+        sums = jnp.sum(pair[seq * pad_rows:(seq + 1) * pad_rows], axis=0, keepdims=True)
+        high = sums.astype(jnp.bfloat16).astype(jnp.float32)
+        middle = (sums - high).astype(jnp.bfloat16).astype(jnp.float32)
+        low = sums - high - middle
+        term = lax.broadcasted_iota(jnp.int32, (8, width), 0)
+        terms = jnp.where(term == 0, high, jnp.where(term == 1, middle, jnp.where(term == 2, low, 0.0)))
+        scores = jnp.sum(dot(terms.astype(jnp.bfloat16), pick), axis=0, keepdims=True)
         at = (position * QUARTERS + quarter) * seq_part + seq
         result = result + jnp.where(line == at, scores, 0.0)
     return result
 
 
 def own_score_kernel(lengths, own, in1, in2, in3, out, act_other):
-    width = act_other.shape[1]
+    rows, width = act_other.shape
+    seq_part = lengths.shape[0] // QUARTERS
+    pad_rows = rows // seq_part
+    quarter = lax.axis_index("layer") % QUARTERS
     full = received(own, (in1, in2, in3))
-    act_other[...] = full[:, 2 * width:]
-    out[...] = score(full[:, :width] * full[:, width:2 * width], lengths, lax.axis_index("loop"), out)
-
-
-def other_score_kernel(lengths, act_other, before, own, in1, in2, in3, out):
+    offset = lax.broadcasted_iota(jnp.int32, (rows, width), 0)
+    live = jnp.zeros((rows, width), jnp.bool_)
+    for seq in range(seq_part):
+        first = seq * pad_rows
+        live = live | ((offset >= first) & (offset < first + lengths[quarter * seq_part + seq]))
+    act_other[...] = jnp.where(live, full[:, 2 * width:], 0.0)
+    pair = jnp.where(live, full[:, :width], 0.0) * full[:, width:2 * width]
+    out[...] = score(pair, seq_part, lax.axis_index("loop"), out)
+
+
+def other_score_kernel(seq_part, act_other, before, own, in1, in2, in3, out):
     pair = act_other[...] * received(own, (in1, in2, in3))
-    out[...] = before[...] + score(pair, lengths, 1 - lax.axis_index("loop"), out)
+    out[...] = before[...] + score(pair, seq_part, 1 - lax.axis_index("loop"), out)
 
 
 def on_device(acts, grads, act_factors, grad_factors, lengths):
+    both = ("layer", "loop")
     loop_count = lax.axis_size("loop")
     layer_count = lax.axis_size("layer")
     acts, grads, act_factors, grad_factors = acts[0], grads[0], act_factors[0], grad_factors[0]
@@ -204,19 +213,20 @@
         8, depth,
     )(in_vmem(grads), in_vmem(other_grad))
     other_in = to_quarters(outs)
+    seq_part = seq_dev // QUARTERS
     before, act_other = kernel(
         own_score_kernel, "own_scores", (score_shape, own_shape(1)), [IN_SMEM] + [IN_VMEM] * 4, [], 8, 0,
     )(lengths, in_vmem(own), *own_in)
     (total,) = kernel(
-        other_score_kernel, "other_scores", (score_shape,), [IN_SMEM] + [IN_VMEM] * 6, [], 8, 0,
-    )(lengths, in_vmem(act_other), in_vmem(before), in_vmem(other), *other_in)
+        functools.partial(other_score_kernel, seq_part), "other_scores", (score_shape,), [IN_VMEM] * 6, [], 8, 0,
+    )(in_vmem(act_other), in_vmem(before), in_vmem(other), *other_in)
 
     total = total + from_partner(total, "loop", 1)
-    gathered = [from_partner(total, "layer", mask) for mask in range(1, QUARTERS)]
+    gathered = [from_partner(total, both, mask * loop_count + 1) for mask in range(1, QUARTERS)]
     total = total + gathered[0] + gathered[1] + gathered[2]
     mask = QUARTERS
     while mask < layer_count:
-        total = total + from_partner(total, "layer", mask)
+        total = total + from_partner(total, both, mask * loop_count + 1)
         mask *= 2
     return total[:, :queries]
 

time: 35.5 us -> 33.4 us (0.941)
  starting transfers between devices: 15.4 us -> 14.6 us
  waiting for transfers between devices: 9.8 us -> 9.09 us
  Pallas kernels: 8.63 us -> 8.09 us
    ppermute x13, starting transfers between devices: 15.4 us -> 14.6 us  [from_partner(): return lax.ppermute(value, axis, pairs)]
    ppermute x13, waiting for transfers between devices: 9.8 us -> 9.09 us  [from_partner(): return lax.ppermute(value, axis, pairs)]
    pallas_call x1, Pallas kernels: 0.78 us -> 0.21 us  [on_device(): kernel(functools.partial(other_score_kernel, seq_part), 'other_scores', (...]
  transfers between devices with their start and end apart: 13 -> 13, of which waited for: 8 -> 8; matrix products, arithmetic and copies ran while one was open for 0% -> 0% of each run, Pallas kernels for 22% -> 24%
where the time goes in v7:
time: 33.4 us; the launch traced here: 33.3 us
  starting transfers between devices  14.6 us (44%)
  waiting for transfers between devices  9.09 us (27%)
  Pallas kernels  8.09 us (24%)
  local copies, waits for them, and re-layouts  0.8 us (2%)
  other arithmetic  0.6 us (2%)
    ppermute x13, starting transfers between devices, from_partner(): return lax.ppermute(value, axis, pairs)  14.6 us
    ppermute x13, waiting for transfers between devices, from_partner(): return lax.ppermute(value, axis, pairs)  9.09 us
    pallas_call x1, Pallas kernels, on_device(): kernel(act_own_kernel, 'act_own_columns', (total_shape, pltpu.VMEM(acts.s...  3.06 us
    pallas_call x1, Pallas kernels, on_device(): kernel(grad_other_kernel, 'grad_other_columns', (own_shape(1), *out_shape...  1.67 us
    pallas_call x1, Pallas kernels, on_device(): kernel(grad_own_kernel, 'grad_own_columns', (total_shape,), [IN_VMEM] * 2...  1.58 us
    pallas_call x1, Pallas kernels, on_device(): kernel(own_score_kernel, 'own_scores', (score_shape, own_shape(1)), [IN_S...  0.9 us
    unnamed x4, local copies, waits for them, and re-layouts  0.8 us
    pallas_call x1, Pallas kernels, on_device(): kernel(act_other_kernel, 'act_other_columns', (own_shape(3), *out_shapes(...  0.67 us
  transfers between devices with their start and end apart: 13, of which 8 were waited for; matrix products, arithmetic and copies ran while one was open for 0% of the time, Pallas kernels for 24%

profile of v7, /device:TPU:0, one launch (start us, length us, event | category | flops | bytes accessed | tf_op | source)
XLA Modules:
  0.0 33.3 jit_solution(1393084091558461201)
XLA Ops:
  0.0 0.0 copy-start
  0.0 0.5 %collective-permute-start = (bf16[2048,256]{1,0:T(8,128)(2,1)}, bf16[2048,256]{1,0:T(8,128)(2,1)S(1)}, u32[]{:S(2)}, u32[]{:S(2)}) collective-permute-start(bf16[2048,256]{1,0:T(8,128)(2,1)} %bitcast.10), channel_id=1, source_target_pairs={{0,1},{1,0},{2,3},{3,2},{4,5},{5,4},{6,7},{7,6},{8,9},{9,8},{10,11... | collective-permute-start | bytes 3145736 | tf_op jit(solution)/shard_map/ppermute | solution.py:35
  0.5 3.1 %act_own_columns.1 = (f32[4,96,256]{2,1,0:T(8,128)S(1)}, bf16[384,2048]{1,0:T(8,128)(2,1)S(1)}, bf16[7168,256]{1,0:T(8,128)(2,1)S(1)}) custom-call(bf16[384,2048]{1,0:T(8,128)(2,1)} %bitcast.9, bf16[2048,256]{1,0:T(8,128)(2,1)} %bitcast.11, bf16[7168,256]{1,0:T(8,128)(2,1)} %bitcast.7), custom_call_target="tpu_custom_call" | custom-call | flops 402653184 | bytes 52428800 | tf_op jit(solution)/shard_map/act_own_columns/pallas_call | solution.py:194
  3.5 0.0 collective-permute-done.other_factor
  3.5 0.1 collective-permute-start.4
  3.6 0.8 %copy-done = bf16[1,384,7168]{2,1,0:T(8,128)(2,1)S(1)} copy-done((bf16[1,384,7168]{2,1,0:T(8,128)(2,1)S(1)}, bf16[1,384,7168]{2,1,0:T(8,128)(2,1)}, u32[]{:S(2)}) %copy-start) | copy-done | bytes 5505048
  4.4 1.6 %grad_own_columns.1.grad_total = f32[4,96,256]{2,1,0:T(8,128)S(1)} custom-call(bf16[384,7168]{1,0:T(8,128)(2,1)S(1)} %bitcast.5, bf16[7168,256]{1,0:T(8,128)(2,1)S(1)} %get-tuple-element.25.factor), custom_call_target="tpu_custom_call" | custom-call | flops 1409286144 | bytes 8388608 | tf_op jit(solution)/shard_map/grad_own_columns/pallas_call | solution.py:203
  6.0 0.7 %act_other_columns.1 = (f32[96,768]{1,0:T(8,128)S(1)}, s16[112,768]{1,0:T(8,128)(2,1)S(1)}, s16[112,768]{1,0:T(8,128)(2,1)S(1)}, s16[112,768]{1,0:T(8,128)(2,1)S(1)}) custom-call(bf16[384,2048]{1,0:T(8,128)(2,1)S(1)} %get-tuple-element.21.act_held, bf16[2048,256]{1,0:T(8,128)(2,1)S(1)} %collective-permute-done.other_factor, ...), custom_call_target="tpu_custom_call" | custom-call | flops 402653184 | bytes 8388608 | tf_op jit(solution)/shard_map/act_other_columns/pallas_call | solution.py:206
  6.7 3.0 %collective-permute-start.1 = (s16[112,768]{1,0:T(8,128)(2,1)S(1)}, s16[112,768]{1,0:T(8,128)(2,1)S(1)}, u32[]{:S(2)}, u32[]{:S(2)}) collective-permute-start(s16[112,768]{1,0:T(8,128)(2,1)S(1)} %get-tuple-element.27), channel_id=1, source_target_pairs={{0,2},{2,0},{4,6},{6,4},{8,10},{10,8},{12,14},{14,12},{1,3},{3,1},... | collective-permute-start | bytes 516104 | tf_op jit(solution)/shard_map/ppermute | solution.py:35
  9.7 1.6 %collective-permute-start.2 = (s16[112,768]{1,0:T(8,128)(2,1)S(1)}, s16[112,768]{1,0:T(8,128)(2,1)S(1)}, u32[]{:S(2)}, u32[]{:S(2)}) collective-permute-start(s16[112,768]{1,0:T(8,128)(2,1)S(1)} %get-tuple-element.28), channel_id=1, source_target_pairs={{0,4},{2,6},{4,0},{6,2},{8,12},{10,14},{12,8},{14,10},{1,5},{3,7},... | collective-permute-start | bytes 516104 | tf_op jit(solution)/shard_map/ppermute | solution.py:35
  11.3 0.0 copy-start.1
  11.3 0.0 collective-permute-start.3
  11.3 0.0 collective-permute-done.4.other_factor
  11.3 1.7 %grad_other_columns.1 = (f32[96,256]{1,0:T(8,128)S(1)}, s16[112,256]{1,0:T(8,128)(2,1)S(1)}, s16[112,256]{1,0:T(8,128)(2,1)S(1)}, s16[112,256]{1,0:T(8,128)(2,1)S(1)}) custom-call(bf16[384,7168]{1,0:T(8,128)(2,1)S(1)} %bitcast.6, bf16[7168,256]{1,0:T(8,128)(2,1)S(1)} %collective-permute-done.4.other_factor), custom_call_target="tpu_custom_call" | custom-call | flops 1409286144 | bytes 8388608 | tf_op jit(solution)/shard_map/grad_other_columns/pallas_call | solution.py:211
  13.0 2.0 %collective-permute-start.5 = (s16[112,256]{1,0:T(8,128)(2,1)S(1)}, s16[112,256]{1,0:T(8,128)(2,1)S(1)}, u32[]{:S(2)}, u32[]{:S(2)}) collective-permute-start(s16[112,256]{1,0:T(8,128)(2,1)S(1)} %get-tuple-element.34), channel_id=1, source_target_pairs={{0,2},{2,0},{4,6},{6,4},{8,10},{10,8},{12,14},{14,12},{1,3},{3,1},... | collective-permute-start | bytes 172040 | tf_op jit(solution)/shard_map/ppermute | solution.py:35
  14.9 1.6 %collective-permute-start.6 = (s16[112,256]{1,0:T(8,128)(2,1)S(1)}, s16[112,256]{1,0:T(8,128)(2,1)S(1)}, u32[]{:S(2)}, u32[]{:S(2)}) collective-permute-start(s16[112,256]{1,0:T(8,128)(2,1)S(1)} %get-tuple-element.35), channel_id=1, source_target_pairs={{0,4},{2,6},{4,0},{6,2},{8,12},{10,14},{12,8},{14,10},{1,5},{3,7},... | collective-permute-start | bytes 172040 | tf_op jit(solution)/shard_map/ppermute | solution.py:35
  16.5 0.0 collective-permute-done.1.in1
  16.5 0.6 %collective-permute-start.7 = (s16[112,256]{1,0:T(8,128)(2,1)S(1)}, s16[112,256]{1,0:T(8,128)(2,1)S(1)}, u32[]{:S(2)}, u32[]{:S(2)}) collective-permute-start(s16[112,256]{1,0:T(8,128)(2,1)S(1)} %get-tuple-element.36), channel_id=1, source_target_pairs={{0,6},{2,4},{4,2},{6,0},{8,14},{10,12},{12,10},{14,8},{1,7},{3,5},... | collective-permute-start | bytes 172040 | tf_op jit(solution)/shard_map/ppermute | solution.py:35
  17.1 0.0 collective-permute-done.2.in2
  17.1 2.6 %collective-permute-done.3.in3 = s16[112,768]{1,0:T(8,128)(2,1)S(1)} collective-permute-done((s16[112,768]{1,0:T(8,128)(2,1)S(1)}, s16[112,768]{1,0:T(8,128)(2,1)S(1)}, u32[]{:S(2)}, u32[]{:S(2)}) %collective-permute-start.3) | collective-permute-done | bytes 172064 | tf_op jit(solution)/shard_map/ppermute | solution.py:35
  19.7 0.0 copy-done.1
  19.8 0.9 %own_scores.1 = (f32[8,128]{1,0:T(8,128)S(1)}, f32[96,256]{1,0:T(8,128)S(1)}) custom-call(s32[4]{0:T(128)S(1)} %copy-done.1, f32[96,768]{1,0:T(8,128)S(1)} %get-tuple-element.26.own, s16[112,768]{1,0:T(8,128)(2,1)S(1)} %collective-permute-done.1.in1, s16[112,768]{1,0:T(8,128)(2,1)S(1)} %collective-permute-done.2.in2, ...), custom_call_target="tpu_custom_call" | custom-call | bytes 8388608 | tf_op jit(solution)/shard_map/own_scores/pallas_call | solution.py:217
  20.6 0.0 collective-permute-done.5.in1
  20.7 0.4 %collective-permute-done.6.in2 = s16[112,256]{1,0:T(8,128)(2,1)S(1)} collective-permute-done((s16[112,256]{1,0:T(8,128)(2,1)S(1)}, s16[112,256]{1,0:T(8,128)(2,1)S(1)}, u32[]{:S(2)}, u32[]{:S(2)}) %collective-permute-start.6) | collective-permute-done | bytes 57376 | tf_op jit(solution)/shard_map/ppermute | solution.py:35
  21.1 0.5 %collective-permute-done.7.in3 = s16[112,256]{1,0:T(8,128)(2,1)S(1)} collective-permute-done((s16[112,256]{1,0:T(8,128)(2,1)S(1)}, s16[112,256]{1,0:T(8,128)(2,1)S(1)}, u32[]{:S(2)}, u32[]{:S(2)}) %collective-permute-start.7) | collective-permute-done | bytes 57376 | tf_op jit(solution)/shard_map/ppermute | solution.py:35
  21.6 0.2 other_scores.1
  21.8 0.0 collective-permute-start.8
  21.8 1.2 %collective-permute-done.8 = f32[8,128]{1,0:T(8,128)S(1)} collective-permute-done((f32[8,128]{1,0:T(8,128)S(1)}, f32[8,128]{1,0:T(8,128)S(1)}, u32[]{:S(2)}, u32[]{:S(2)}) %collective-permute-start.8) | collective-permute-done | bytes 4128 | tf_op jit(solution)/shard_map/ppermute | solution.py:35
  23.0 2.3 %collective-permute-start.11 = (f32[8,128]{1,0:T(8,128)S(1)}, f32[8,128]{1,0:T(8,128)S(1)}, u32[]{:S(2)}, u32[]{:S(2)}) collective-permute-start(f32[8,128]{1,0:T(8,128)S(1)} %add.15), channel_id=1, source_target_pairs={{0,7},{1,6},{2,5},{3,4},{4,3},{5,2},{6,1},{7,0},{8,15},{9,14},{10,... | collective-permute-start | bytes 12296 | tf_op jit(solution)/shard_map/ppermute | solution.py:35
  25.3 0.4 %collective-permute-start.10 = (f32[8,128]{1,0:T(8,128)S(1)}, f32[8,128]{1,0:T(8,128)S(1)}, u32[]{:S(2)}, u32[]{:S(2)}) collective-permute-start(f32[8,128]{1,0:T(8,128)S(1)} %add.15), channel_id=1, source_target_pairs={{0,5},{1,4},{2,7},{3,6},{4,1},{5,0},{6,3},{7,2},{8,13},{9,12},{10,... | collective-permute-start | bytes 12296 | tf_op jit(solution)/shard_map/ppermute | solution.py:35
  25.7 0.2 collective-permute-start.9
  26.0 0.9 %collective-permute-done.11 = f32[8,128]{1,0:T(8,128)S(1)} collective-permute-done((f32[8,128]{1,0:T(8,128)S(1)}, f32[8,128]{1,0:T(8,128)S(1)}, u32[]{:S(2)}, u32[]{:S(2)}) %collective-permute-start.11) | collective-permute-done | bytes 4128 | tf_op jit(solution)/shard_map/ppermute | solution.py:35
  26.9 1.4 %collective-permute-done.10 = f32[8,128]{1,0:T(8,128)S(1)} collective-permute-done((f32[8,128]{1,0:T(8,128)S(1)}, f32[8,128]{1,0:T(8,128)S(1)}, u32[]{:S(2)}, u32[]{:S(2)}) %collective-permute-start.10) | collective-permute-done | bytes 4128 | tf_op jit(solution)/shard_map/ppermute | solution.py:35
  28.4 0.4 %collective-permute-done.9 = f32[8,128]{1,0:T(8,128)S(1)} collective-permute-done((f32[8,128]{1,0:T(8,128)S(1)}, f32[8,128]{1,0:T(8,128)S(1)}, u32[]{:S(2)}, u32[]{:S(2)}) %collective-permute-start.9) | collective-permute-done | bytes 4128 | tf_op jit(solution)/shard_map/ppermute | solution.py:35
  28.8 2.4 %collective-permute-start.12 = (f32[8,128]{1,0:T(8,128)S(1)}, f32[8,128]{1,0:T(8,128)S(1)}, u32[]{:S(2)}, u32[]{:S(2)}) collective-permute-start(f32[8,128]{1,0:T(8,128)S(1)} %add_add_fusion), channel_id=1, source_target_pairs={{0,9},{1,8},{2,11},{3,10},{4,13},{5,12},{6,15},{7,14},{8,1},{9,0},... | collective-permute-start | bytes 12296 | tf_op jit(solution)/shard_map/ppermute | solution.py:35
  31.1 1.6 %collective-permute-done.12 = f32[8,128]{1,0:T(8,128)S(1)} collective-permute-done((f32[8,128]{1,0:T(8,128)S(1)}, f32[8,128]{1,0:T(8,128)S(1)}, u32[]{:S(2)}, u32[]{:S(2)}) %collective-permute-start.12) | collective-permute-done | bytes 4128 | tf_op jit(solution)/shard_map/ppermute | solution.py:35
  32.7 0.6 %add.19 = f32[8,128]{1,0:T(8,128)} add(f32[8,128]{1,0:T(8,128)S(1)} %add_add_fusion, f32[8,128]{1,0:T(8,128)S(1)} %collective-permute-done.12) | non-fusion elementwise | flops 1024 | bytes 12288 | tf_op jit(solution)/shard_map/add | solution.py:229
  (2 shorter events, 0.0 us)
Async XLA Ops:
  0.0 4.4 %copy-start = (bf16[1,384,7168]{2,1,0:T(8,128)(2,1)S(1)}, bf16[1,384,7168]{2,1,0:T(8,128)(2,1)}, u32[]{:S(2)}) copy-start(bf16[1,384,7168]{2,1,0:T(8,128)(2,1)} %param.6) | copy-start | bytes 16515076
  0.0 3.5 %collective-permute-start = (bf16[2048,256]{1,0:T(8,128)(2,1)}, bf16[2048,256]{1,0:T(8,128)(2,1)S(1)}, u32[]{:S(2)}, u32[]{:S(2)}) collective-permute-start(bf16[2048,256]{1,0:T(8,128)(2,1)} %bitcast.10), channel_id=1, source_target_pairs={{0,1},{1,0},{2,3},{3,2},{4,5},{5,4},{6,7},{7,6},{8,9},{9,8},{10,11... | collective-permute-start | bytes 3145736 | tf_op jit(solution)/shard_map/ppermute | solution.py:35
  3.5 7.8 %collective-permute-start.4 = (bf16[7168,256]{1,0:T(8,128)(2,1)}, bf16[7168,256]{1,0:T(8,128)(2,1)S(1)}, u32[]{:S(2)}, u32[]{:S(2)}) collective-permute-start(bf16[7168,256]{1,0:T(8,128)(2,1)} %bitcast.8), channel_id=1, source_target_pairs={{0,1},{1,0},{2,3},{3,2},{4,5},{5,4},{6,7},{7,6},{8,9},{9,8},{10,11... | collective-permute-start | bytes 11010056 | tf_op jit(solution)/shard_map/ppermute | solution.py:35
  6.7 9.8 %collective-permute-start.1 = (s16[112,768]{1,0:T(8,128)(2,1)S(1)}, s16[112,768]{1,0:T(8,128)(2,1)S(1)}, u32[]{:S(2)}, u32[]{:S(2)}) collective-permute-start(s16[112,768]{1,0:T(8,128)(2,1)S(1)} %get-tuple-element.27), channel_id=1, source_target_pairs={{0,2},{2,0},{4,6},{6,4},{8,10},{10,8},{12,14},{14,12},{1,3},{3,1},... | collective-permute-start | bytes 516104 | tf_op jit(solution)/shard_map/ppermute | solution.py:35
  9.7 7.4 %collective-permute-start.2 = (s16[112,768]{1,0:T(8,128)(2,1)S(1)}, s16[112,768]{1,0:T(8,128)(2,1)S(1)}, u32[]{:S(2)}, u32[]{:S(2)}) collective-permute-start(s16[112,768]{1,0:T(8,128)(2,1)S(1)} %get-tuple-element.28), channel_id=1, source_target_pairs={{0,4},{2,6},{4,0},{6,2},{8,12},{10,14},{12,8},{14,10},{1,5},{3,7},... | collective-permute-start | bytes 516104 | tf_op jit(solution)/shard_map/ppermute | solution.py:35
  11.3 8.5 %copy-start.1 = (s32[4]{0:T(128)S(1)}, s32[4]{0:T(128)}, u32[]{:S(2)}) copy-start(s32[4]{0:T(128)} %lengths.1) | copy-start | bytes 52
  11.3 8.5 %collective-permute-start.3 = (s16[112,768]{1,0:T(8,128)(2,1)S(1)}, s16[112,768]{1,0:T(8,128)(2,1)S(1)}, u32[]{:S(2)}, u32[]{:S(2)}) collective-permute-start(s16[112,768]{1,0:T(8,128)(2,1)S(1)} %get-tuple-element.29), channel_id=1, source_target_pairs={{0,6},{2,4},{4,2},{6,0},{8,14},{10,12},{12,10},{14,8},{1,7},{3,5},... | collective-permute-start | bytes 516104 | tf_op jit(solution)/shard_map/ppermute | solution.py:35
  13.0 7.7 %collective-permute-start.5 = (s16[112,256]{1,0:T(8,128)(2,1)S(1)}, s16[112,256]{1,0:T(8,128)(2,1)S(1)}, u32[]{:S(2)}, u32[]{:S(2)}) collective-permute-start(s16[112,256]{1,0:T(8,128)(2,1)S(1)} %get-tuple-element.34), channel_id=1, source_target_pairs={{0,2},{2,0},{4,6},{6,4},{8,10},{10,8},{12,14},{14,12},{1,3},{3,1},... | collective-permute-start | bytes 172040 | tf_op jit(solution)/shard_map/ppermute | solution.py:35
  14.9 6.1 %collective-permute-start.6 = (s16[112,256]{1,0:T(8,128)(2,1)S(1)}, s16[112,256]{1,0:T(8,128)(2,1)S(1)}, u32[]{:S(2)}, u32[]{:S(2)}) collective-permute-start(s16[112,256]{1,0:T(8,128)(2,1)S(1)} %get-tuple-element.35), channel_id=1, source_target_pairs={{0,4},{2,6},{4,0},{6,2},{8,12},{10,14},{12,8},{14,10},{1,5},{3,7},... | collective-permute-start | bytes 172040 | tf_op jit(solution)/shard_map/ppermute | solution.py:35
  16.5 5.1 %collective-permute-start.7 = (s16[112,256]{1,0:T(8,128)(2,1)S(1)}, s16[112,256]{1,0:T(8,128)(2,1)S(1)}, u32[]{:S(2)}, u32[]{:S(2)}) collective-permute-start(s16[112,256]{1,0:T(8,128)(2,1)S(1)} %get-tuple-element.36), channel_id=1, source_target_pairs={{0,6},{2,4},{4,2},{6,0},{8,14},{10,12},{12,10},{14,8},{1,7},{3,5},... | collective-permute-start | bytes 172040 | tf_op jit(solution)/shard_map/ppermute | solution.py:35
  21.8 1.2 %collective-permute-start.8 = (f32[8,128]{1,0:T(8,128)S(1)}, f32[8,128]{1,0:T(8,128)S(1)}, u32[]{:S(2)}, u32[]{:S(2)}) collective-permute-start(f32[8,128]{1,0:T(8,128)S(1)} %other_scores.1), channel_id=1, source_target_pairs={{0,1},{1,0},{2,3},{3,2},{4,5},{5,4},{6,7},{7,6},{8,9},{9,8},{10,11... | collective-permute-start | bytes 12296 | tf_op jit(solution)/shard_map/ppermute | solution.py:35
  23.0 3.9 %collective-permute-start.11 = (f32[8,128]{1,0:T(8,128)S(1)}, f32[8,128]{1,0:T(8,128)S(1)}, u32[]{:S(2)}, u32[]{:S(2)}) collective-permute-start(f32[8,128]{1,0:T(8,128)S(1)} %add.15), channel_id=1, source_target_pairs={{0,7},{1,6},{2,5},{3,4},{4,3},{5,2},{6,1},{7,0},{8,15},{9,14},{10,... | collective-permute-start | bytes 12296 | tf_op jit(solution)/shard_map/ppermute | solution.py:35
  25.3 3.0 %collective-permute-start.10 = (f32[8,128]{1,0:T(8,128)S(1)}, f32[8,128]{1,0:T(8,128)S(1)}, u32[]{:S(2)}, u32[]{:S(2)}) collective-permute-start(f32[8,128]{1,0:T(8,128)S(1)} %add.15), channel_id=1, source_target_pairs={{0,5},{1,4},{2,7},{3,6},{4,1},{5,0},{6,3},{7,2},{8,13},{9,12},{10,... | collective-permute-start | bytes 12296 | tf_op jit(solution)/shard_map/ppermute | solution.py:35
  25.7 3.0 %collective-permute-start.9 = (f32[8,128]{1,0:T(8,128)S(1)}, f32[8,128]{1,0:T(8,128)S(1)}, u32[]{:S(2)}, u32[]{:S(2)}) collective-permute-start(f32[8,128]{1,0:T(8,128)S(1)} %add.15), channel_id=1, source_target_pairs={{0,3},{1,2},{2,1},{3,0},{4,7},{5,6},{6,5},{7,4},{8,11},{9,10},{10,... | collective-permute-start | bytes 12296 | tf_op jit(solution)/shard_map/ppermute | solution.py:35
  28.8 3.9 %collective-permute-start.12 = (f32[8,128]{1,0:T(8,128)S(1)}, f32[8,128]{1,0:T(8,128)S(1)}, u32[]{:S(2)}, u32[]{:S(2)}) collective-permute-start(f32[8,128]{1,0:T(8,128)S(1)} %add_add_fusion), channel_id=1, source_target_pairs={{0,9},{1,8},{2,11},{3,10},{4,13},{5,12},{6,15},{7,14},{8,1},{9,0},... | collective-permute-start | bytes 12296 | tf_op jit(solution)/shard_map/ppermute | solution.py:35

commit v8 on v7

--- a/solution.py
+++ b/solution.py
@@ -10,7 +10,7 @@
 RANK = 32
 QUARTERS = 4
 LANES = 128
-CODE_ROWS = 16
+SUBLANES = 16
 TOP = 32000.0
 STEPS = 256.0
 FLOOR = 2.0**-112
@@ -39,18 +39,41 @@
     return jnp.dot(rows, factor, preferred_element_type=jnp.float32)
 
 
-def encode(part):
+def blocks(rows, width):
+    return [
+        (lane * (rows // SUBLANES) + row, row * SUBLANES, lane * LANES)
+        for lane in range(width // LANES)
+        for row in range(rows // SUBLANES)
+    ]
+
+
+def encode(part, out, codes, first):
+    rows, width = part.shape
     peak = jnp.max(jnp.abs(part), axis=0, keepdims=True)
     code = jnp.ceil(jnp.log2(jnp.maximum(peak, FLOOR)) * STEPS) + 1.0
     fixed = jnp.round(part * (TOP * jnp.exp2(code * (-1.0 / STEPS))))
-    code = jnp.broadcast_to(code, (CODE_ROWS, part.shape[1]))
-    return fixed.astype(jnp.int32).astype(jnp.int16), code.astype(jnp.int32).astype(jnp.int16)
-
-
-def decode(message, rows):
-    fixed = message[:rows, :].astype(jnp.int32).astype(jnp.float32)
-    code = message[rows:, :].astype(jnp.int32).astype(jnp.float32)[:1]
-    return fixed * (jnp.exp2(code * (1.0 / STEPS)) * (1.0 / TOP))
+    fixed = fixed.astype(jnp.int32).astype(jnp.int16)
+    lines, tiles = first // LANES, first // LANES * (rows // SUBLANES)
+    for tile, row, lane in blocks(rows, width):
+        out[tiles + tile] = fixed[row:row + SUBLANES, lane:lane + LANES]
+    for index in range(width // LANES):
+        codes[lines + index:lines + index + 1, :] = code[:, index * LANES:(index + 1) * LANES]
+
+
+def received(own, messages, out):
+    rows, width = own.shape
+    last = messages[0].shape[0] - 1
+    scales = [
+        jnp.exp2(message[last].astype(jnp.int32).astype(jnp.float32) * (1.0 / STEPS)) * (1.0 / TOP)
+        for message in messages
+    ]
+    for tile, row, lane in blocks(rows, width):
+        here = (slice(row, row + SUBLANES), slice(lane, lane + LANES))
+        line = lane // LANES
+        full = own[here]
+        for message, scale in zip(messages, scales):
+            full = full + message[tile].astype(jnp.int32).astype(jnp.float32) * scale[line:line + 1, :]
+        out[here] = full
 
 
 def keep(part, total):
@@ -59,14 +82,16 @@
         total[index] = part[index * rows:(index + 1) * rows]
 
 
-def share(total, quarter, own_ref, out_refs, first):
-    rows = own_ref.shape[0]
-    columns = slice(first, first + total.shape[2])
-    own_ref[:, columns] = total[quarter]
+def share(parts, quarter, own, outs, codes):
+    width = parts[0].shape[2]
+    for index, part in enumerate(parts):
+        own[:, index * width:(index + 1) * width] = part[quarter]
     for mask in range(1, QUARTERS):
-        fixed, code = encode(total[quarter ^ mask])
-        out_refs[mask - 1][:rows, columns] = fixed
-        out_refs[mask - 1][rows:, columns] = code
+        out = outs[mask - 1]
+        codes[...] = jnp.zeros_like(codes)
+        for index, part in enumerate(parts):
+            encode(part[quarter ^ mask], out, codes, index * width)
+        out[out.shape[0] - 1] = codes[...].astype(jnp.int32).astype(jnp.int16)
 
 
 def act_own_kernel(acts, factor, grad_factor, total, rows_held, grad_factor_held, factor_held, sems):
@@ -87,26 +112,16 @@
     keep(dot(grads[...], factor[...]), total)
 
 
-def act_other_kernel(act_held, other_factor, act_total, grad_total, own, out1, out2, out3, total):
+def act_other_kernel(act_held, other_factor, act_total, grad_total, own, out1, out2, out3, total, codes):
     quarter = lax.axis_index("layer") % QUARTERS
-    outs = (out1, out2, out3)
-    width = total.shape[2]
     keep(dot(act_held[...], other_factor[...]), total)
-    for index, part in enumerate((act_total, grad_total, total)):
-        share(part, quarter, own, outs, index * width)
-
-
-def grad_other_kernel(grads, other_factor, own, out1, out2, out3, total):
+    share((act_total, grad_total, total), quarter, own, (out1, out2, out3), codes)
+
+
+def grad_other_kernel(grads, other_factor, own, out1, out2, out3, total, codes):
     quarter = lax.axis_index("layer") % QUARTERS
     keep(dot(grads[...], other_factor[...]), total)
-    share(total, quarter, own, (out1, out2, out3), 0)
-
-
-def received(own, messages):
-    full = own[...]
-    for message in messages:
-        full = full + decode(message[...], own.shape[0])
-    return full
+    share((total,), quarter, own, (out1, out2, out3), codes)
 
 
 def score(pair, seq_part, holder, out):
@@ -131,12 +146,12 @@
     return result
 
 
-def own_score_kernel(lengths, own, in1, in2, in3, out, act_other):
+def own_score_kernel(lengths, own, in1, in2, in3, out, act_other, full):
     rows, width = act_other.shape
     seq_part = lengths.shape[0] // QUARTERS
     pad_rows = rows // seq_part
     quarter = lax.axis_index("layer") % QUARTERS
-    full = received(own, (in1, in2, in3))
+    received(own, (in1, in2, in3), full)
     offset = lax.broadcasted_iota(jnp.int32, (rows, width), 0)
     live = jnp.zeros((rows, width), jnp.bool_)
     for seq in range(seq_part):
@@ -147,8 +162,9 @@
     out[...] = score(pair, seq_part, lax.axis_index("loop"), out)
 
 
-def other_score_kernel(seq_part, act_other, before, own, in1, in2, in3, out):
-    pair = act_other[...] * received(own, (in1, in2, in3))
+def other_score_kernel(seq_part, act_other, before, own, in1, in2, in3, out, full):
+    received(own, (in1, in2, in3), full)
+    pair = act_other[...] * full[...]
     out[...] = before[...] + score(pair, seq_part, 1 - lax.axis_index("loop"), out)
 
 
@@ -182,12 +198,14 @@
         return pltpu.VMEM((rows, parts * width), jnp.float32)
 
     def out_shapes(parts):
-        return [pltpu.VMEM((rows + CODE_ROWS, parts * width), jnp.int16)] * (QUARTERS - 1)
+        tiles = (rows // SUBLANES) * (parts * width // LANES) + 1
+        return [pltpu.VMEM((tiles, SUBLANES, LANES), jnp.int16)] * (QUARTERS - 1)
 
     def to_quarters(outs):
-        return [in_vmem(from_partner(outs[mask - 1], "layer", mask)) for mask in range(1, QUARTERS)]
+        return [in_vmem(from_partner(outs[mask - 1], "layer", mask)) for mask in (3, 2, 1)]
 
     total_shape = pltpu.VMEM((QUARTERS, rows, width), jnp.float32)
+    codes_shape = pltpu.VMEM((SUBLANES, LANES), jnp.float32)
     score_shape = pltpu.VMEM((seq_dev * loop_count, LANES), jnp.float32)
 
     other_act = from_partner(act_factors, "loop", 1)
@@ -204,21 +222,22 @@
         grad_own_kernel, "grad_own_columns", (total_shape,), [IN_VMEM] * 2, [], 8, depth,
     )(in_vmem(grads), in_vmem(factor_held))
     own, *outs = kernel(
-        act_other_kernel, "act_other_columns", (own_shape(3), *out_shapes(3)), [IN_VMEM] * 4, [total_shape],
-        8, acts.shape[1],
+        act_other_kernel, "act_other_columns", (own_shape(3), *out_shapes(3)), [IN_VMEM] * 4,
+        [total_shape, codes_shape], 8, acts.shape[1],
     )(in_vmem(act_held), in_vmem(other_act), in_vmem(act_total), in_vmem(grad_total))
     own_in = to_quarters(outs)
     other, *outs = kernel(
-        grad_other_kernel, "grad_other_columns", (own_shape(1), *out_shapes(1)), [IN_VMEM] * 2, [total_shape],
-        8, depth,
+        grad_other_kernel, "grad_other_columns", (own_shape(1), *out_shapes(1)), [IN_VMEM] * 2,
+        [total_shape, codes_shape], 8, depth,
     )(in_vmem(grads), in_vmem(other_grad))
     other_in = to_quarters(outs)
     seq_part = seq_dev // QUARTERS
     before, act_other = kernel(
-        own_score_kernel, "own_scores", (score_shape, own_shape(1)), [IN_SMEM] + [IN_VMEM] * 4, [], 8, 0,
+        own_score_kernel, "own_scores", (score_shape, own_shape(1)), [IN_SMEM] + [IN_VMEM] * 4, [own_shape(3)], 8, 0,
     )(lengths, in_vmem(own), *own_in)
     (total,) = kernel(
-        functools.partial(other_score_kernel, seq_part), "other_scores", (score_shape,), [IN_VMEM] * 6, [], 8, 0,
+        functools.partial(other_score_kernel, seq_part), "other_scores", (score_shape,), [IN_VMEM] * 6,
+        [own_shape(1)], 8, 0,
     )(in_vmem(act_other), in_vmem(before), in_vmem(other), *other_in)
 
     total = total + from_partner(total, "loop", 1)

time: 33.4 us -> 32.1 us (0.961)
  waiting for transfers between devices: 9.09 us -> 7.48 us
  starting transfers between devices: 14.6 us -> 15 us
    ppermute x13, waiting for transfers between devices: 9.09 us -> 7.48 us  [from_partner(): return lax.ppermute(value, axis, pairs)]
    ppermute x13, starting transfers between devices: 14.6 us -> 15 us  [from_partner(): return lax.ppermute(value, axis, pairs)]
  transfers between devices with their start and end apart: 13 -> 13, of which waited for: 8 -> 8; matrix products, arithmetic and copies ran while one was open for 0% -> 0% of each run, Pallas kernels for 24% -> 25%
where the time goes in v8:
time: 32.1 us; the launch traced here: 32 us
  starting transfers between devices  15 us (47%)
  Pallas kernels  8.06 us (25%)
  waiting for transfers between devices  7.48 us (23%)
  local copies, waits for them, and re-layouts  0.8 us (2%)
  other arithmetic  0.6 us (2%)
    ppermute x13, starting transfers between devices, from_partner(): return lax.ppermute(value, axis, pairs)  15 us
    ppermute x13, waiting for transfers between devices, from_partner(): return lax.ppermute(value, axis, pairs)  7.48 us
    pallas_call x1, Pallas kernels, on_device(): kernel(act_own_kernel, 'act_own_columns', (total_shape, pltpu.VMEM(acts.s...  3.06 us
    pallas_call x1, Pallas kernels, on_device(): kernel(grad_other_kernel, 'grad_other_columns', (own_shape(1), *out_shape...  1.67 us
    pallas_call x1, Pallas kernels, on_device(): kernel(grad_own_kernel, 'grad_own_columns', (total_shape,), [IN_VMEM] * 2...  1.58 us
    pallas_call x1, Pallas kernels, on_device(): kernel(own_score_kernel, 'own_scores', (score_shape, own_shape(1)), [IN_S...  0.83 us
    unnamed x4, local copies, waits for them, and re-layouts  0.8 us
    pallas_call x1, Pallas kernels, on_device(): kernel(act_other_kernel, 'act_other_columns', (own_shape(3), *out_shapes(...  0.71 us
  transfers between devices with their start and end apart: 13, of which 8 were waited for; matrix products, arithmetic and copies ran while one was open for 0% of the time, Pallas kernels for 25%

profile of v8, /device:TPU:0, one launch (start us, length us, event | category | flops | bytes accessed | tf_op | source)
XLA Modules:
  0.0 32.0 jit_solution(7108514176527316781)
XLA Ops:
  0.0 0.0 copy-start
  0.0 0.5 %collective-permute-start = (bf16[2048,256]{1,0:T(8,128)(2,1)}, bf16[2048,256]{1,0:T(8,128)(2,1)S(1)}, u32[]{:S(2)}, u32[]{:S(2)}) collective-permute-start(bf16[2048,256]{1,0:T(8,128)(2,1)} %bitcast.10), channel_id=1, source_target_pairs={{0,1},{1,0},{2,3},{3,2},{4,5},{5,4},{6,7},{7,6},{8,9},{9,8},{10,11... | collective-permute-start | bytes 3145736 | tf_op jit(solution)/shard_map/ppermute | solution.py:35
  0.5 3.1 %act_own_columns.1 = (f32[4,96,256]{2,1,0:T(8,128)S(1)}, bf16[384,2048]{1,0:T(8,128)(2,1)S(1)}, bf16[7168,256]{1,0:T(8,128)(2,1)S(1)}) custom-call(bf16[384,2048]{1,0:T(8,128)(2,1)} %bitcast.9, bf16[2048,256]{1,0:T(8,128)(2,1)} %bitcast.11, bf16[7168,256]{1,0:T(8,128)(2,1)} %bitcast.7), custom_call_target="tpu_custom_call" | custom-call | flops 402653184 | bytes 52428800 | tf_op jit(solution)/shard_map/act_own_columns/pallas_call | solution.py:212
  3.5 0.0 collective-permute-done.other_factor
  3.5 0.1 collective-permute-start.4
  3.6 0.8 %copy-done = bf16[1,384,7168]{2,1,0:T(8,128)(2,1)S(1)} copy-done((bf16[1,384,7168]{2,1,0:T(8,128)(2,1)S(1)}, bf16[1,384,7168]{2,1,0:T(8,128)(2,1)}, u32[]{:S(2)}) %copy-start) | copy-done | bytes 5505048
  4.4 1.6 %grad_own_columns.1.grad_total = f32[4,96,256]{2,1,0:T(8,128)S(1)} custom-call(bf16[384,7168]{1,0:T(8,128)(2,1)S(1)} %bitcast.5, bf16[7168,256]{1,0:T(8,128)(2,1)S(1)} %get-tuple-element.25.factor), custom_call_target="tpu_custom_call" | custom-call | flops 1409286144 | bytes 8388608 | tf_op jit(solution)/shard_map/grad_own_columns/pallas_call | solution.py:221
  6.0 0.7 %act_other_columns.1 = (f32[96,768]{1,0:T(8,128)S(1)}, s16[37,16,128]{2,1,0:T(8,128)(2,1)S(1)}, s16[37,16,128]{2,1,0:T(8,128)(2,1)S(1)}, s16[37,16,128]{2,1,0:T(8,128)(2,1)S(1)}) custom-call(bf16[384,2048]{1,0:T(8,128)(2,1)S(1)} %get-tuple-element.21.act_held, bf16[2048,256]{1,0:T(8,128)(2,1)S(1)} %collective-permute-done.other_factor, ...), custom_call_target="tpu_custom_call" | custom-call | flops 402653184 | bytes 8388608 | tf_op jit(solution)/shard_map/act_other_columns/pallas_call | solution.py:224
  6.7 4.0 %collective-permute-start.1 = (s16[37,16,128]{2,1,0:T(8,128)(2,1)S(1)}, s16[37,16,128]{2,1,0:T(8,128)(2,1)S(1)}, u32[]{:S(2)}, u32[]{:S(2)}) collective-permute-start(s16[37,16,128]{2,1,0:T(8,128)(2,1)S(1)} %get-tuple-element.27), channel_id=1, source_target_pairs={{0,6},{2,4},{4,2},{6,0},{8,14},{10,12},{12,10},{14,8},{1,7},{3,5},... | collective-permute-start | bytes 454664 | tf_op jit(solution)/shard_map/ppermute | solution.py:35
  10.8 0.4 %collective-permute-start.2 = (s16[37,16,128]{2,1,0:T(8,128)(2,1)S(1)}, s16[37,16,128]{2,1,0:T(8,128)(2,1)S(1)}, u32[]{:S(2)}, u32[]{:S(2)}) collective-permute-start(s16[37,16,128]{2,1,0:T(8,128)(2,1)S(1)} %get-tuple-element.28), channel_id=1, source_target_pairs={{0,4},{2,6},{4,0},{6,2},{8,12},{10,14},{12,8},{14,10},{1,5},{3,7},... | collective-permute-start | bytes 454664 | tf_op jit(solution)/shard_map/ppermute | solution.py:35
  11.2 0.0 copy-start.1
  11.2 0.2 collective-permute-start.3
  11.4 0.0 collective-permute-done.4.other_factor
  11.4 1.7 %grad_other_columns.1 = (f32[96,256]{1,0:T(8,128)S(1)}, s16[13,16,128]{2,1,0:T(8,128)(2,1)S(1)}, s16[13,16,128]{2,1,0:T(8,128)(2,1)S(1)}, s16[13,16,128]{2,1,0:T(8,128)(2,1)S(1)}) custom-call(bf16[384,7168]{1,0:T(8,128)(2,1)S(1)} %bitcast.6, bf16[7168,256]{1,0:T(8,128)(2,1)S(1)} %collective-permute-done.4.other_factor), custom_call_target="tpu_custom_call" | custom-call | flops 1409286144 | bytes 8388608 | tf_op jit(solution)/shard_map/grad_other_columns/pallas_call | solution.py:229
  13.1 2.9 %collective-permute-start.5 = (s16[13,16,128]{2,1,0:T(8,128)(2,1)S(1)}, s16[13,16,128]{2,1,0:T(8,128)(2,1)S(1)}, u32[]{:S(2)}, u32[]{:S(2)}) collective-permute-start(s16[13,16,128]{2,1,0:T(8,128)(2,1)S(1)} %get-tuple-element.34), channel_id=1, source_target_pairs={{0,6},{2,4},{4,2},{6,0},{8,14},{10,12},{12,10},{14,8},{1,7},{3,5},... | collective-permute-start | bytes 159752 | tf_op jit(solution)/shard_map/ppermute | solution.py:35
  16.0 0.4 %collective-permute-start.6 = (s16[13,16,128]{2,1,0:T(8,128)(2,1)S(1)}, s16[13,16,128]{2,1,0:T(8,128)(2,1)S(1)}, u32[]{:S(2)}, u32[]{:S(2)}) collective-permute-start(s16[13,16,128]{2,1,0:T(8,128)(2,1)S(1)} %get-tuple-element.35), channel_id=1, source_target_pairs={{0,4},{2,6},{4,0},{6,2},{8,12},{10,14},{12,8},{14,10},{1,5},{3,7},... | collective-permute-start | bytes 159752 | tf_op jit(solution)/shard_map/ppermute | solution.py:35
  16.4 0.0 collective-permute-done.1.in1
  16.4 1.0 %collective-permute-start.7 = (s16[13,16,128]{2,1,0:T(8,128)(2,1)S(1)}, s16[13,16,128]{2,1,0:T(8,128)(2,1)S(1)}, u32[]{:S(2)}, u32[]{:S(2)}) collective-permute-start(s16[13,16,128]{2,1,0:T(8,128)(2,1)S(1)} %get-tuple-element.36), channel_id=1, source_target_pairs={{0,2},{2,0},{4,6},{6,4},{8,10},{10,8},{12,14},{14,12},{1,3},{3,1},... | collective-permute-start | bytes 159752 | tf_op jit(solution)/shard_map/ppermute | solution.py:35
  17.5 1.4 %collective-permute-done.2.in2 = s16[37,16,128]{2,1,0:T(8,128)(2,1)S(1)} collective-permute-done((s16[37,16,128]{2,1,0:T(8,128)(2,1)S(1)}, s16[37,16,128]{2,1,0:T(8,128)(2,1)S(1)}, u32[]{:S(2)}, u32[]{:S(2)}) %collective-permute-start.2) | collective-permute-done | bytes 151584 | tf_op jit(solution)/shard_map/ppermute | solution.py:35
  18.9 0.0 collective-permute-done.3.in3
  18.9 0.0 copy-done.1
  18.9 0.8 %own_scores.1 = (f32[8,128]{1,0:T(8,128)S(1)}, f32[96,256]{1,0:T(8,128)S(1)}) custom-call(s32[4]{0:T(128)S(1)} %copy-done.1, f32[96,768]{1,0:T(8,128)S(1)} %get-tuple-element.26.own, s16[37,16,128]{2,1,0:T(8,128)(2,1)S(1)} %collective-permute-done.1.in1, s16[37,16,128]{2,1,0:T(8,128)(2,1)S(1)} %collective-permute-done.2.in2, ...), custom_call_target="tpu_custom_call" | custom-call | bytes 8388608 | tf_op jit(solution)/shard_map/own_scores/pallas_call | solution.py:235
  19.7 0.0 collective-permute-done.5.in1
  19.7 0.7 %collective-permute-done.6.in2 = s16[13,16,128]{2,1,0:T(8,128)(2,1)S(1)} collective-permute-done((s16[13,16,128]{2,1,0:T(8,128)(2,1)S(1)}, s16[13,16,128]{2,1,0:T(8,128)(2,1)S(1)}, u32[]{:S(2)}, u32[]{:S(2)}) %collective-permute-start.6) | collective-permute-done | bytes 53280 | tf_op jit(solution)/shard_map/ppermute | solution.py:35
  20.4 0.2 collective-permute-done.7.in3
  20.6 0.2 other_scores.1
  20.8 0.0 collective-permute-start.8
  20.8 1.2 %collective-permute-done.8 = f32[8,128]{1,0:T(8,128)S(1)} collective-permute-done((f32[8,128]{1,0:T(8,128)S(1)}, f32[8,128]{1,0:T(8,128)S(1)}, u32[]{:S(2)}, u32[]{:S(2)}) %collective-permute-start.8) | collective-permute-done | bytes 4128 | tf_op jit(solution)/shard_map/ppermute | solution.py:35
  22.0 2.1 %collective-permute-start.11 = (f32[8,128]{1,0:T(8,128)S(1)}, f32[8,128]{1,0:T(8,128)S(1)}, u32[]{:S(2)}, u32[]{:S(2)}) collective-permute-start(f32[8,128]{1,0:T(8,128)S(1)} %add.15), channel_id=1, source_target_pairs={{0,7},{1,6},{2,5},{3,4},{4,3},{5,2},{6,1},{7,0},{8,15},{9,14},{10,... | collective-permute-start | bytes 12296 | tf_op jit(solution)/shard_map/ppermute | solution.py:35
  24.0 0.4 %collective-permute-start.10 = (f32[8,128]{1,0:T(8,128)S(1)}, f32[8,128]{1,0:T(8,128)S(1)}, u32[]{:S(2)}, u32[]{:S(2)}) collective-permute-start(f32[8,128]{1,0:T(8,128)S(1)} %add.15), channel_id=1, source_target_pairs={{0,5},{1,4},{2,7},{3,6},{4,1},{5,0},{6,3},{7,2},{8,13},{9,12},{10,... | collective-permute-start | bytes 12296 | tf_op jit(solution)/shard_map/ppermute | solution.py:35
  24.4 0.5 %collective-permute-start.9 = (f32[8,128]{1,0:T(8,128)S(1)}, f32[8,128]{1,0:T(8,128)S(1)}, u32[]{:S(2)}, u32[]{:S(2)}) collective-permute-start(f32[8,128]{1,0:T(8,128)S(1)} %add.15), channel_id=1, source_target_pairs={{0,3},{1,2},{2,1},{3,0},{4,7},{5,6},{6,5},{7,4},{8,11},{9,10},{10,... | collective-permute-start | bytes 12296 | tf_op jit(solution)/shard_map/ppermute | solution.py:35
  24.9 0.9 %collective-permute-done.11 = f32[8,128]{1,0:T(8,128)S(1)} collective-permute-done((f32[8,128]{1,0:T(8,128)S(1)}, f32[8,128]{1,0:T(8,128)S(1)}, u32[]{:S(2)}, u32[]{:S(2)}) %collective-permute-start.11) | collective-permute-done | bytes 4128 | tf_op jit(solution)/shard_map/ppermute | solution.py:35
  25.9 1.2 %collective-permute-done.10 = f32[8,128]{1,0:T(8,128)S(1)} collective-permute-done((f32[8,128]{1,0:T(8,128)S(1)}, f32[8,128]{1,0:T(8,128)S(1)}, u32[]{:S(2)}, u32[]{:S(2)}) %collective-permute-start.10) | collective-permute-done | bytes 4128 | tf_op jit(solution)/shard_map/ppermute | solution.py:35
  27.1 0.4 %collective-permute-done.9 = f32[8,128]{1,0:T(8,128)S(1)} collective-permute-done((f32[8,128]{1,0:T(8,128)S(1)}, f32[8,128]{1,0:T(8,128)S(1)}, u32[]{:S(2)}, u32[]{:S(2)}) %collective-permute-start.9) | collective-permute-done | bytes 4128 | tf_op jit(solution)/shard_map/ppermute | solution.py:35
  27.5 2.4 %collective-permute-start.12 = (f32[8,128]{1,0:T(8,128)S(1)}, f32[8,128]{1,0:T(8,128)S(1)}, u32[]{:S(2)}, u32[]{:S(2)}) collective-permute-start(f32[8,128]{1,0:T(8,128)S(1)} %add_add_fusion), channel_id=1, source_target_pairs={{0,9},{1,8},{2,11},{3,10},{4,13},{5,12},{6,15},{7,14},{8,1},{9,0},... | collective-permute-start | bytes 12296 | tf_op jit(solution)/shard_map/ppermute | solution.py:35
  29.8 1.6 %collective-permute-done.12 = f32[8,128]{1,0:T(8,128)S(1)} collective-permute-done((f32[8,128]{1,0:T(8,128)S(1)}, f32[8,128]{1,0:T(8,128)S(1)}, u32[]{:S(2)}, u32[]{:S(2)}) %collective-permute-start.12) | collective-permute-done | bytes 4128 | tf_op jit(solution)/shard_map/ppermute | solution.py:35
  31.4 0.6 %add.19 = f32[8,128]{1,0:T(8,128)} add(f32[8,128]{1,0:T(8,128)S(1)} %add_add_fusion, f32[8,128]{1,0:T(8,128)S(1)} %collective-permute-done.12) | non-fusion elementwise | flops 1024 | bytes 12288 | tf_op jit(solution)/shard_map/add | solution.py:248
  (2 shorter events, 0.0 us)
Async XLA Ops:
  0.0 4.4 %copy-start = (bf16[1,384,7168]{2,1,0:T(8,128)(2,1)S(1)}, bf16[1,384,7168]{2,1,0:T(8,128)(2,1)}, u32[]{:S(2)}) copy-start(bf16[1,384,7168]{2,1,0:T(8,128)(2,1)} %param.6) | copy-start | bytes 16515076
  0.0 3.5 %collective-permute-start = (bf16[2048,256]{1,0:T(8,128)(2,1)}, bf16[2048,256]{1,0:T(8,128)(2,1)S(1)}, u32[]{:S(2)}, u32[]{:S(2)}) collective-permute-start(bf16[2048,256]{1,0:T(8,128)(2,1)} %bitcast.10), channel_id=1, source_target_pairs={{0,1},{1,0},{2,3},{3,2},{4,5},{5,4},{6,7},{7,6},{8,9},{9,8},{10,11... | collective-permute-start | bytes 3145736 | tf_op jit(solution)/shard_map/ppermute | solution.py:35
  3.5 7.9 %collective-permute-start.4 = (bf16[7168,256]{1,0:T(8,128)(2,1)}, bf16[7168,256]{1,0:T(8,128)(2,1)S(1)}, u32[]{:S(2)}, u32[]{:S(2)}) collective-permute-start(bf16[7168,256]{1,0:T(8,128)(2,1)} %bitcast.8), channel_id=1, source_target_pairs={{0,1},{1,0},{2,3},{3,2},{4,5},{5,4},{6,7},{7,6},{8,9},{9,8},{10,11... | collective-permute-start | bytes 11010056 | tf_op jit(solution)/shard_map/ppermute | solution.py:35
  6.7 9.7 %collective-permute-start.1 = (s16[37,16,128]{2,1,0:T(8,128)(2,1)S(1)}, s16[37,16,128]{2,1,0:T(8,128)(2,1)S(1)}, u32[]{:S(2)}, u32[]{:S(2)}) collective-permute-start(s16[37,16,128]{2,1,0:T(8,128)(2,1)S(1)} %get-tuple-element.27), channel_id=1, source_target_pairs={{0,6},{2,4},{4,2},{6,0},{8,14},{10,12},{12,10},{14,8},{1,7},{3,5},... | collective-permute-start | bytes 454664 | tf_op jit(solution)/shard_map/ppermute | solution.py:35
  10.8 8.1 %collective-permute-start.2 = (s16[37,16,128]{2,1,0:T(8,128)(2,1)S(1)}, s16[37,16,128]{2,1,0:T(8,128)(2,1)S(1)}, u32[]{:S(2)}, u32[]{:S(2)}) collective-permute-start(s16[37,16,128]{2,1,0:T(8,128)(2,1)S(1)} %get-tuple-element.28), channel_id=1, source_target_pairs={{0,4},{2,6},{4,0},{6,2},{8,12},{10,14},{12,8},{14,10},{1,5},{3,7},... | collective-permute-start | bytes 454664 | tf_op jit(solution)/shard_map/ppermute | solution.py:35
  11.2 7.7 %copy-start.1 = (s32[4]{0:T(128)S(1)}, s32[4]{0:T(128)}, u32[]{:S(2)}) copy-start(s32[4]{0:T(128)} %lengths.1) | copy-start | bytes 52
  11.2 7.7 %collective-permute-start.3 = (s16[37,16,128]{2,1,0:T(8,128)(2,1)S(1)}, s16[37,16,128]{2,1,0:T(8,128)(2,1)S(1)}, u32[]{:S(2)}, u32[]{:S(2)}) collective-permute-start(s16[37,16,128]{2,1,0:T(8,128)(2,1)S(1)} %get-tuple-element.29), channel_id=1, source_target_pairs={{0,2},{2,0},{4,6},{6,4},{8,10},{10,8},{12,14},{14,12},{1,3},{3,1},... | collective-permute-start | bytes 454664 | tf_op jit(solution)/shard_map/ppermute | solution.py:35
  13.1 6.7 %collective-permute-start.5 = (s16[13,16,128]{2,1,0:T(8,128)(2,1)S(1)}, s16[13,16,128]{2,1,0:T(8,128)(2,1)S(1)}, u32[]{:S(2)}, u32[]{:S(2)}) collective-permute-start(s16[13,16,128]{2,1,0:T(8,128)(2,1)S(1)} %get-tuple-element.34), channel_id=1, source_target_pairs={{0,6},{2,4},{4,2},{6,0},{8,14},{10,12},{12,10},{14,8},{1,7},{3,5},... | collective-permute-start | bytes 159752 | tf_op jit(solution)/shard_map/ppermute | solution.py:35
  16.0 4.4 %collective-permute-start.6 = (s16[13,16,128]{2,1,0:T(8,128)(2,1)S(1)}, s16[13,16,128]{2,1,0:T(8,128)(2,1)S(1)}, u32[]{:S(2)}, u32[]{:S(2)}) collective-permute-start(s16[13,16,128]{2,1,0:T(8,128)(2,1)S(1)} %get-tuple-element.35), channel_id=1, source_target_pairs={{0,4},{2,6},{4,0},{6,2},{8,12},{10,14},{12,8},{14,10},{1,5},{3,7},... | collective-permute-start | bytes 159752 | tf_op jit(solution)/shard_map/ppermute | solution.py:35
  16.4 4.1 %collective-permute-start.7 = (s16[13,16,128]{2,1,0:T(8,128)(2,1)S(1)}, s16[13,16,128]{2,1,0:T(8,128)(2,1)S(1)}, u32[]{:S(2)}, u32[]{:S(2)}) collective-permute-start(s16[13,16,128]{2,1,0:T(8,128)(2,1)S(1)} %get-tuple-element.36), channel_id=1, source_target_pairs={{0,2},{2,0},{4,6},{6,4},{8,10},{10,8},{12,14},{14,12},{1,3},{3,1},... | collective-permute-start | bytes 159752 | tf_op jit(solution)/shard_map/ppermute | solution.py:35
  20.8 1.2 %collective-permute-start.8 = (f32[8,128]{1,0:T(8,128)S(1)}, f32[8,128]{1,0:T(8,128)S(1)}, u32[]{:S(2)}, u32[]{:S(2)}) collective-permute-start(f32[8,128]{1,0:T(8,128)S(1)} %other_scores.1), channel_id=1, source_target_pairs={{0,1},{1,0},{2,3},{3,2},{4,5},{5,4},{6,7},{7,6},{8,9},{9,8},{10,11... | collective-permute-start | bytes 12296 | tf_op jit(solution)/shard_map/ppermute | solution.py:35
  22.0 3.9 %collective-permute-start.11 = (f32[8,128]{1,0:T(8,128)S(1)}, f32[8,128]{1,0:T(8,128)S(1)}, u32[]{:S(2)}, u32[]{:S(2)}) collective-permute-start(f32[8,128]{1,0:T(8,128)S(1)} %add.15), channel_id=1, source_target_pairs={{0,7},{1,6},{2,5},{3,4},{4,3},{5,2},{6,1},{7,0},{8,15},{9,14},{10,... | collective-permute-start | bytes 12296 | tf_op jit(solution)/shard_map/ppermute | solution.py:35
  24.0 3.0 %collective-permute-start.10 = (f32[8,128]{1,0:T(8,128)S(1)}, f32[8,128]{1,0:T(8,128)S(1)}, u32[]{:S(2)}, u32[]{:S(2)}) collective-permute-start(f32[8,128]{1,0:T(8,128)S(1)} %add.15), channel_id=1, source_target_pairs={{0,5},{1,4},{2,7},{3,6},{4,1},{5,0},{6,3},{7,2},{8,13},{9,12},{10,... | collective-permute-start | bytes 12296 | tf_op jit(solution)/shard_map/ppermute | solution.py:35
  24.4 3.0 %collective-permute-start.9 = (f32[8,128]{1,0:T(8,128)S(1)}, f32[8,128]{1,0:T(8,128)S(1)}, u32[]{:S(2)}, u32[]{:S(2)}) collective-permute-start(f32[8,128]{1,0:T(8,128)S(1)} %add.15), channel_id=1, source_target_pairs={{0,3},{1,2},{2,1},{3,0},{4,7},{5,6},{6,5},{7,4},{8,11},{9,10},{10,... | collective-permute-start | bytes 12296 | tf_op jit(solution)/shard_map/ppermute | solution.py:35
  27.5 3.9 %collective-permute-start.12 = (f32[8,128]{1,0:T(8,128)S(1)}, f32[8,128]{1,0:T(8,128)S(1)}, u32[]{:S(2)}, u32[]{:S(2)}) collective-permute-start(f32[8,128]{1,0:T(8,128)S(1)} %add_add_fusion), channel_id=1, source_target_pairs={{0,9},{1,8},{2,11},{3,10},{4,13},{5,12},{6,15},{7,14},{8,1},{9,0},... | collective-permute-start | bytes 12296 | tf_op jit(solution)/shard_map/ppermute | solution.py:35

commit v9 on v1

v9 whole, which is shorter than its diff:
```python
import functools

import jax
import jax.numpy as jnp
from jax import lax
from jax.experimental import pallas as pl
from jax.experimental.pallas import tpu as pltpu
from jax.sharding import PartitionSpec as P

RANK = 32
QUARTERS = 4
LANES = 128
SUBLANES = 16
TOP = 32000.0
STEPS = 256.0
FLOOR = 2.0**-112
MIB = 2**20
ACT_OWN_MIB = 50

IN_VMEM = pl.BlockSpec(memory_space=pltpu.VMEM)
IN_HBM = pl.BlockSpec(memory_space=pltpu.HBM)
IN_SMEM = pl.BlockSpec(memory_space=pltpu.SMEM)


def in_vmem(value):
    return pltpu.with_memory_space_constraint(value, pltpu.VMEM)


def in_hbm(value):
    return pltpu.with_memory_space_constraint(value, pltpu.HBM)


def from_partner(value, axis, mask):
    pairs = [(source, source ^ mask) for source in range(lax.axis_size(axis))]
    return lax.ppermute(value, axis, pairs)


def dot(rows, factor):
    return jnp.dot(rows, factor, preferred_element_type=jnp.float32)


def blocks(rows, width):
    return [
        (lane * (rows // SUBLANES) + row, row * SUBLANES, lane * LANES)
        for lane in range(width // LANES)
        for row in range(rows // SUBLANES)
    ]


def blocks(rows, width):
    return [
        (lane * (rows // SUBLANES) + row, row * SUBLANES, lane * LANES)
        for lane in range(width // LANES)
        for row in range(rows // SUBLANES)
    ]


def encode(total, out, codes):
    count, rows, width = total.shape
    tiles, lines = (rows // SUBLANES) * (width // LANES), width // LANES
    codes[...] = jnp.zeros_like(codes)
    for index in range(count):
        part = total[index]
        peak = jnp.max(jnp.abs(part), axis=0, keepdims=True)
        code = jnp.ceil(jnp.log2(jnp.maximum(peak, FLOOR)) * STEPS) + 1.0
        fixed = jnp.round(part * (TOP * jnp.exp2(code * (-1.0 / STEPS))))
        fixed = fixed.astype(jnp.int32).astype(jnp.int16)
        for tile, row, lane in blocks(rows, width):
            out[index * tiles + tile] = fixed[row:row + SUBLANES, lane:lane + LANES]
        for line in range(lines):
            at = index * lines + line
            codes[at:at + 1, :] = code[:, line * LANES:(line + 1) * LANES]
    out[count * tiles] = codes[...].astype(jnp.int32).astype(jnp.int16)


def add(total, message, out):
    count, rows, width = total.shape
    tiles, lines = (rows // SUBLANES) * (width // LANES), width // LANES
    codes = message[count * tiles].astype(jnp.int32).astype(jnp.float32)
    scale = jnp.exp2(codes * (1.0 / STEPS)) * (1.0 / TOP)
    for index in range(count):
        for tile, row, lane in blocks(rows, width):
            here = (index, slice(row, row + SUBLANES), slice(lane, lane + LANES))
            line = index * lines + lane // LANES
            fixed = message[index * tiles + tile].astype(jnp.int32).astype(jnp.float32)
            out[here] = total[here] + fixed * scale[line:line + 1, :]


def keep(part, total):
    rows = total.shape[1]
    for index in range(total.shape[0]):
        total[index] = part[index * rows:(index + 1) * rows]


def act_own_kernel(acts, factor, grad_factor, total, out, rows_held, grad_factor_held, factor_held, codes, sems):
    copies = (
        pltpu.make_async_copy(factor, factor_held, sems.at[0]),
        pltpu.make_async_copy(acts, rows_held, sems.at[1]),
        pltpu.make_async_copy(grad_factor, grad_factor_held, sems.at[2]),
    )
    for copy in copies:
        copy.start()
    copies[0].wait()
    copies[1].wait()
    keep(dot(rows_held[...], factor_held[...]), total)
    encode(total, out, codes)
    copies[2].wait()


def act_other_kernel(rows_held, factor, total, out, codes):
    keep(dot(rows_held[...], factor[...]), total)
    encode(total, out, codes)


def pair_kernel(total, message, *refs):
    pair_total, out, codes = refs[-3:]
    add(total, message, pair_total)
    encode(pair_total, out, codes)


def grad_kernel(lengths, grads, factor, total):
    keep(dot(grads[...], factor[...]), total)
    offsets = lax.broadcasted_iota(jnp.int32, total.shape[1:], 0)
    for seq in range(total.shape[0]):
        total[seq] = jnp.where(offsets < lengths[seq], total[seq], 0.0)


def score_kernel(is_own, act_total, message, grad_total, before, out, act):
    add(act_total, message, act)
    position = lax.axis_index("loop")
    holder = position if is_own else 1 - position
    count, rows, width = act.shape
    column = lax.broadcasted_iota(jnp.int32, (width, LANES), 0)
    lane = lax.broadcasted_iota(jnp.int32, (width, LANES), 1)
    pick = (lane == column // RANK + holder * (width // RANK)).astype(jnp.float32).astype(jnp.bfloat16)
    line = lax.broadcasted_iota(jnp.int32, (8, LANES), 0)
    term = lax.broadcasted_iota(jnp.int32, (8, width), 0)
    for first in range(0, out.shape[0], 8):
        result = jnp.zeros((8, LANES), jnp.float32) if is_own else before[first:first + 8, :]
        high = middle = low = jnp.zeros((8, width), jnp.float32)
        for seq in range(count):
            sums = jnp.sum(act[seq] * grad_total[seq], axis=0, keepdims=True)
            here = term == position * count + seq - first
            high_part = sums.astype(jnp.bfloat16).astype(jnp.float32)
            middle_part = (sums - high_part).astype(jnp.bfloat16).astype(jnp.float32)
            high = jnp.where(here, high_part, high)
            middle = jnp.where(here, middle_part, middle)
            low = jnp.where(here, sums - high_part - middle_part, low)
        terms = jnp.concatenate([high, middle, low], axis=0).astype(jnp.bfloat16)
        scores = dot(terms, pick)
        out[first:first + 8, :] = result + scores[:8] + scores[8:16] + scores[16:]


def on_device(acts, grads, act_factors, grad_factors, lengths):
    both = ("layer", "loop")
    loop_count = lax.axis_size("loop")
    layer_count = lax.axis_size("layer")
    acts, grads, act_factors, grad_factors = acts[0], grads[0], act_factors[0], grad_factors[0]
    seq_dev = lengths.shape[0]
    tok_rows, width = acts.shape[0], act_factors.shape[1]
    pad_rows = tok_rows // seq_dev
    queries = width * loop_count // RANK

    depth = grads.shape[1]

    def kernel(body, name, outs, specs, scratch, mib, work):
        return pl.pallas_call(
            body,
            name=name,
            out_shape=tuple(outs),
            in_specs=specs,
            out_specs=(IN_VMEM,) * len(outs),
            scratch_shapes=scratch,
            compiler_params=pltpu.CompilerParams(vmem_limit_bytes=mib * MIB),
            cost_estimate=pl.CostEstimate(
                flops=2 * tok_rows * width * work, bytes_accessed=mib * MIB, transcendentals=0
            ),
        )

    seqs_shape = pltpu.VMEM((seq_dev, pad_rows, width), jnp.float32)
    codes_shape = pltpu.VMEM((SUBLANES, LANES), jnp.float32)
    score_shape = pltpu.VMEM((seq_dev * loop_count, LANES), jnp.float32)
    tiles = (tok_rows // SUBLANES) * (width // LANES) + 1
    message_shape = pltpu.VMEM((tiles, SUBLANES, LANES), jnp.int16)

    def to_pair(out, step):
        pairs = [
            (source * loop_count + core, (source ^ (1 << (core ^ step))) * loop_count + core)
            for source in range(layer_count)
            for core in range(loop_count)
        ]
        return in_vmem(lax.ppermute(out, both, pairs))

    other_act = from_partner(act_factors, "loop", 1)
    own_total, own_out, act_held, factor_held = kernel(
        act_own_kernel, "act_own_columns",
        (
            seqs_shape, message_shape, pltpu.VMEM(acts.shape, acts.dtype),
            pltpu.VMEM(grad_factors.shape, grad_factors.dtype),
        ),
        [IN_HBM] * 3,
        [pltpu.VMEM(act_factors.shape, act_factors.dtype), codes_shape, pltpu.SemaphoreType.DMA((3,))],
        ACT_OWN_MIB, acts.shape[1],
    )(in_hbm(acts), in_hbm(act_factors), in_hbm(grad_factors))
    own_in = to_pair(own_out, 0)
    later_factors, other_act, own_total = lax.optimization_barrier((grad_factors, other_act, own_total))
    other_grad = from_partner(later_factors, "loop", 1)
    other_total, other_out = kernel(
        act_other_kernel, "act_other_columns", (seqs_shape, message_shape), [IN_VMEM] * 2, [codes_shape],
        8, acts.shape[1],
    )(in_vmem(act_held), in_vmem(other_act))
    other_in = to_pair(other_out, 0)
    (grad_own,) = kernel(
        grad_kernel, "grad_own_columns", (seqs_shape,), [IN_SMEM] + [IN_VMEM] * 2, [], 8, depth,
    )(lengths, in_vmem(grads), in_vmem(factor_held))
    own_pair, own_out = kernel(
        pair_kernel, "own_pair", (seqs_shape, message_shape), [IN_VMEM] * 3, [codes_shape], 8, 0,
    )(in_vmem(own_total), own_in, in_vmem(grad_own))
    own_in = to_pair(own_out, 1)
    other_pair, other_out = kernel(
        pair_kernel, "other_pair", (seqs_shape, message_shape), [IN_VMEM] * 2, [codes_shape], 8, 0,
    )(in_vmem(other_total), other_in)
    other_in = to_pair(other_out, 1)
    (grad_other,) = kernel(
        grad_kernel, "grad_other_columns", (seqs_shape,), [IN_SMEM] + [IN_VMEM] * 2, [], 8, depth,
    )(lengths, in_vmem(grads), in_vmem(other_grad))
    (own_scores,) = kernel(
        functools.partial(score_kernel, True), "own_scores", (score_shape,), [IN_VMEM] * 4, [seqs_shape], 8, 0,
    )(in_vmem(own_pair), own_in, in_vmem(grad_own), in_vmem(grad_other))
    (total,) = kernel(
        functools.partial(score_kernel, False), "other_scores", (score_shape,), [IN_VMEM] * 4, [seqs_shape], 8, 0,
    )(in_vmem(other_pair), other_in, in_vmem(grad_other), in_vmem(own_scores))

    total = total + from_partner(total, "loop", 1)
    gathered = [from_partner(total, both, mask * loop_count + 1) for mask in range(1, QUARTERS)]
    total = total + gathered[0] + gathered[1] + gathered[2]
    mask = QUARTERS
    while mask < layer_count:
        total = total + from_partner(total, both, mask * loop_count + 1)
        mask *= 2
    return total[:, :queries]


def solution(mesh):
    in_specs = (
        P("layer", ("groups", "loop"), None),
        P("layer", ("groups", "loop"), None),
        P("layer", None, "loop"),
        P("layer", None, "loop"),
        P(("groups", "loop")),
    )
    out_specs = P("groups", None)
    return jax.shard_map(
        on_device, mesh=mesh, in_specs=in_specs, out_specs=out_specs, check_vma=False
    )
```

time: 52.1 us -> 30.7 us (0.59)
  matrix products: 15.5 us -> 0 us
  Pallas kernels: 0 us -> 8.65 us
  waiting for transfers between devices: 13.2 us -> 8.63 us
  local copies, waits for them, and re-layouts: 4.23 us -> 0.01 us
  other arithmetic: 3.87 us -> 0.6 us
  starting transfers between devices: 14.8 us -> 12.6 us
    dot_general x4 -> x0, matrix products: 15.5 us -> none  [project(): return jnp.dot(rows, factor, preferred_element_type=jnp.float32)]
    ppermute x13 -> x7, starting transfers between devices: 14.8 us -> 5.94 us  [from_partner(): return lax.ppermute(value, axis, pairs)]
    pallas_call x0 -> x8, Pallas kernels: none -> 8.65 us  [the longest x1 3 us: on_device(): kernel(act_own_kernel, 'act_own_columns', (seqs_shape, message_shape, plt...]
    ppermute x13 -> x7, waiting for transfers between devices: 13.2 us -> 5.18 us  [from_partner(): return lax.ppermute(value, axis, pairs)]
    ppermute x0 -> x4, starting transfers between devices: none -> 6.66 us  [to_pair(): return in_vmem(lax.ppermute(out, both, pairs))]
    ppermute x0 -> x4, waiting for transfers between devices: none -> 3.45 us  [to_pair(): return in_vmem(lax.ppermute(out, both, pairs))]
    concatenate x2 -> x0, local copies, waits for them, and re-layouts: 1.66 us -> none  [the longest x1 1.39 us: on_device(): jnp.concatenate([project(acts[0], other_act), project(grads[0], other_gra...]
    add x3 -> x2, other arithmetic: 1.74 us -> 0.6 us  [the longest x1 0.6 us: on_device(): total = total + from_partner(total, both, mask * loop_count + 1)]
  transfers between devices with their start and end apart: 13 -> 11, of which waited for: 8 -> 8; matrix products, arithmetic and copies ran while one was open for 41% -> 0% of each run, Pallas kernels for 0% -> 27%
where the time goes in v9:
time: 30.7 us; the launch traced here: 30.6 us
  starting transfers between devices  12.6 us (41%)
  Pallas kernels  8.65 us (28%)
  waiting for transfers between devices  8.63 us (28%)
  other arithmetic  0.6 us (2%)
    ppermute x4, starting transfers between devices, to_pair(): return in_vmem(lax.ppermute(out, both, pairs))  6.66 us
    ppermute x7, starting transfers between devices, from_partner(): return lax.ppermute(value, axis, pairs)  5.94 us
    ppermute x7, waiting for transfers between devices, from_partner(): return lax.ppermute(value, axis, pairs)  5.18 us
    ppermute x4, waiting for transfers between devices, to_pair(): return in_vmem(lax.ppermute(out, both, pairs))  3.45 us
    pallas_call x1, Pallas kernels, on_device(): kernel(act_own_kernel, 'act_own_columns', (seqs_shape, message_shape, plt...  3 us
    pallas_call x1, Pallas kernels, on_device(): kernel(grad_kernel, 'grad_own_columns', (seqs_shape,), [IN_SMEM] + [IN_VM...  2.14 us
    pallas_call x1, Pallas kernels, on_device(): kernel(grad_kernel, 'grad_other_columns', (seqs_shape,), [IN_SMEM] + [IN_...  2.12 us
    pallas_call x1, Pallas kernels, on_device(): kernel(act_other_kernel, 'act_other_columns', (seqs_shape, message_shape)...  0.62 us
  transfers between devices with their start and end apart: 11, of which 8 were waited for; matrix products, arithmetic and copies ran while one was open for 0% of the time, Pallas kernels for 27%

profile of v9, /device:TPU:0, one launch (start us, length us, event | category | flops | bytes accessed | tf_op | source)
XLA Modules:
  0.0 30.6 jit_solution(4158947420276121605)
XLA Ops:
  0.0 0.5 %collective-permute-start = (bf16[2048,256]{1,0:T(8,128)(2,1)}, bf16[2048,256]{1,0:T(8,128)(2,1)S(1)}, u32[]{:S(2)}, u32[]{:S(2)}) collective-permute-start(bf16[2048,256]{1,0:T(8,128)(2,1)} %bitcast.10), channel_id=1, source_target_pairs={{0,1},{1,0},{2,3},{3,2},{4,5},{5,4},{6,7},{7,6},{8,9},{9,8},{10,11... | collective-permute-start | bytes 3145736 | tf_op jit(solution)/shard_map/ppermute | solution.py:35
  0.5 0.0 copy-start
  0.5 0.0 copy-start.1
  0.5 3.0 %act_own_columns.1 = (f32[4,96,256]{2,1,0:T(8,128)S(1)}, s16[49,16,128]{2,1,0:T(8,128)(2,1)S(1)}, bf16[384,2048]{1,0:T(8,128)(2,1)S(1)}, bf16[7168,256]{1,0:T(8,128)(2,1)S(1)}) custom-call(bf16[384,2048]{1,0:T(8,128)(2,1)} %bitcast.9, bf16[2048,256]{1,0:T(8,128)(2,1)} %bitcast.11, bf16[7168,256]{1,0:T(8,128)(2,1)} %bitcast.7), custom_call_target="tpu_custom_call" | custom-call | flops 402653184 | bytes 52428800 | tf_op jit(solution)/shard_map/act_own_columns/pallas_call | solution.py:195
  3.5 0.0 collective-permute-done.factor
  3.5 0.1 collective-permute-start.3
  3.6 3.0 %collective-permute-start.4 = (s16[49,16,128]{2,1,0:T(8,128)(2,1)S(1)}, s16[49,16,128]{2,1,0:T(8,128)(2,1)S(1)}, u32[]{:S(2)}, u32[]{:S(2)}) collective-permute-start(s16[49,16,128]{2,1,0:T(8,128)(2,1)S(1)} %get-tuple-element.27), channel_id=1, source_target_pairs={{0,2},{1,5},{2,0},{3,7},{4,6},{5,1},{6,4},{7,3},{8,10},{9,13},{10,... | collective-permute-start | bytes 602120 | tf_op jit(solution)/shard_map/ppermute | solution.py:192
  6.6 0.6 %act_other_columns.1 = (f32[4,96,256]{2,1,0:T(8,128)S(1)}, s16[49,16,128]{2,1,0:T(8,128)(2,1)S(1)}) custom-call(bf16[384,2048]{1,0:T(8,128)(2,1)S(1)} %get-tuple-element.18.rows_held, bf16[2048,256]{1,0:T(8,128)(2,1)S(1)} %collective-permute-done.factor), custom_call_target="tpu_custom_call" | custom-call | flops 402653184 | bytes 8388608 | tf_op jit(solution)/shard_map/act_other_columns/pallas_call | solution.py:208
  7.2 0.1 collective-permute-start.1
  7.3 0.0 copy-done
  7.3 0.0 copy-done.1
  7.3 2.1 %grad_own_columns.1.refs_0_.grad_total = f32[4,96,256]{2,1,0:T(8,128)S(1)} custom-call(s32[4]{0:T(128)S(1)} %copy-done.1, bf16[384,7168]{1,0:T(8,128)(2,1)S(1)} %bitcast.5, bf16[7168,256]{1,0:T(8,128)(2,1)S(1)} %get-tuple-element.28.factor), custom_call_target="tpu_custom_call" | custom-call | flops 1409286144 | bytes 8388608 | tf_op jit(solution)/shard_map/grad_own_columns/pallas_call | solution.py:213
  9.4 0.8 %collective-permute-done.4.message = s16[49,16,128]{2,1,0:T(8,128)(2,1)S(1)} collective-permute-done((s16[49,16,128]{2,1,0:T(8,128)(2,1)S(1)}, s16[49,16,128]{2,1,0:T(8,128)(2,1)S(1)}, u32[]{:S(2)}, u32[]{:S(2)}) %collective-permute-start.4) | collective-permute-done | bytes 200736 | tf_op jit(solution)/shard_map/ppermute | solution.py:192
  10.3 0.1 own_pair.1
  10.4 2.1 %collective-permute-start.5 = (s16[49,16,128]{2,1,0:T(8,128)(2,1)S(1)}, s16[49,16,128]{2,1,0:T(8,128)(2,1)S(1)}, u32[]{:S(2)}, u32[]{:S(2)}) collective-permute-start(s16[49,16,128]{2,1,0:T(8,128)(2,1)S(1)} %get-tuple-element.30), channel_id=1, source_target_pairs={{0,4},{1,3},{2,6},{3,1},{4,0},{5,7},{6,2},{7,5},{8,12},{9,11},{10,... | collective-permute-start | bytes 602120 | tf_op jit(solution)/shard_map/ppermute | solution.py:192
  12.5 0.7 %collective-permute-done.1.message = s16[49,16,128]{2,1,0:T(8,128)(2,1)S(1)} collective-permute-done((s16[49,16,128]{2,1,0:T(8,128)(2,1)S(1)}, s16[49,16,128]{2,1,0:T(8,128)(2,1)S(1)}, u32[]{:S(2)}, u32[]{:S(2)}) %collective-permute-start.1) | collective-permute-done | bytes 200736 | tf_op jit(solution)/shard_map/ppermute | solution.py:192
  13.3 0.1 other_pair.1
  13.4 1.5 %collective-permute-start.2 = (s16[49,16,128]{2,1,0:T(8,128)(2,1)S(1)}, s16[49,16,128]{2,1,0:T(8,128)(2,1)S(1)}, u32[]{:S(2)}, u32[]{:S(2)}) collective-permute-start(s16[49,16,128]{2,1,0:T(8,128)(2,1)S(1)} %get-tuple-element.24), channel_id=1, source_target_pairs={{0,4},{1,3},{2,6},{3,1},{4,0},{5,7},{6,2},{7,5},{8,12},{9,11},{10,... | collective-permute-start | bytes 602120 | tf_op jit(solution)/shard_map/ppermute | solution.py:192
  14.9 0.0 collective-permute-done.3.factor
  14.9 2.1 %grad_other_columns.1.before.grad_total = f32[4,96,256]{2,1,0:T(8,128)S(1)} custom-call(s32[4]{0:T(128)S(1)} %copy-done.1, bf16[384,7168]{1,0:T(8,128)(2,1)S(1)} %bitcast.6, bf16[7168,256]{1,0:T(8,128)(2,1)S(1)} %collective-permute-done.3.factor), custom_call_target="tpu_custom_call" | custom-call | flops 1409286144 | bytes 8388608 | tf_op jit(solution)/shard_map/grad_other_columns/pallas_call | solution.py:224
  17.0 0.0 collective-permute-done.5.message
  17.0 0.2 own_scores.1.before
  17.3 1.9 %collective-permute-done.2.message = s16[49,16,128]{2,1,0:T(8,128)(2,1)S(1)} collective-permute-done((s16[49,16,128]{2,1,0:T(8,128)(2,1)S(1)}, s16[49,16,128]{2,1,0:T(8,128)(2,1)S(1)}, u32[]{:S(2)}, u32[]{:S(2)}) %collective-permute-start.2) | collective-permute-done | bytes 200736 | tf_op jit(solution)/shard_map/ppermute | solution.py:192
  19.2 0.2 other_scores.1
  19.4 0.0 collective-permute-start.6
  19.4 1.2 %collective-permute-done.6 = f32[8,128]{1,0:T(8,128)S(1)} collective-permute-done((f32[8,128]{1,0:T(8,128)S(1)}, f32[8,128]{1,0:T(8,128)S(1)}, u32[]{:S(2)}, u32[]{:S(2)}) %collective-permute-start.6) | collective-permute-done | bytes 4128 | tf_op jit(solution)/shard_map/ppermute | solution.py:35
  20.6 2.0 %collective-permute-start.9 = (f32[8,128]{1,0:T(8,128)S(1)}, f32[8,128]{1,0:T(8,128)S(1)}, u32[]{:S(2)}, u32[]{:S(2)}) collective-permute-start(f32[8,128]{1,0:T(8,128)S(1)} %add.15), channel_id=1, source_target_pairs={{0,7},{1,6},{2,5},{3,4},{4,3},{5,2},{6,1},{7,0},{8,15},{9,14},{10,... | collective-permute-start | bytes 12296 | tf_op jit(solution)/shard_map/ppermute | solution.py:35
  22.6 0.4 %collective-permute-start.8 = (f32[8,128]{1,0:T(8,128)S(1)}, f32[8,128]{1,0:T(8,128)S(1)}, u32[]{:S(2)}, u32[]{:S(2)}) collective-permute-start(f32[8,128]{1,0:T(8,128)S(1)} %add.15), channel_id=1, source_target_pairs={{0,5},{1,4},{2,7},{3,6},{4,1},{5,0},{6,3},{7,2},{8,13},{9,12},{10,... | collective-permute-start | bytes 12296 | tf_op jit(solution)/shard_map/ppermute | solution.py:35
  23.0 0.6 %collective-permute-start.7 = (f32[8,128]{1,0:T(8,128)S(1)}, f32[8,128]{1,0:T(8,128)S(1)}, u32[]{:S(2)}, u32[]{:S(2)}) collective-permute-start(f32[8,128]{1,0:T(8,128)S(1)} %add.15), channel_id=1, source_target_pairs={{0,3},{1,2},{2,1},{3,0},{4,7},{5,6},{6,5},{7,4},{8,11},{9,10},{10,... | collective-permute-start | bytes 12296 | tf_op jit(solution)/shard_map/ppermute | solution.py:35
  23.6 0.9 %collective-permute-done.9 = f32[8,128]{1,0:T(8,128)S(1)} collective-permute-done((f32[8,128]{1,0:T(8,128)S(1)}, f32[8,128]{1,0:T(8,128)S(1)}, u32[]{:S(2)}, u32[]{:S(2)}) %collective-permute-start.9) | collective-permute-done | bytes 4128 | tf_op jit(solution)/shard_map/ppermute | solution.py:35
  24.5 1.1 %collective-permute-done.8 = f32[8,128]{1,0:T(8,128)S(1)} collective-permute-done((f32[8,128]{1,0:T(8,128)S(1)}, f32[8,128]{1,0:T(8,128)S(1)}, u32[]{:S(2)}, u32[]{:S(2)}) %collective-permute-start.8) | collective-permute-done | bytes 4128 | tf_op jit(solution)/shard_map/ppermute | solution.py:35
  25.6 0.4 %collective-permute-done.7 = f32[8,128]{1,0:T(8,128)S(1)} collective-permute-done((f32[8,128]{1,0:T(8,128)S(1)}, f32[8,128]{1,0:T(8,128)S(1)}, u32[]{:S(2)}, u32[]{:S(2)}) %collective-permute-start.7) | collective-permute-done | bytes 4128 | tf_op jit(solution)/shard_map/ppermute | solution.py:35
  26.0 2.4 %collective-permute-start.10 = (f32[8,128]{1,0:T(8,128)S(1)}, f32[8,128]{1,0:T(8,128)S(1)}, u32[]{:S(2)}, u32[]{:S(2)}) collective-permute-start(f32[8,128]{1,0:T(8,128)S(1)} %add_add_fusion), channel_id=1, source_target_pairs={{0,9},{1,8},{2,11},{3,10},{4,13},{5,12},{6,15},{7,14},{8,1},{9,0},... | collective-permute-start | bytes 12296 | tf_op jit(solution)/shard_map/ppermute | solution.py:35
  28.4 1.6 %collective-permute-done.10 = f32[8,128]{1,0:T(8,128)S(1)} collective-permute-done((f32[8,128]{1,0:T(8,128)S(1)}, f32[8,128]{1,0:T(8,128)S(1)}, u32[]{:S(2)}, u32[]{:S(2)}) %collective-permute-start.10) | collective-permute-done | bytes 4128 | tf_op jit(solution)/shard_map/ppermute | solution.py:35
  30.0 0.6 %add.19 = f32[8,128]{1,0:T(8,128)} add(f32[8,128]{1,0:T(8,128)S(1)} %add_add_fusion, f32[8,128]{1,0:T(8,128)S(1)} %collective-permute-done.10) | non-fusion elementwise | flops 1024 | bytes 12288 | tf_op jit(solution)/shard_map/add | solution.py:239
  (2 shorter events, 0.0 us)
Async XLA Ops:
  0.0 3.5 %collective-permute-start = (bf16[2048,256]{1,0:T(8,128)(2,1)}, bf16[2048,256]{1,0:T(8,128)(2,1)S(1)}, u32[]{:S(2)}, u32[]{:S(2)}) collective-permute-start(bf16[2048,256]{1,0:T(8,128)(2,1)} %bitcast.10), channel_id=1, source_target_pairs={{0,1},{1,0},{2,3},{3,2},{4,5},{5,4},{6,7},{7,6},{8,9},{9,8},{10,11... | collective-permute-start | bytes 3145736 | tf_op jit(solution)/shard_map/ppermute | solution.py:35
  0.5 6.8 %copy-start = (bf16[1,384,7168]{2,1,0:T(8,128)(2,1)S(1)}, bf16[1,384,7168]{2,1,0:T(8,128)(2,1)}, u32[]{:S(2)}) copy-start(bf16[1,384,7168]{2,1,0:T(8,128)(2,1)} %param.6) | copy-start | bytes 16515076
  0.5 6.8 %copy-start.1 = (s32[4]{0:T(128)S(1)}, s32[4]{0:T(128)}, u32[]{:S(2)}) copy-start(s32[4]{0:T(128)} %lengths.3) | copy-start | bytes 52
  3.5 11.4 %collective-permute-start.3 = (bf16[7168,256]{1,0:T(8,128)(2,1)}, bf16[7168,256]{1,0:T(8,128)(2,1)S(1)}, u32[]{:S(2)}, u32[]{:S(2)}) collective-permute-start(bf16[7168,256]{1,0:T(8,128)(2,1)} %bitcast.8), channel_id=1, source_target_pairs={{0,1},{1,0},{2,3},{3,2},{4,5},{5,4},{6,7},{7,6},{8,9},{9,8},{10,11... | collective-permute-start | bytes 11010056 | tf_op jit(solution)/shard_map/ppermute | solution.py:35
  3.6 6.7 %collective-permute-start.4 = (s16[49,16,128]{2,1,0:T(8,128)(2,1)S(1)}, s16[49,16,128]{2,1,0:T(8,128)(2,1)S(1)}, u32[]{:S(2)}, u32[]{:S(2)}) collective-permute-start(s16[49,16,128]{2,1,0:T(8,128)(2,1)S(1)} %get-tuple-element.27), channel_id=1, source_target_pairs={{0,2},{1,5},{2,0},{3,7},{4,6},{5,1},{6,4},{7,3},{8,10},{9,13},{10,... | collective-permute-start | bytes 602120 | tf_op jit(solution)/shard_map/ppermute | solution.py:192
  7.2 6.1 %collective-permute-start.1 = (s16[49,16,128]{2,1,0:T(8,128)(2,1)S(1)}, s16[49,16,128]{2,1,0:T(8,128)(2,1)S(1)}, u32[]{:S(2)}, u32[]{:S(2)}) collective-permute-start(s16[49,16,128]{2,1,0:T(8,128)(2,1)S(1)} %get-tuple-element.22), channel_id=1, source_target_pairs={{0,2},{1,5},{2,0},{3,7},{4,6},{5,1},{6,4},{7,3},{8,10},{9,13},{10,... | collective-permute-start | bytes 602120 | tf_op jit(solution)/shard_map/ppermute | solution.py:192
  10.4 6.6 %collective-permute-start.5 = (s16[49,16,128]{2,1,0:T(8,128)(2,1)S(1)}, s16[49,16,128]{2,1,0:T(8,128)(2,1)S(1)}, u32[]{:S(2)}, u32[]{:S(2)}) collective-permute-start(s16[49,16,128]{2,1,0:T(8,128)(2,1)S(1)} %get-tuple-element.30), channel_id=1, source_target_pairs={{0,4},{1,3},{2,6},{3,1},{4,0},{5,7},{6,2},{7,5},{8,12},{9,11},{10,... | collective-permute-start | bytes 602120 | tf_op jit(solution)/shard_map/ppermute | solution.py:192
  13.4 5.8 %collective-permute-start.2 = (s16[49,16,128]{2,1,0:T(8,128)(2,1)S(1)}, s16[49,16,128]{2,1,0:T(8,128)(2,1)S(1)}, u32[]{:S(2)}, u32[]{:S(2)}) collective-permute-start(s16[49,16,128]{2,1,0:T(8,128)(2,1)S(1)} %get-tuple-element.24), channel_id=1, source_target_pairs={{0,4},{1,3},{2,6},{3,1},{4,0},{5,7},{6,2},{7,5},{8,12},{9,11},{10,... | collective-permute-start | bytes 602120 | tf_op jit(solution)/shard_map/ppermute | solution.py:192
  19.4 1.2 %collective-permute-start.6 = (f32[8,128]{1,0:T(8,128)S(1)}, f32[8,128]{1,0:T(8,128)S(1)}, u32[]{:S(2)}, u32[]{:S(2)}) collective-permute-start(f32[8,128]{1,0:T(8,128)S(1)} %other_scores.1), channel_id=1, source_target_pairs={{0,1},{1,0},{2,3},{3,2},{4,5},{5,4},{6,7},{7,6},{8,9},{9,8},{10,11... | collective-permute-start | bytes 12296 | tf_op jit(solution)/shard_map/ppermute | solution.py:35
  20.6 3.9 %collective-permute-start.9 = (f32[8,128]{1,0:T(8,128)S(1)}, f32[8,128]{1,0:T(8,128)S(1)}, u32[]{:S(2)}, u32[]{:S(2)}) collective-permute-start(f32[8,128]{1,0:T(8,128)S(1)} %add.15), channel_id=1, source_target_pairs={{0,7},{1,6},{2,5},{3,4},{4,3},{5,2},{6,1},{7,0},{8,15},{9,14},{10,... | collective-permute-start | bytes 12296 | tf_op jit(solution)/shard_map/ppermute | solution.py:35
  22.6 3.0 %collective-permute-start.8 = (f32[8,128]{1,0:T(8,128)S(1)}, f32[8,128]{1,0:T(8,128)S(1)}, u32[]{:S(2)}, u32[]{:S(2)}) collective-permute-start(f32[8,128]{1,0:T(8,128)S(1)} %add.15), channel_id=1, source_target_pairs={{0,5},{1,4},{2,7},{3,6},{4,1},{5,0},{6,3},{7,2},{8,13},{9,12},{10,... | collective-permute-start | bytes 12296 | tf_op jit(solution)/shard_map/ppermute | solution.py:35
  23.0 3.0 %collective-permute-start.7 = (f32[8,128]{1,0:T(8,128)S(1)}, f32[8,128]{1,0:T(8,128)S(1)}, u32[]{:S(2)}, u32[]{:S(2)}) collective-permute-start(f32[8,128]{1,0:T(8,128)S(1)} %add.15), channel_id=1, source_target_pairs={{0,3},{1,2},{2,1},{3,0},{4,7},{5,6},{6,5},{7,4},{8,11},{9,10},{10,... | collective-permute-start | bytes 12296 | tf_op jit(solution)/shard_map/ppermute | solution.py:35
  26.0 3.9 %collective-permute-start.10 = (f32[8,128]{1,0:T(8,128)S(1)}, f32[8,128]{1,0:T(8,128)S(1)}, u32[]{:S(2)}, u32[]{:S(2)}) collective-permute-start(f32[8,128]{1,0:T(8,128)S(1)} %add_add_fusion), channel_id=1, source_target_pairs={{0,9},{1,8},{2,11},{3,10},{4,13},{5,12},{6,15},{7,14},{8,1},{9,0},... | collective-permute-start | bytes 12296 | tf_op jit(solution)/shard_map/ppermute | solution.py:35

commit v10 on v9

--- a/solution.py
+++ b/solution.py
@@ -15,6 +15,7 @@
 STEPS = 256.0
 FLOOR = 2.0**-112
 MIB = 2**20
+GRAD_STEP = 1
 ACT_OWN_MIB = 50
 
 IN_VMEM = pl.BlockSpec(memory_space=pltpu.VMEM)
@@ -118,28 +119,33 @@
     encode(pair_total, out, codes)
 
 
-def grad_kernel(lengths, grads, factor, total):
+def grad_own_kernel(grads, factor, total, out, codes):
     keep(dot(grads[...], factor[...]), total)
+    encode(total, out, codes)
+
+
+def drop_padding(total, lengths):
     offsets = lax.broadcasted_iota(jnp.int32, total.shape[1:], 0)
     for seq in range(total.shape[0]):
         total[seq] = jnp.where(offsets < lengths[seq], total[seq], 0.0)
 
 
-def score_kernel(is_own, act_total, message, grad_total, before, out, act):
-    add(act_total, message, act)
+def grad_other_kernel(lengths, grads, factor, total):
+    keep(dot(grads[...], factor[...]), total)
+    drop_padding(total, lengths)
+
+
+def score(act, grad, holder, out, before):
     position = lax.axis_index("loop")
-    holder = position if is_own else 1 - position
     count, rows, width = act.shape
     column = lax.broadcasted_iota(jnp.int32, (width, LANES), 0)
     lane = lax.broadcasted_iota(jnp.int32, (width, LANES), 1)
     pick = (lane == column // RANK + holder * (width // RANK)).astype(jnp.float32).astype(jnp.bfloat16)
-    line = lax.broadcasted_iota(jnp.int32, (8, LANES), 0)
     term = lax.broadcasted_iota(jnp.int32, (8, width), 0)
     for first in range(0, out.shape[0], 8):
-        result = jnp.zeros((8, LANES), jnp.float32) if is_own else before[first:first + 8, :]
         high = middle = low = jnp.zeros((8, width), jnp.float32)
         for seq in range(count):
-            sums = jnp.sum(act[seq] * grad_total[seq], axis=0, keepdims=True)
+            sums = jnp.sum(act[seq] * grad[seq], axis=0, keepdims=True)
             here = term == position * count + seq - first
             high_part = sums.astype(jnp.bfloat16).astype(jnp.float32)
             middle_part = (sums - high_part).astype(jnp.bfloat16).astype(jnp.float32)
@@ -148,7 +154,20 @@
             low = jnp.where(here, sums - high_part - middle_part, low)
         terms = jnp.concatenate([high, middle, low], axis=0).astype(jnp.bfloat16)
         scores = dot(terms, pick)
-        out[first:first + 8, :] = result + scores[:8] + scores[8:16] + scores[16:]
+        scores = scores[:8] + scores[8:16] + scores[16:]
+        out[first:first + 8, :] = scores if before is None else before[first:first + 8, :] + scores
+
+
+def own_score_kernel(lengths, act_total, act_message, grad_total, grad_message, after, out, act, grad):
+    add(act_total, act_message, act)
+    add(grad_total, grad_message, grad)
+    drop_padding(act, lengths)
+    score(act, grad, lax.axis_index("loop"), out, None)
+
+
+def other_score_kernel(act_total, message, grad_total, before, out, act):
+    add(act_total, message, act)
+    score(act, grad_total, 1 - lax.axis_index("loop"), out, before)
 
 
 def on_device(acts, grads, act_factors, grad_factors, lengths):
@@ -202,7 +221,7 @@
         [pltpu.VMEM(act_factors.shape, act_factors.dtype), codes_shape, pltpu.SemaphoreType.DMA((3,))],
         ACT_OWN_MIB, acts.shape[1],
     )(in_hbm(acts), in_hbm(act_factors), in_hbm(grad_factors))
-    own_in = to_pair(own_out, 0)
+    own_in = to_pair(own_out, 1 - GRAD_STEP)
     later_factors, other_act, own_total = lax.optimization_barrier((grad_factors, other_act, own_total))
     other_grad = from_partner(later_factors, "loop", 1)
     other_total, other_out = kernel(
@@ -210,25 +229,22 @@
         8, acts.shape[1],
     )(in_vmem(act_held), in_vmem(other_act))
     other_in = to_pair(other_out, 0)
-    (grad_own,) = kernel(
-        grad_kernel, "grad_own_columns", (seqs_shape,), [IN_SMEM] + [IN_VMEM] * 2, [], 8, depth,
-    )(lengths, in_vmem(grads), in_vmem(factor_held))
-    own_pair, own_out = kernel(
-        pair_kernel, "own_pair", (seqs_shape, message_shape), [IN_VMEM] * 3, [codes_shape], 8, 0,
-    )(in_vmem(own_total), own_in, in_vmem(grad_own))
-    own_in = to_pair(own_out, 1)
+    grad_own, grad_out = kernel(
+        grad_own_kernel, "grad_own_columns", (seqs_shape, message_shape), [IN_VMEM] * 2, [codes_shape], 8, depth,
+    )(in_vmem(grads), in_vmem(factor_held))
+    grad_in = to_pair(grad_out, GRAD_STEP)
     other_pair, other_out = kernel(
-        pair_kernel, "other_pair", (seqs_shape, message_shape), [IN_VMEM] * 2, [codes_shape], 8, 0,
-    )(in_vmem(other_total), other_in)
+        pair_kernel, "other_pair", (seqs_shape, message_shape), [IN_VMEM] * 3, [codes_shape], 8, 0,
+    )(in_vmem(other_total), other_in, in_vmem(grad_own))
     other_in = to_pair(other_out, 1)
     (grad_other,) = kernel(
-        grad_kernel, "grad_other_columns", (seqs_shape,), [IN_SMEM] + [IN_VMEM] * 2, [], 8, depth,
+        grad_other_kernel, "grad_other_columns", (seqs_shape,), [IN_SMEM] + [IN_VMEM] * 2, [], 8, depth,
     )(lengths, in_vmem(grads), in_vmem(other_grad))
     (own_scores,) = kernel(
-        functools.partial(score_kernel, True), "own_scores", (score_shape,), [IN_VMEM] * 4, [seqs_shape], 8, 0,
-    )(in_vmem(own_pair), own_in, in_vmem(grad_own), in_vmem(grad_other))
+        own_score_kernel, "own_scores", (score_shape,), [IN_SMEM] + [IN_VMEM] * 5, [seqs_shape] * 2, 8, 0,
+    )(lengths, in_vmem(own_total), own_in, in_vmem(grad_own), grad_in, in_vmem(grad_other))
     (total,) = kernel(
-        functools.partial(score_kernel, False), "other_scores", (score_shape,), [IN_VMEM] * 4, [seqs_shape], 8, 0,
+        other_score_kernel, "other_scores", (score_shape,), [IN_VMEM] * 4, [seqs_shape], 8, 0,
     )(in_vmem(other_pair), other_in, in_vmem(grad_other), in_vmem(own_scores))
 
     total = total + from_partner(total, "loop", 1)

time: 30.7 us -> 29.2 us (0.951)
  waiting for transfers between devices: 8.63 us -> 5.96 us
  starting transfers between devices: 12.6 us -> 13.8 us
    ppermute x4, waiting for transfers between devices: 3.45 us -> 0.72 us  [to_pair(): return in_vmem(lax.ppermute(out, both, pairs))]
    ppermute x7, starting transfers between devices: 5.94 us -> 6.58 us  [from_partner(): return lax.ppermute(value, axis, pairs)]
    ppermute x4, starting transfers between devices: 6.66 us -> 7.22 us  [to_pair(): return in_vmem(lax.ppermute(out, both, pairs))]
    pallas_call x5 -> x4, Pallas kernels: 4.88 us -> 4.87 us  [the longest x1 2.12 us: on_device(): kernel(grad_other_kernel, 'grad_other_columns', (seqs_shape,), [IN_SMEM]...]
  transfers between devices with their start and end apart: 11 -> 11, of which waited for: 8 -> 6; matrix products, arithmetic and copies ran while one was open for 0% -> 0% of each run, Pallas kernels for 27% -> 29%
where the time goes in v10:
time: 29.2 us; the launch traced here: 29.1 us
  starting transfers between devices  13.8 us (47%)
  Pallas kernels  8.63 us (30%)
  waiting for transfers between devices  5.96 us (20%)
  other arithmetic  0.6 us (2%)
    ppermute x4, starting transfers between devices, to_pair(): return in_vmem(lax.ppermute(out, both, pairs))  7.22 us
    ppermute x7, starting transfers between devices, from_partner(): return lax.ppermute(value, axis, pairs)  6.58 us
    ppermute x7, waiting for transfers between devices, from_partner(): return lax.ppermute(value, axis, pairs)  5.24 us
    pallas_call x1, Pallas kernels, on_device(): kernel(act_own_kernel, 'act_own_columns', (seqs_shape, message_shape, plt...  3 us
    pallas_call x1, Pallas kernels, on_device(): kernel(grad_other_kernel, 'grad_other_columns', (seqs_shape,), [IN_SMEM]...  2.12 us
    pallas_call x1, Pallas kernels, on_device(): kernel(grad_own_kernel, 'grad_own_columns', (seqs_shape, message_shape),...  1.63 us
    pallas_call x1, Pallas kernels, on_device(): kernel(own_score_kernel, 'own_scores', (score_shape,), [IN_SMEM] + [IN_VM...  0.87 us
    ppermute x4, waiting for transfers between devices, to_pair(): return in_vmem(lax.ppermute(out, both, pairs))  0.72 us
  transfers between devices with their start and end apart: 11, of which 6 were waited for; matrix products, arithmetic and copies ran while one was open for 0% of the time, Pallas kernels for 29%

profile of v10, /device:TPU:0, one launch (start us, length us, event | category | flops | bytes accessed | tf_op | source)
XLA Modules:
  0.0 29.1 jit_solution(10544997074448498283)
XLA Ops:
  0.0 0.5 %collective-permute-start = (bf16[2048,256]{1,0:T(8,128)(2,1)}, bf16[2048,256]{1,0:T(8,128)(2,1)S(1)}, u32[]{:S(2)}, u32[]{:S(2)}) collective-permute-start(bf16[2048,256]{1,0:T(8,128)(2,1)} %bitcast.10), channel_id=1, source_target_pairs={{0,1},{1,0},{2,3},{3,2},{4,5},{5,4},{6,7},{7,6},{8,9},{9,8},{10,11... | collective-permute-start | bytes 3145736 | tf_op jit(solution)/shard_map/ppermute | solution.py:36
  0.5 0.0 copy-start
  0.5 3.0 %act_own_columns.1 = (f32[4,96,256]{2,1,0:T(8,128)S(1)}, s16[49,16,128]{2,1,0:T(8,128)(2,1)S(1)}, bf16[384,2048]{1,0:T(8,128)(2,1)S(1)}, bf16[7168,256]{1,0:T(8,128)(2,1)S(1)}) custom-call(bf16[384,2048]{1,0:T(8,128)(2,1)} %bitcast.9, bf16[2048,256]{1,0:T(8,128)(2,1)} %bitcast.11, bf16[7168,256]{1,0:T(8,128)(2,1)} %bitcast.7), custom_call_target="tpu_custom_call" | custom-call | flops 402653184 | bytes 52428800 | tf_op jit(solution)/shard_map/act_own_columns/pallas_call | solution.py:214
  3.5 0.0 collective-permute-done.factor
  3.5 0.1 collective-permute-start.3
  3.6 0.6 %act_other_columns.1 = (f32[4,96,256]{2,1,0:T(8,128)S(1)}, s16[49,16,128]{2,1,0:T(8,128)(2,1)S(1)}) custom-call(bf16[384,2048]{1,0:T(8,128)(2,1)S(1)} %get-tuple-element.18.rows_held, bf16[2048,256]{1,0:T(8,128)(2,1)S(1)} %collective-permute-done.factor), custom_call_target="tpu_custom_call" | custom-call | flops 402653184 | bytes 8388608 | tf_op jit(solution)/shard_map/act_other_columns/pallas_call | solution.py:227
  4.2 3.0 %collective-permute-start.1 = (s16[49,16,128]{2,1,0:T(8,128)(2,1)S(1)}, s16[49,16,128]{2,1,0:T(8,128)(2,1)S(1)}, u32[]{:S(2)}, u32[]{:S(2)}) collective-permute-start(s16[49,16,128]{2,1,0:T(8,128)(2,1)S(1)} %get-tuple-element.22), channel_id=1, source_target_pairs={{0,2},{1,5},{2,0},{3,7},{4,6},{5,1},{6,4},{7,3},{8,10},{9,13},{10,... | collective-permute-start | bytes 602120 | tf_op jit(solution)/shard_map/ppermute | solution.py:211
  7.3 0.1 collective-permute-start.4
  7.3 0.0 copy-done
  7.3 0.0 copy-start.1
  7.3 1.6 %grad_own_columns.1 = (f32[4,96,256]{2,1,0:T(8,128)S(1)}, s16[49,16,128]{2,1,0:T(8,128)(2,1)S(1)}) custom-call(bf16[384,7168]{1,0:T(8,128)(2,1)S(1)} %bitcast.5, bf16[7168,256]{1,0:T(8,128)(2,1)S(1)} %get-tuple-element.23.factor), custom_call_target="tpu_custom_call" | custom-call | flops 1409286144 | bytes 8388608 | tf_op jit(solution)/shard_map/grad_own_columns/pallas_call | solution.py:232
  9.0 2.1 %collective-permute-start.5 = (s16[49,16,128]{2,1,0:T(8,128)(2,1)S(1)}, s16[49,16,128]{2,1,0:T(8,128)(2,1)S(1)}, u32[]{:S(2)}, u32[]{:S(2)}) collective-permute-start(s16[49,16,128]{2,1,0:T(8,128)(2,1)S(1)} %get-tuple-element.30), channel_id=1, source_target_pairs={{0,4},{1,3},{2,6},{3,1},{4,0},{5,7},{6,2},{7,5},{8,12},{9,11},{10,... | collective-permute-start | bytes 602120 | tf_op jit(solution)/shard_map/ppermute | solution.py:211
  11.1 0.0 collective-permute-done.1.message
  11.1 0.1 other_pair.1
  11.2 2.0 %collective-permute-start.2 = (s16[49,16,128]{2,1,0:T(8,128)(2,1)S(1)}, s16[49,16,128]{2,1,0:T(8,128)(2,1)S(1)}, u32[]{:S(2)}, u32[]{:S(2)}) collective-permute-start(s16[49,16,128]{2,1,0:T(8,128)(2,1)S(1)} %get-tuple-element.26), channel_id=1, source_target_pairs={{0,4},{1,3},{2,6},{3,1},{4,0},{5,7},{6,2},{7,5},{8,12},{9,11},{10,... | collective-permute-start | bytes 602120 | tf_op jit(solution)/shard_map/ppermute | solution.py:211
  13.2 0.0 collective-permute-done.3.factor
  13.2 0.0 copy-done.1
  13.2 2.1 %grad_other_columns.1.after.grad_total = f32[4,96,256]{2,1,0:T(8,128)S(1)} custom-call(s32[4]{0:T(128)S(1)} %copy-done.1, bf16[384,7168]{1,0:T(8,128)(2,1)S(1)} %bitcast.6, bf16[7168,256]{1,0:T(8,128)(2,1)S(1)} %collective-permute-done.3.factor), custom_call_target="tpu_custom_call" | custom-call | flops 1409286144 | bytes 8388608 | tf_op jit(solution)/shard_map/grad_other_columns/pallas_call | solution.py:240
  15.4 0.0 collective-permute-done.4.act_message
  15.4 0.0 collective-permute-done.5.grad_message
  15.4 0.9 %own_scores.1.before = f32[8,128]{1,0:T(8,128)S(1)} custom-call(s32[4]{0:T(128)S(1)} %copy-done.1, f32[4,96,256]{2,1,0:T(8,128)S(1)} %get-tuple-element.28.act_total, s16[49,16,128]{2,1,0:T(8,128)(2,1)S(1)} %collective-permute-done.4.act_message, f32[4,96,256]{2,1,0:T(8,128)S(1)} %get-tuple-element.24.refs_0_.grad_total, ...), custom_call_target="tpu_custom_call" | custom-call | bytes 8388608 | tf_op jit(solution)/shard_map/own_scores/pallas_call | solution.py:243
  16.3 0.7 %collective-permute-done.2.message = s16[49,16,128]{2,1,0:T(8,128)(2,1)S(1)} collective-permute-done((s16[49,16,128]{2,1,0:T(8,128)(2,1)S(1)}, s16[49,16,128]{2,1,0:T(8,128)(2,1)S(1)}, u32[]{:S(2)}, u32[]{:S(2)}) %collective-permute-start.2) | collective-permute-done | bytes 200736 | tf_op jit(solution)/shard_map/ppermute | solution.py:211
  17.0 0.2 other_scores.1
  17.2 0.2 collective-permute-start.6
  17.5 0.9 %collective-permute-done.6 = f32[8,128]{1,0:T(8,128)S(1)} collective-permute-done((f32[8,128]{1,0:T(8,128)S(1)}, f32[8,128]{1,0:T(8,128)S(1)}, u32[]{:S(2)}, u32[]{:S(2)}) %collective-permute-start.6) | collective-permute-done | bytes 4128 | tf_op jit(solution)/shard_map/ppermute | solution.py:36
  18.4 2.9 %collective-permute-start.9 = (f32[8,128]{1,0:T(8,128)S(1)}, f32[8,128]{1,0:T(8,128)S(1)}, u32[]{:S(2)}, u32[]{:S(2)}) collective-permute-start(f32[8,128]{1,0:T(8,128)S(1)} %add.15), channel_id=1, source_target_pairs={{0,7},{1,6},{2,5},{3,4},{4,3},{5,2},{6,1},{7,0},{8,15},{9,14},{10,... | collective-permute-start | bytes 12296 | tf_op jit(solution)/shard_map/ppermute | solution.py:36
  21.3 0.2 collective-permute-start.8
  21.5 0.1 collective-permute-start.7
  21.6 1.0 %collective-permute-done.9 = f32[8,128]{1,0:T(8,128)S(1)} collective-permute-done((f32[8,128]{1,0:T(8,128)S(1)}, f32[8,128]{1,0:T(8,128)S(1)}, u32[]{:S(2)}, u32[]{:S(2)}) %collective-permute-start.9) | collective-permute-done | bytes 4128 | tf_op jit(solution)/shard_map/ppermute | solution.py:36
  22.6 1.7 %collective-permute-done.8 = f32[8,128]{1,0:T(8,128)S(1)} collective-permute-done((f32[8,128]{1,0:T(8,128)S(1)}, f32[8,128]{1,0:T(8,128)S(1)}, u32[]{:S(2)}, u32[]{:S(2)}) %collective-permute-start.8) | collective-permute-done | bytes 4128 | tf_op jit(solution)/shard_map/ppermute | solution.py:36
  24.3 0.2 collective-permute-done.7
  24.5 2.5 %collective-permute-start.10 = (f32[8,128]{1,0:T(8,128)S(1)}, f32[8,128]{1,0:T(8,128)S(1)}, u32[]{:S(2)}, u32[]{:S(2)}) collective-permute-start(f32[8,128]{1,0:T(8,128)S(1)} %add_add_fusion), channel_id=1, source_target_pairs={{0,9},{1,8},{2,11},{3,10},{4,13},{5,12},{6,15},{7,14},{8,1},{9,0},... | collective-permute-start | bytes 12296 | tf_op jit(solution)/shard_map/ppermute | solution.py:36
  27.1 1.4 %collective-permute-done.10 = f32[8,128]{1,0:T(8,128)S(1)} collective-permute-done((f32[8,128]{1,0:T(8,128)S(1)}, f32[8,128]{1,0:T(8,128)S(1)}, u32[]{:S(2)}, u32[]{:S(2)}) %collective-permute-start.10) | collective-permute-done | bytes 4128 | tf_op jit(solution)/shard_map/ppermute | solution.py:36
  28.5 0.6 %add.19 = f32[8,128]{1,0:T(8,128)} add(f32[8,128]{1,0:T(8,128)S(1)} %add_add_fusion, f32[8,128]{1,0:T(8,128)S(1)} %collective-permute-done.10) | non-fusion elementwise | flops 1024 | bytes 12288 | tf_op jit(solution)/shard_map/add | solution.py:255
  (2 shorter events, 0.0 us)
Async XLA Ops:
  0.0 3.5 %collective-permute-start = (bf16[2048,256]{1,0:T(8,128)(2,1)}, bf16[2048,256]{1,0:T(8,128)(2,1)S(1)}, u32[]{:S(2)}, u32[]{:S(2)}) collective-permute-start(bf16[2048,256]{1,0:T(8,128)(2,1)} %bitcast.10), channel_id=1, source_target_pairs={{0,1},{1,0},{2,3},{3,2},{4,5},{5,4},{6,7},{7,6},{8,9},{9,8},{10,11... | collective-permute-start | bytes 3145736 | tf_op jit(solution)/shard_map/ppermute | solution.py:36
  0.5 6.9 %copy-start = (bf16[1,384,7168]{2,1,0:T(8,128)(2,1)S(1)}, bf16[1,384,7168]{2,1,0:T(8,128)(2,1)}, u32[]{:S(2)}) copy-start(bf16[1,384,7168]{2,1,0:T(8,128)(2,1)} %param.6) | copy-start | bytes 16515076
  3.5 9.8 %collective-permute-start.3 = (bf16[7168,256]{1,0:T(8,128)(2,1)}, bf16[7168,256]{1,0:T(8,128)(2,1)S(1)}, u32[]{:S(2)}, u32[]{:S(2)}) collective-permute-start(bf16[7168,256]{1,0:T(8,128)(2,1)} %bitcast.8), channel_id=1, source_target_pairs={{0,1},{1,0},{2,3},{3,2},{4,5},{5,4},{6,7},{7,6},{8,9},{9,8},{10,11... | collective-permute-start | bytes 11010056 | tf_op jit(solution)/shard_map/ppermute | solution.py:36
  4.2 6.8 %collective-permute-start.1 = (s16[49,16,128]{2,1,0:T(8,128)(2,1)S(1)}, s16[49,16,128]{2,1,0:T(8,128)(2,1)S(1)}, u32[]{:S(2)}, u32[]{:S(2)}) collective-permute-start(s16[49,16,128]{2,1,0:T(8,128)(2,1)S(1)} %get-tuple-element.22), channel_id=1, source_target_pairs={{0,2},{1,5},{2,0},{3,7},{4,6},{5,1},{6,4},{7,3},{8,10},{9,13},{10,... | collective-permute-start | bytes 602120 | tf_op jit(solution)/shard_map/ppermute | solution.py:211
  7.3 8.1 %collective-permute-start.4 = (s16[49,16,128]{2,1,0:T(8,128)(2,1)S(1)}, s16[49,16,128]{2,1,0:T(8,128)(2,1)S(1)}, u32[]{:S(2)}, u32[]{:S(2)}) collective-permute-start(s16[49,16,128]{2,1,0:T(8,128)(2,1)S(1)} %get-tuple-element.29), channel_id=1, source_target_pairs={{0,2},{1,5},{2,0},{3,7},{4,6},{5,1},{6,4},{7,3},{8,10},{9,13},{10,... | collective-permute-start | bytes 602120 | tf_op jit(solution)/shard_map/ppermute | solution.py:211
  7.3 5.9 %copy-start.1 = (s32[4]{0:T(128)S(1)}, s32[4]{0:T(128)}, u32[]{:S(2)}) copy-start(s32[4]{0:T(128)} %lengths.3) | copy-start | bytes 52
  9.0 6.4 %collective-permute-start.5 = (s16[49,16,128]{2,1,0:T(8,128)(2,1)S(1)}, s16[49,16,128]{2,1,0:T(8,128)(2,1)S(1)}, u32[]{:S(2)}, u32[]{:S(2)}) collective-permute-start(s16[49,16,128]{2,1,0:T(8,128)(2,1)S(1)} %get-tuple-element.30), channel_id=1, source_target_pairs={{0,4},{1,3},{2,6},{3,1},{4,0},{5,7},{6,2},{7,5},{8,12},{9,11},{10,... | collective-permute-start | bytes 602120 | tf_op jit(solution)/shard_map/ppermute | solution.py:211
  11.2 5.8 %collective-permute-start.2 = (s16[49,16,128]{2,1,0:T(8,128)(2,1)S(1)}, s16[49,16,128]{2,1,0:T(8,128)(2,1)S(1)}, u32[]{:S(2)}, u32[]{:S(2)}) collective-permute-start(s16[49,16,128]{2,1,0:T(8,128)(2,1)S(1)} %get-tuple-element.26), channel_id=1, source_target_pairs={{0,4},{1,3},{2,6},{3,1},{4,0},{5,7},{6,2},{7,5},{8,12},{9,11},{10,... | collective-permute-start | bytes 602120 | tf_op jit(solution)/shard_map/ppermute | solution.py:211
  17.2 1.2 %collective-permute-start.6 = (f32[8,128]{1,0:T(8,128)S(1)}, f32[8,128]{1,0:T(8,128)S(1)}, u32[]{:S(2)}, u32[]{:S(2)}) collective-permute-start(f32[8,128]{1,0:T(8,128)S(1)} %other_scores.1), channel_id=1, source_target_pairs={{0,1},{1,0},{2,3},{3,2},{4,5},{5,4},{6,7},{7,6},{8,9},{9,8},{10,11... | collective-permute-start | bytes 12296 | tf_op jit(solution)/shard_map/ppermute | solution.py:36
  18.4 4.2 %collective-permute-start.9 = (f32[8,128]{1,0:T(8,128)S(1)}, f32[8,128]{1,0:T(8,128)S(1)}, u32[]{:S(2)}, u32[]{:S(2)}) collective-permute-start(f32[8,128]{1,0:T(8,128)S(1)} %add.15), channel_id=1, source_target_pairs={{0,7},{1,6},{2,5},{3,4},{4,3},{5,2},{6,1},{7,0},{8,15},{9,14},{10,... | collective-permute-start | bytes 12296 | tf_op jit(solution)/shard_map/ppermute | solution.py:36
  21.3 3.0 %collective-permute-start.8 = (f32[8,128]{1,0:T(8,128)S(1)}, f32[8,128]{1,0:T(8,128)S(1)}, u32[]{:S(2)}, u32[]{:S(2)}) collective-permute-start(f32[8,128]{1,0:T(8,128)S(1)} %add.15), channel_id=1, source_target_pairs={{0,5},{1,4},{2,7},{3,6},{4,1},{5,0},{6,3},{7,2},{8,13},{9,12},{10,... | collective-permute-start | bytes 12296 | tf_op jit(solution)/shard_map/ppermute | solution.py:36
  21.5 3.0 %collective-permute-start.7 = (f32[8,128]{1,0:T(8,128)S(1)}, f32[8,128]{1,0:T(8,128)S(1)}, u32[]{:S(2)}, u32[]{:S(2)}) collective-permute-start(f32[8,128]{1,0:T(8,128)S(1)} %add.15), channel_id=1, source_target_pairs={{0,3},{1,2},{2,1},{3,0},{4,7},{5,6},{6,5},{7,4},{8,11},{9,10},{10,... | collective-permute-start | bytes 12296 | tf_op jit(solution)/shard_map/ppermute | solution.py:36
  24.5 3.9 %collective-permute-start.10 = (f32[8,128]{1,0:T(8,128)S(1)}, f32[8,128]{1,0:T(8,128)S(1)}, u32[]{:S(2)}, u32[]{:S(2)}) collective-permute-start(f32[8,128]{1,0:T(8,128)S(1)} %add_add_fusion), channel_id=1, source_target_pairs={{0,9},{1,8},{2,11},{3,10},{4,13},{5,12},{6,15},{7,14},{8,1},{9,0},... | collective-permute-start | bytes 12296 | tf_op jit(solution)/shard_map/ppermute | solution.py:36

commit v11 on v10

--- a/solution.py
+++ b/solution.py
@@ -16,7 +16,7 @@
 FLOOR = 2.0**-112
 MIB = 2**20
 GRAD_STEP = 1
-ACT_OWN_MIB = 50
+ACT_OWN_MIB = 16
 
 IN_VMEM = pl.BlockSpec(memory_space=pltpu.VMEM)
 IN_HBM = pl.BlockSpec(memory_space=pltpu.HBM)
@@ -230,7 +230,7 @@
     )(in_vmem(act_held), in_vmem(other_act))
     other_in = to_pair(other_out, 0)
     grad_own, grad_out = kernel(
-        grad_own_kernel, "grad_own_columns", (seqs_shape, message_shape), [IN_VMEM] * 2, [codes_shape], 8, depth,
+        grad_own_kernel, "grad_own_columns", (seqs_shape, message_shape), [IN_VMEM] * 2, [codes_shape], 16, depth,
     )(in_vmem(grads), in_vmem(factor_held))
     grad_in = to_pair(grad_out, GRAD_STEP)
     other_pair, other_out = kernel(
@@ -238,7 +238,7 @@
     )(in_vmem(other_total), other_in, in_vmem(grad_own))
     other_in = to_pair(other_out, 1)
     (grad_other,) = kernel(
-        grad_other_kernel, "grad_other_columns", (seqs_shape,), [IN_SMEM] + [IN_VMEM] * 2, [], 8, depth,
+        grad_other_kernel, "grad_other_columns", (seqs_shape,), [IN_SMEM] + [IN_VMEM] * 2, [], 16, depth,
     )(lengths, in_vmem(grads), in_vmem(other_grad))
     (own_scores,) = kernel(
         own_score_kernel, "own_scores", (score_shape,), [IN_SMEM] + [IN_VMEM] * 5, [seqs_shape] * 2, 8, 0,

time: 29.2 us -> 29.2 us (level)
  no operation moved by 1% of the time
where the time goes in v11:
time: 29.2 us; the launch traced here: 29.1 us
  starting transfers between devices  13.8 us (47%)
  Pallas kernels  8.65 us (30%)
  waiting for transfers between devices  5.95 us (20%)
  other arithmetic  0.6 us (2%)
    ppermute x4, starting transfers between devices, to_pair(): return in_vmem(lax.ppermute(out, both, pairs))  7.22 us
    ppermute x7, starting transfers between devices, from_partner(): return lax.ppermute(value, axis, pairs)  6.57 us
    ppermute x7, waiting for transfers between devices, from_partner(): return lax.ppermute(value, axis, pairs)  5.24 us
    pallas_call x1, Pallas kernels, on_device(): kernel(act_own_kernel, 'act_own_columns', (seqs_shape, message_shape, plt...  3 us
    pallas_call x1, Pallas kernels, on_device(): kernel(grad_other_kernel, 'grad_other_columns', (seqs_shape,), [IN_SMEM]...  2.12 us
    pallas_call x1, Pallas kernels, on_device(): kernel(grad_own_kernel, 'grad_own_columns', (seqs_shape, message_shape),...  1.63 us
    pallas_call x1, Pallas kernels, on_device(): kernel(own_score_kernel, 'own_scores', (score_shape,), [IN_SMEM] + [IN_VM...  0.88 us
    ppermute x4, waiting for transfers between devices, to_pair(): return in_vmem(lax.ppermute(out, both, pairs))  0.72 us
  transfers between devices with their start and end apart: 11, of which 6 were waited for; matrix products, arithmetic and copies ran while one was open for 0% of the time, Pallas kernels for 29%

profile of v11, /device:TPU:0, one launch (start us, length us, event | category | flops | bytes accessed | tf_op | source)
XLA Modules:
  0.0 29.1 jit_solution(1553899368985855210)
XLA Ops:
  0.0 0.5 %collective-permute-start = (bf16[2048,256]{1,0:T(8,128)(2,1)}, bf16[2048,256]{1,0:T(8,128)(2,1)S(1)}, u32[]{:S(2)}, u32[]{:S(2)}) collective-permute-start(bf16[2048,256]{1,0:T(8,128)(2,1)} %bitcast.10), channel_id=1, source_target_pairs={{0,1},{1,0},{2,3},{3,2},{4,5},{5,4},{6,7},{7,6},{8,9},{9,8},{10,11... | collective-permute-start | bytes 3145736 | tf_op jit(solution)/shard_map/ppermute | solution.py:36
  0.5 0.0 copy-start
  0.5 3.0 %act_own_columns.1 = (f32[4,96,256]{2,1,0:T(8,128)S(1)}, s16[49,16,128]{2,1,0:T(8,128)(2,1)S(1)}, bf16[384,2048]{1,0:T(8,128)(2,1)S(1)}, bf16[7168,256]{1,0:T(8,128)(2,1)S(1)}) custom-call(bf16[384,2048]{1,0:T(8,128)(2,1)} %bitcast.9, bf16[2048,256]{1,0:T(8,128)(2,1)} %bitcast.11, bf16[7168,256]{1,0:T(8,128)(2,1)} %bitcast.7), custom_call_target="tpu_custom_call" | custom-call | flops 402653184 | bytes 16777216 | tf_op jit(solution)/shard_map/act_own_columns/pallas_call | solution.py:214
  3.5 0.0 collective-permute-done.factor
  3.5 0.1 collective-permute-start.3
  3.6 0.6 %act_other_columns.1 = (f32[4,96,256]{2,1,0:T(8,128)S(1)}, s16[49,16,128]{2,1,0:T(8,128)(2,1)S(1)}) custom-call(bf16[384,2048]{1,0:T(8,128)(2,1)S(1)} %get-tuple-element.18.rows_held, bf16[2048,256]{1,0:T(8,128)(2,1)S(1)} %collective-permute-done.factor), custom_call_target="tpu_custom_call" | custom-call | flops 402653184 | bytes 8388608 | tf_op jit(solution)/shard_map/act_other_columns/pallas_call | solution.py:227
  4.2 3.0 %collective-permute-start.1 = (s16[49,16,128]{2,1,0:T(8,128)(2,1)S(1)}, s16[49,16,128]{2,1,0:T(8,128)(2,1)S(1)}, u32[]{:S(2)}, u32[]{:S(2)}) collective-permute-start(s16[49,16,128]{2,1,0:T(8,128)(2,1)S(1)} %get-tuple-element.22), channel_id=1, source_target_pairs={{0,2},{1,5},{2,0},{3,7},{4,6},{5,1},{6,4},{7,3},{8,10},{9,13},{10,... | collective-permute-start | bytes 602120 | tf_op jit(solution)/shard_map/ppermute | solution.py:211
  7.3 0.1 collective-permute-start.4
  7.3 0.0 copy-done
  7.3 0.0 copy-start.1
  7.3 1.6 %grad_own_columns.1 = (f32[4,96,256]{2,1,0:T(8,128)S(1)}, s16[49,16,128]{2,1,0:T(8,128)(2,1)S(1)}) custom-call(bf16[384,7168]{1,0:T(8,128)(2,1)S(1)} %bitcast.5, bf16[7168,256]{1,0:T(8,128)(2,1)S(1)} %get-tuple-element.23.factor), custom_call_target="tpu_custom_call" | custom-call | flops 1409286144 | bytes 16777216 | tf_op jit(solution)/shard_map/grad_own_columns/pallas_call | solution.py:232
  9.0 2.1 %collective-permute-start.5 = (s16[49,16,128]{2,1,0:T(8,128)(2,1)S(1)}, s16[49,16,128]{2,1,0:T(8,128)(2,1)S(1)}, u32[]{:S(2)}, u32[]{:S(2)}) collective-permute-start(s16[49,16,128]{2,1,0:T(8,128)(2,1)S(1)} %get-tuple-element.30), channel_id=1, source_target_pairs={{0,4},{1,3},{2,6},{3,1},{4,0},{5,7},{6,2},{7,5},{8,12},{9,11},{10,... | collective-permute-start | bytes 602120 | tf_op jit(solution)/shard_map/ppermute | solution.py:211
  11.1 0.0 collective-permute-done.1.message
  11.1 0.1 other_pair.1
  11.2 2.0 %collective-permute-start.2 = (s16[49,16,128]{2,1,0:T(8,128)(2,1)S(1)}, s16[49,16,128]{2,1,0:T(8,128)(2,1)S(1)}, u32[]{:S(2)}, u32[]{:S(2)}) collective-permute-start(s16[49,16,128]{2,1,0:T(8,128)(2,1)S(1)} %get-tuple-element.26), channel_id=1, source_target_pairs={{0,4},{1,3},{2,6},{3,1},{4,0},{5,7},{6,2},{7,5},{8,12},{9,11},{10,... | collective-permute-start | bytes 602120 | tf_op jit(solution)/shard_map/ppermute | solution.py:211
  13.2 0.0 collective-permute-done.3.factor
  13.2 0.0 copy-done.1
  13.3 2.1 %grad_other_columns.1.after.grad_total = f32[4,96,256]{2,1,0:T(8,128)S(1)} custom-call(s32[4]{0:T(128)S(1)} %copy-done.1, bf16[384,7168]{1,0:T(8,128)(2,1)S(1)} %bitcast.6, bf16[7168,256]{1,0:T(8,128)(2,1)S(1)} %collective-permute-done.3.factor), custom_call_target="tpu_custom_call" | custom-call | flops 1409286144 | bytes 16777216 | tf_op jit(solution)/shard_map/grad_other_columns/pallas_call | solution.py:240
  15.4 0.0 collective-permute-done.4.act_message
  15.4 0.0 collective-permute-done.5.grad_message
  15.4 0.9 %own_scores.1.before = f32[8,128]{1,0:T(8,128)S(1)} custom-call(s32[4]{0:T(128)S(1)} %copy-done.1, f32[4,96,256]{2,1,0:T(8,128)S(1)} %get-tuple-element.28.act_total, s16[49,16,128]{2,1,0:T(8,128)(2,1)S(1)} %collective-permute-done.4.act_message, f32[4,96,256]{2,1,0:T(8,128)S(1)} %get-tuple-element.24.refs_0_.grad_total, ...), custom_call_target="tpu_custom_call" | custom-call | bytes 8388608 | tf_op jit(solution)/shard_map/own_scores/pallas_call | solution.py:243
  16.3 0.7 %collective-permute-done.2.message = s16[49,16,128]{2,1,0:T(8,128)(2,1)S(1)} collective-permute-done((s16[49,16,128]{2,1,0:T(8,128)(2,1)S(1)}, s16[49,16,128]{2,1,0:T(8,128)(2,1)S(1)}, u32[]{:S(2)}, u32[]{:S(2)}) %collective-permute-start.2) | collective-permute-done | bytes 200736 | tf_op jit(solution)/shard_map/ppermute | solution.py:211
  17.0 0.2 other_scores.1
  17.2 0.2 collective-permute-start.6
  17.5 0.9 %collective-permute-done.6 = f32[8,128]{1,0:T(8,128)S(1)} collective-permute-done((f32[8,128]{1,0:T(8,128)S(1)}, f32[8,128]{1,0:T(8,128)S(1)}, u32[]{:S(2)}, u32[]{:S(2)}) %collective-permute-start.6) | collective-permute-done | bytes 4128 | tf_op jit(solution)/shard_map/ppermute | solution.py:36
  18.4 2.9 %collective-permute-start.9 = (f32[8,128]{1,0:T(8,128)S(1)}, f32[8,128]{1,0:T(8,128)S(1)}, u32[]{:S(2)}, u32[]{:S(2)}) collective-permute-start(f32[8,128]{1,0:T(8,128)S(1)} %add.15), channel_id=1, source_target_pairs={{0,7},{1,6},{2,5},{3,4},{4,3},{5,2},{6,1},{7,0},{8,15},{9,14},{10,... | collective-permute-start | bytes 12296 | tf_op jit(solution)/shard_map/ppermute | solution.py:36
  21.3 0.2 collective-permute-start.8
  21.5 0.1 collective-permute-start.7
  21.6 1.0 %collective-permute-done.9 = f32[8,128]{1,0:T(8,128)S(1)} collective-permute-done((f32[8,128]{1,0:T(8,128)S(1)}, f32[8,128]{1,0:T(8,128)S(1)}, u32[]{:S(2)}, u32[]{:S(2)}) %collective-permute-start.9) | collective-permute-done | bytes 4128 | tf_op jit(solution)/shard_map/ppermute | solution.py:36
  22.6 1.7 %collective-permute-done.8 = f32[8,128]{1,0:T(8,128)S(1)} collective-permute-done((f32[8,128]{1,0:T(8,128)S(1)}, f32[8,128]{1,0:T(8,128)S(1)}, u32[]{:S(2)}, u32[]{:S(2)}) %collective-permute-start.8) | collective-permute-done | bytes 4128 | tf_op jit(solution)/shard_map/ppermute | solution.py:36
  24.3 0.2 collective-permute-done.7
  24.5 2.5 %collective-permute-start.10 = (f32[8,128]{1,0:T(8,128)S(1)}, f32[8,128]{1,0:T(8,128)S(1)}, u32[]{:S(2)}, u32[]{:S(2)}) collective-permute-start(f32[8,128]{1,0:T(8,128)S(1)} %add_add_fusion), channel_id=1, source_target_pairs={{0,9},{1,8},{2,11},{3,10},{4,13},{5,12},{6,15},{7,14},{8,1},{9,0},... | collective-permute-start | bytes 12296 | tf_op jit(solution)/shard_map/ppermute | solution.py:36
  27.1 1.4 %collective-permute-done.10 = f32[8,128]{1,0:T(8,128)S(1)} collective-permute-done((f32[8,128]{1,0:T(8,128)S(1)}, f32[8,128]{1,0:T(8,128)S(1)}, u32[]{:S(2)}, u32[]{:S(2)}) %collective-permute-start.10) | collective-permute-done | bytes 4128 | tf_op jit(solution)/shard_map/ppermute | solution.py:36
  28.5 0.6 %add.19 = f32[8,128]{1,0:T(8,128)} add(f32[8,128]{1,0:T(8,128)S(1)} %add_add_fusion, f32[8,128]{1,0:T(8,128)S(1)} %collective-permute-done.10) | non-fusion elementwise | flops 1024 | bytes 12288 | tf_op jit(solution)/shard_map/add | solution.py:255
  (2 shorter events, 0.0 us)
Async XLA Ops:
  0.0 3.5 %collective-permute-start = (bf16[2048,256]{1,0:T(8,128)(2,1)}, bf16[2048,256]{1,0:T(8,128)(2,1)S(1)}, u32[]{:S(2)}, u32[]{:S(2)}) collective-permute-start(bf16[2048,256]{1,0:T(8,128)(2,1)} %bitcast.10), channel_id=1, source_target_pairs={{0,1},{1,0},{2,3},{3,2},{4,5},{5,4},{6,7},{7,6},{8,9},{9,8},{10,11... | collective-permute-start | bytes 3145736 | tf_op jit(solution)/shard_map/ppermute | solution.py:36
  0.5 6.9 %copy-start = (bf16[1,384,7168]{2,1,0:T(8,128)(2,1)S(1)}, bf16[1,384,7168]{2,1,0:T(8,128)(2,1)}, u32[]{:S(2)}) copy-start(bf16[1,384,7168]{2,1,0:T(8,128)(2,1)} %param.6) | copy-start | bytes 16515076
  3.5 9.8 %collective-permute-start.3 = (bf16[7168,256]{1,0:T(8,128)(2,1)}, bf16[7168,256]{1,0:T(8,128)(2,1)S(1)}, u32[]{:S(2)}, u32[]{:S(2)}) collective-permute-start(bf16[7168,256]{1,0:T(8,128)(2,1)} %bitcast.8), channel_id=1, source_target_pairs={{0,1},{1,0},{2,3},{3,2},{4,5},{5,4},{6,7},{7,6},{8,9},{9,8},{10,11... | collective-permute-start | bytes 11010056 | tf_op jit(solution)/shard_map/ppermute | solution.py:36
  4.2 6.8 %collective-permute-start.1 = (s16[49,16,128]{2,1,0:T(8,128)(2,1)S(1)}, s16[49,16,128]{2,1,0:T(8,128)(2,1)S(1)}, u32[]{:S(2)}, u32[]{:S(2)}) collective-permute-start(s16[49,16,128]{2,1,0:T(8,128)(2,1)S(1)} %get-tuple-element.22), channel_id=1, source_target_pairs={{0,2},{1,5},{2,0},{3,7},{4,6},{5,1},{6,4},{7,3},{8,10},{9,13},{10,... | collective-permute-start | bytes 602120 | tf_op jit(solution)/shard_map/ppermute | solution.py:211
  7.3 8.1 %collective-permute-start.4 = (s16[49,16,128]{2,1,0:T(8,128)(2,1)S(1)}, s16[49,16,128]{2,1,0:T(8,128)(2,1)S(1)}, u32[]{:S(2)}, u32[]{:S(2)}) collective-permute-start(s16[49,16,128]{2,1,0:T(8,128)(2,1)S(1)} %get-tuple-element.29), channel_id=1, source_target_pairs={{0,2},{1,5},{2,0},{3,7},{4,6},{5,1},{6,4},{7,3},{8,10},{9,13},{10,... | collective-permute-start | bytes 602120 | tf_op jit(solution)/shard_map/ppermute | solution.py:211
  7.3 5.9 %copy-start.1 = (s32[4]{0:T(128)S(1)}, s32[4]{0:T(128)}, u32[]{:S(2)}) copy-start(s32[4]{0:T(128)} %lengths.3) | copy-start | bytes 52
  9.0 6.4 %collective-permute-start.5 = (s16[49,16,128]{2,1,0:T(8,128)(2,1)S(1)}, s16[49,16,128]{2,1,0:T(8,128)(2,1)S(1)}, u32[]{:S(2)}, u32[]{:S(2)}) collective-permute-start(s16[49,16,128]{2,1,0:T(8,128)(2,1)S(1)} %get-tuple-element.30), channel_id=1, source_target_pairs={{0,4},{1,3},{2,6},{3,1},{4,0},{5,7},{6,2},{7,5},{8,12},{9,11},{10,... | collective-permute-start | bytes 602120 | tf_op jit(solution)/shard_map/ppermute | solution.py:211
  11.2 5.8 %collective-permute-start.2 = (s16[49,16,128]{2,1,0:T(8,128)(2,1)S(1)}, s16[49,16,128]{2,1,0:T(8,128)(2,1)S(1)}, u32[]{:S(2)}, u32[]{:S(2)}) collective-permute-start(s16[49,16,128]{2,1,0:T(8,128)(2,1)S(1)} %get-tuple-element.26), channel_id=1, source_target_pairs={{0,4},{1,3},{2,6},{3,1},{4,0},{5,7},{6,2},{7,5},{8,12},{9,11},{10,... | collective-permute-start | bytes 602120 | tf_op jit(solution)/shard_map/ppermute | solution.py:211
  17.2 1.2 %collective-permute-start.6 = (f32[8,128]{1,0:T(8,128)S(1)}, f32[8,128]{1,0:T(8,128)S(1)}, u32[]{:S(2)}, u32[]{:S(2)}) collective-permute-start(f32[8,128]{1,0:T(8,128)S(1)} %other_scores.1), channel_id=1, source_target_pairs={{0,1},{1,0},{2,3},{3,2},{4,5},{5,4},{6,7},{7,6},{8,9},{9,8},{10,11... | collective-permute-start | bytes 12296 | tf_op jit(solution)/shard_map/ppermute | solution.py:36
  18.4 4.2 %collective-permute-start.9 = (f32[8,128]{1,0:T(8,128)S(1)}, f32[8,128]{1,0:T(8,128)S(1)}, u32[]{:S(2)}, u32[]{:S(2)}) collective-permute-start(f32[8,128]{1,0:T(8,128)S(1)} %add.15), channel_id=1, source_target_pairs={{0,7},{1,6},{2,5},{3,4},{4,3},{5,2},{6,1},{7,0},{8,15},{9,14},{10,... | collective-permute-start | bytes 12296 | tf_op jit(solution)/shard_map/ppermute | solution.py:36
  21.3 3.0 %collective-permute-start.8 = (f32[8,128]{1,0:T(8,128)S(1)}, f32[8,128]{1,0:T(8,128)S(1)}, u32[]{:S(2)}, u32[]{:S(2)}) collective-permute-start(f32[8,128]{1,0:T(8,128)S(1)} %add.15), channel_id=1, source_target_pairs={{0,5},{1,4},{2,7},{3,6},{4,1},{5,0},{6,3},{7,2},{8,13},{9,12},{10,... | collective-permute-start | bytes 12296 | tf_op jit(solution)/shard_map/ppermute | solution.py:36
  21.5 3.0 %collective-permute-start.7 = (f32[8,128]{1,0:T(8,128)S(1)}, f32[8,128]{1,0:T(8,128)S(1)}, u32[]{:S(2)}, u32[]{:S(2)}) collective-permute-start(f32[8,128]{1,0:T(8,128)S(1)} %add.15), channel_id=1, source_target_pairs={{0,3},{1,2},{2,1},{3,0},{4,7},{5,6},{6,5},{7,4},{8,11},{9,10},{10,... | collective-permute-start | bytes 12296 | tf_op jit(solution)/shard_map/ppermute | solution.py:36
  24.5 3.9 %collective-permute-start.10 = (f32[8,128]{1,0:T(8,128)S(1)}, f32[8,128]{1,0:T(8,128)S(1)}, u32[]{:S(2)}, u32[]{:S(2)}) collective-permute-start(f32[8,128]{1,0:T(8,128)S(1)} %add_add_fusion), channel_id=1, source_target_pairs={{0,9},{1,8},{2,11},{3,10},{4,13},{5,12},{6,15},{7,14},{8,1},{9,0},... | collective-permute-start | bytes 12296 | tf_op jit(solution)/shard_map/ppermute | solution.py:36

commit v12 on v11

--- a/solution.py
+++ b/solution.py
@@ -130,9 +130,8 @@
         total[seq] = jnp.where(offsets < lengths[seq], total[seq], 0.0)
 
 
-def grad_other_kernel(lengths, grads, factor, total):
+def grad_other_kernel(grads, factor, total):
     keep(dot(grads[...], factor[...]), total)
-    drop_padding(total, lengths)
 
 
 def score(act, grad, holder, out, before):
@@ -158,10 +157,12 @@
         out[first:first + 8, :] = scores if before is None else before[first:first + 8, :] + scores
 
 
-def own_score_kernel(lengths, act_total, act_message, grad_total, grad_message, after, out, act, grad):
+def own_score_kernel(lengths, act_total, act_message, grad_total, grad_message, grad_other, out, live, act, grad):
     add(act_total, act_message, act)
     add(grad_total, grad_message, grad)
     drop_padding(act, lengths)
+    live[...] = grad_other[...]
+    drop_padding(live, lengths)
     score(act, grad, lax.axis_index("loop"), out, None)
 
 
@@ -238,10 +239,10 @@
     )(in_vmem(other_total), other_in, in_vmem(grad_own))
     other_in = to_pair(other_out, 1)
     (grad_other,) = kernel(
-        grad_other_kernel, "grad_other_columns", (seqs_shape,), [IN_SMEM] + [IN_VMEM] * 2, [], 16, depth,
-    )(lengths, in_vmem(grads), in_vmem(other_grad))
-    (own_scores,) = kernel(
-        own_score_kernel, "own_scores", (score_shape,), [IN_SMEM] + [IN_VMEM] * 5, [seqs_shape] * 2, 8, 0,
+        grad_other_kernel, "grad_other_columns", (seqs_shape,), [IN_VMEM] * 2, [], 16, depth,
+    )(in_vmem(grads), in_vmem(other_grad))
+    own_scores, grad_other = kernel(
+        own_score_kernel, "own_scores", (score_shape, seqs_shape), [IN_SMEM] + [IN_VMEM] * 5, [seqs_shape] * 2, 8, 0,
     )(lengths, in_vmem(own_total), own_in, in_vmem(grad_own), grad_in, in_vmem(grad_other))
     (total,) = kernel(
         other_score_kernel, "other_scores", (score_shape,), [IN_VMEM] * 4, [seqs_shape], 8, 0,

time: 29.2 us -> 29.2 us (level)
  Pallas kernels: 8.65 us -> 8.13 us
  waiting for transfers between devices: 5.95 us -> 6.47 us
    pallas_call x2, Pallas kernels: 3 us -> 2.49 us  [the longest x1 1.58 us: on_device(): kernel(grad_other_kernel, 'grad_other_columns', (seqs_shape,), [IN_VMEM]...]
    ppermute x4, waiting for transfers between devices: 0.72 us -> 1.22 us  [to_pair(): return in_vmem(lax.ppermute(out, both, pairs))]
  transfers between devices with their start and end apart: 11 -> 11, of which waited for: 6 -> 6; matrix products, arithmetic and copies ran while one was open for 0% -> 0% of each run, Pallas kernels for 29% -> 27%
where the time goes in v12:
time: 29.2 us; the launch traced here: 29.1 us
  starting transfers between devices  13.8 us (47%)
  Pallas kernels  8.13 us (28%)
  waiting for transfers between devices  6.47 us (22%)
  other arithmetic  0.6 us (2%)
    ppermute x4, starting transfers between devices, to_pair(): return in_vmem(lax.ppermute(out, both, pairs))  7.22 us
    ppermute x7, starting transfers between devices, from_partner(): return lax.ppermute(value, axis, pairs)  6.55 us
    ppermute x7, waiting for transfers between devices, from_partner(): return lax.ppermute(value, axis, pairs)  5.25 us
    pallas_call x1, Pallas kernels, on_device(): kernel(act_own_kernel, 'act_own_columns', (seqs_shape, message_shape, plt...  3 us
    pallas_call x1, Pallas kernels, on_device(): kernel(grad_own_kernel, 'grad_own_columns', (seqs_shape, message_shape),...  1.63 us
    pallas_call x1, Pallas kernels, on_device(): kernel(grad_other_kernel, 'grad_other_columns', (seqs_shape,), [IN_VMEM]...  1.58 us
    ppermute x4, waiting for transfers between devices, to_pair(): return in_vmem(lax.ppermute(out, both, pairs))  1.22 us
    pallas_call x1, Pallas kernels, on_device(): kernel(own_score_kernel, 'own_scores', (score_shape, seqs_shape), [IN_SME...  0.9 us
  transfers between devices with their start and end apart: 11, of which 6 were waited for; matrix products, arithmetic and copies ran while one was open for 0% of the time, Pallas kernels for 27%

profile of v12, /device:TPU:0, one launch (start us, length us, event | category | flops | bytes accessed | tf_op | source)
XLA Modules:
  0.0 29.1 jit_solution(15350390295675196423)
XLA Ops:
  0.0 0.5 %collective-permute-start = (bf16[2048,256]{1,0:T(8,128)(2,1)}, bf16[2048,256]{1,0:T(8,128)(2,1)S(1)}, u32[]{:S(2)}, u32[]{:S(2)}) collective-permute-start(bf16[2048,256]{1,0:T(8,128)(2,1)} %bitcast.10), channel_id=1, source_target_pairs={{0,1},{1,0},{2,3},{3,2},{4,5},{5,4},{6,7},{7,6},{8,9},{9,8},{10,11... | collective-permute-start | bytes 3145736 | tf_op jit(solution)/shard_map/ppermute | solution.py:36
  0.5 0.0 copy-start
  0.5 3.0 %act_own_columns.1 = (f32[4,96,256]{2,1,0:T(8,128)S(1)}, s16[49,16,128]{2,1,0:T(8,128)(2,1)S(1)}, bf16[384,2048]{1,0:T(8,128)(2,1)S(1)}, bf16[7168,256]{1,0:T(8,128)(2,1)S(1)}) custom-call(bf16[384,2048]{1,0:T(8,128)(2,1)} %bitcast.9, bf16[2048,256]{1,0:T(8,128)(2,1)} %bitcast.11, bf16[7168,256]{1,0:T(8,128)(2,1)} %bitcast.7), custom_call_target="tpu_custom_call" | custom-call | flops 402653184 | bytes 16777216 | tf_op jit(solution)/shard_map/act_own_columns/pallas_call | solution.py:215
  3.5 0.0 collective-permute-done.factor
  3.5 0.1 collective-permute-start.5
  3.6 0.6 %act_other_columns.1 = (f32[4,96,256]{2,1,0:T(8,128)S(1)}, s16[49,16,128]{2,1,0:T(8,128)(2,1)S(1)}) custom-call(bf16[384,2048]{1,0:T(8,128)(2,1)S(1)} %get-tuple-element.20.rows_held, bf16[2048,256]{1,0:T(8,128)(2,1)S(1)} %collective-permute-done.factor), custom_call_target="tpu_custom_call" | custom-call | flops 402653184 | bytes 8388608 | tf_op jit(solution)/shard_map/act_other_columns/pallas_call | solution.py:228
  4.2 3.0 %collective-permute-start.1 = (s16[49,16,128]{2,1,0:T(8,128)(2,1)S(1)}, s16[49,16,128]{2,1,0:T(8,128)(2,1)S(1)}, u32[]{:S(2)}, u32[]{:S(2)}) collective-permute-start(s16[49,16,128]{2,1,0:T(8,128)(2,1)S(1)} %get-tuple-element.24), channel_id=1, source_target_pairs={{0,2},{1,5},{2,0},{3,7},{4,6},{5,1},{6,4},{7,3},{8,10},{9,13},{10,... | collective-permute-start | bytes 602120 | tf_op jit(solution)/shard_map/ppermute | solution.py:212
  7.3 0.1 collective-permute-start.3
  7.3 0.0 copy-done
  7.3 1.6 %grad_own_columns.1 = (f32[4,96,256]{2,1,0:T(8,128)S(1)}, s16[49,16,128]{2,1,0:T(8,128)(2,1)S(1)}) custom-call(bf16[384,7168]{1,0:T(8,128)(2,1)S(1)} %bitcast.5, bf16[7168,256]{1,0:T(8,128)(2,1)S(1)} %get-tuple-element.25.factor), custom_call_target="tpu_custom_call" | custom-call | flops 1409286144 | bytes 16777216 | tf_op jit(solution)/shard_map/grad_own_columns/pallas_call | solution.py:233
  9.0 2.1 %collective-permute-start.4 = (s16[49,16,128]{2,1,0:T(8,128)(2,1)S(1)}, s16[49,16,128]{2,1,0:T(8,128)(2,1)S(1)}, u32[]{:S(2)}, u32[]{:S(2)}) collective-permute-start(s16[49,16,128]{2,1,0:T(8,128)(2,1)S(1)} %get-tuple-element.31), channel_id=1, source_target_pairs={{0,4},{1,3},{2,6},{3,1},{4,0},{5,7},{6,2},{7,5},{8,12},{9,11},{10,... | collective-permute-start | bytes 602120 | tf_op jit(solution)/shard_map/ppermute | solution.py:212
  11.1 0.0 collective-permute-done.1.message
  11.1 0.1 other_pair.1
  11.2 0.0 copy-start.1
  11.2 2.0 %collective-permute-start.2 = (s16[49,16,128]{2,1,0:T(8,128)(2,1)S(1)}, s16[49,16,128]{2,1,0:T(8,128)(2,1)S(1)}, u32[]{:S(2)}, u32[]{:S(2)}) collective-permute-start(s16[49,16,128]{2,1,0:T(8,128)(2,1)S(1)} %get-tuple-element.28), channel_id=1, source_target_pairs={{0,4},{1,3},{2,6},{3,1},{4,0},{5,7},{6,2},{7,5},{8,12},{9,11},{10,... | collective-permute-start | bytes 602120 | tf_op jit(solution)/shard_map/ppermute | solution.py:212
  13.3 0.0 collective-permute-done.5.factor
  13.3 1.6 %grad_other_columns.1.grad_other = f32[4,96,256]{2,1,0:T(8,128)S(1)} custom-call(bf16[384,7168]{1,0:T(8,128)(2,1)S(1)} %bitcast.6, bf16[7168,256]{1,0:T(8,128)(2,1)S(1)} %collective-permute-done.5.factor), custom_call_target="tpu_custom_call" | custom-call | flops 1409286144 | bytes 16777216 | tf_op jit(solution)/shard_map/grad_other_columns/pallas_call | solution.py:241
  14.8 0.0 collective-permute-done.3.act_message
  14.9 0.0 collective-permute-done.4.grad_message
  14.9 0.0 copy-done.1
  14.9 0.9 %own_scores.1 = (f32[8,128]{1,0:T(8,128)S(1)}, f32[4,96,256]{2,1,0:T(8,128)S(1)}) custom-call(s32[4]{0:T(128)S(1)} %copy-done.1, f32[4,96,256]{2,1,0:T(8,128)S(1)} %get-tuple-element.29.act_total, s16[49,16,128]{2,1,0:T(8,128)(2,1)S(1)} %collective-permute-done.3.act_message, f32[4,96,256]{2,1,0:T(8,128)S(1)} %get-tuple-element.26.refs_0_.grad_total, ...), custom_call_target="tpu_custom_call" | custom-call | bytes 8388608 | tf_op jit(solution)/shard_map/own_scores/pallas_call | solution.py:244
  15.8 1.2 %collective-permute-done.2.message = s16[49,16,128]{2,1,0:T(8,128)(2,1)S(1)} collective-permute-done((s16[49,16,128]{2,1,0:T(8,128)(2,1)S(1)}, s16[49,16,128]{2,1,0:T(8,128)(2,1)S(1)}, u32[]{:S(2)}, u32[]{:S(2)}) %collective-permute-start.2) | collective-permute-done | bytes 200736 | tf_op jit(solution)/shard_map/ppermute | solution.py:212
  17.0 0.2 other_scores.1
  17.2 0.2 collective-permute-start.6
  17.5 0.9 %collective-permute-done.6 = f32[8,128]{1,0:T(8,128)S(1)} collective-permute-done((f32[8,128]{1,0:T(8,128)S(1)}, f32[8,128]{1,0:T(8,128)S(1)}, u32[]{:S(2)}, u32[]{:S(2)}) %collective-permute-start.6) | collective-permute-done | bytes 4128 | tf_op jit(solution)/shard_map/ppermute | solution.py:36
  18.4 2.9 %collective-permute-start.9 = (f32[8,128]{1,0:T(8,128)S(1)}, f32[8,128]{1,0:T(8,128)S(1)}, u32[]{:S(2)}, u32[]{:S(2)}) collective-permute-start(f32[8,128]{1,0:T(8,128)S(1)} %add.15), channel_id=1, source_target_pairs={{0,7},{1,6},{2,5},{3,4},{4,3},{5,2},{6,1},{7,0},{8,15},{9,14},{10,... | collective-permute-start | bytes 12296 | tf_op jit(solution)/shard_map/ppermute | solution.py:36
  21.3 0.2 collective-permute-start.8
  21.5 0.1 collective-permute-start.7
  21.6 1.0 %collective-permute-done.9 = f32[8,128]{1,0:T(8,128)S(1)} collective-permute-done((f32[8,128]{1,0:T(8,128)S(1)}, f32[8,128]{1,0:T(8,128)S(1)}, u32[]{:S(2)}, u32[]{:S(2)}) %collective-permute-start.9) | collective-permute-done | bytes 4128 | tf_op jit(solution)/shard_map/ppermute | solution.py:36
  22.6 1.7 %collective-permute-done.8 = f32[8,128]{1,0:T(8,128)S(1)} collective-permute-done((f32[8,128]{1,0:T(8,128)S(1)}, f32[8,128]{1,0:T(8,128)S(1)}, u32[]{:S(2)}, u32[]{:S(2)}) %collective-permute-start.8) | collective-permute-done | bytes 4128 | tf_op jit(solution)/shard_map/ppermute | solution.py:36
  24.3 0.2 collective-permute-done.7
  24.6 2.5 %collective-permute-start.10 = (f32[8,128]{1,0:T(8,128)S(1)}, f32[8,128]{1,0:T(8,128)S(1)}, u32[]{:S(2)}, u32[]{:S(2)}) collective-permute-start(f32[8,128]{1,0:T(8,128)S(1)} %add_add_fusion), channel_id=1, source_target_pairs={{0,9},{1,8},{2,11},{3,10},{4,13},{5,12},{6,15},{7,14},{8,1},{9,0},... | collective-permute-start | bytes 12296 | tf_op jit(solution)/shard_map/ppermute | solution.py:36
  27.1 1.4 %collective-permute-done.10 = f32[8,128]{1,0:T(8,128)S(1)} collective-permute-done((f32[8,128]{1,0:T(8,128)S(1)}, f32[8,128]{1,0:T(8,128)S(1)}, u32[]{:S(2)}, u32[]{:S(2)}) %collective-permute-start.10) | collective-permute-done | bytes 4128 | tf_op jit(solution)/shard_map/ppermute | solution.py:36
  28.5 0.6 %add.19 = f32[8,128]{1,0:T(8,128)} add(f32[8,128]{1,0:T(8,128)S(1)} %add_add_fusion, f32[8,128]{1,0:T(8,128)S(1)} %collective-permute-done.10) | non-fusion elementwise | flops 1024 | bytes 12288 | tf_op jit(solution)/shard_map/add | solution.py:256
  (2 shorter events, 0.0 us)
Async XLA Ops:
  0.0 3.5 %collective-permute-start = (bf16[2048,256]{1,0:T(8,128)(2,1)}, bf16[2048,256]{1,0:T(8,128)(2,1)S(1)}, u32[]{:S(2)}, u32[]{:S(2)}) collective-permute-start(bf16[2048,256]{1,0:T(8,128)(2,1)} %bitcast.10), channel_id=1, source_target_pairs={{0,1},{1,0},{2,3},{3,2},{4,5},{5,4},{6,7},{7,6},{8,9},{9,8},{10,11... | collective-permute-start | bytes 3145736 | tf_op jit(solution)/shard_map/ppermute | solution.py:36
  0.5 6.9 %copy-start = (bf16[1,384,7168]{2,1,0:T(8,128)(2,1)S(1)}, bf16[1,384,7168]{2,1,0:T(8,128)(2,1)}, u32[]{:S(2)}) copy-start(bf16[1,384,7168]{2,1,0:T(8,128)(2,1)} %param.6) | copy-start | bytes 16515076
  3.5 9.8 %collective-permute-start.5 = (bf16[7168,256]{1,0:T(8,128)(2,1)}, bf16[7168,256]{1,0:T(8,128)(2,1)S(1)}, u32[]{:S(2)}, u32[]{:S(2)}) collective-permute-start(bf16[7168,256]{1,0:T(8,128)(2,1)} %bitcast.8), channel_id=1, source_target_pairs={{0,1},{1,0},{2,3},{3,2},{4,5},{5,4},{6,7},{7,6},{8,9},{9,8},{10,11... | collective-permute-start | bytes 11010056 | tf_op jit(solution)/shard_map/ppermute | solution.py:36
  4.2 6.8 %collective-permute-start.1 = (s16[49,16,128]{2,1,0:T(8,128)(2,1)S(1)}, s16[49,16,128]{2,1,0:T(8,128)(2,1)S(1)}, u32[]{:S(2)}, u32[]{:S(2)}) collective-permute-start(s16[49,16,128]{2,1,0:T(8,128)(2,1)S(1)} %get-tuple-element.24), channel_id=1, source_target_pairs={{0,2},{1,5},{2,0},{3,7},{4,6},{5,1},{6,4},{7,3},{8,10},{9,13},{10,... | collective-permute-start | bytes 602120 | tf_op jit(solution)/shard_map/ppermute | solution.py:212
  7.3 7.6 %collective-permute-start.3 = (s16[49,16,128]{2,1,0:T(8,128)(2,1)S(1)}, s16[49,16,128]{2,1,0:T(8,128)(2,1)S(1)}, u32[]{:S(2)}, u32[]{:S(2)}) collective-permute-start(s16[49,16,128]{2,1,0:T(8,128)(2,1)S(1)} %get-tuple-element.30), channel_id=1, source_target_pairs={{0,2},{1,5},{2,0},{3,7},{4,6},{5,1},{6,4},{7,3},{8,10},{9,13},{10,... | collective-permute-start | bytes 602120 | tf_op jit(solution)/shard_map/ppermute | solution.py:212
  9.0 5.9 %collective-permute-start.4 = (s16[49,16,128]{2,1,0:T(8,128)(2,1)S(1)}, s16[49,16,128]{2,1,0:T(8,128)(2,1)S(1)}, u32[]{:S(2)}, u32[]{:S(2)}) collective-permute-start(s16[49,16,128]{2,1,0:T(8,128)(2,1)S(1)} %get-tuple-element.31), channel_id=1, source_target_pairs={{0,4},{1,3},{2,6},{3,1},{4,0},{5,7},{6,2},{7,5},{8,12},{9,11},{10,... | collective-permute-start | bytes 602120 | tf_op jit(solution)/shard_map/ppermute | solution.py:212
  11.2 3.7 %copy-start.1 = (s32[4]{0:T(128)S(1)}, s32[4]{0:T(128)}, u32[]{:S(2)}) copy-start(s32[4]{0:T(128)} %lengths.1) | copy-start | bytes 52
  11.2 5.8 %collective-permute-start.2 = (s16[49,16,128]{2,1,0:T(8,128)(2,1)S(1)}, s16[49,16,128]{2,1,0:T(8,128)(2,1)S(1)}, u32[]{:S(2)}, u32[]{:S(2)}) collective-permute-start(s16[49,16,128]{2,1,0:T(8,128)(2,1)S(1)} %get-tuple-element.28), channel_id=1, source_target_pairs={{0,4},{1,3},{2,6},{3,1},{4,0},{5,7},{6,2},{7,5},{8,12},{9,11},{10,... | collective-permute-start | bytes 602120 | tf_op jit(solution)/shard_map/ppermute | solution.py:212
  17.2 1.2 %collective-permute-start.6 = (f32[8,128]{1,0:T(8,128)S(1)}, f32[8,128]{1,0:T(8,128)S(1)}, u32[]{:S(2)}, u32[]{:S(2)}) collective-permute-start(f32[8,128]{1,0:T(8,128)S(1)} %other_scores.1), channel_id=1, source_target_pairs={{0,1},{1,0},{2,3},{3,2},{4,5},{5,4},{6,7},{7,6},{8,9},{9,8},{10,11... | collective-permute-start | bytes 12296 | tf_op jit(solution)/shard_map/ppermute | solution.py:36
  18.4 4.2 %collective-permute-start.9 = (f32[8,128]{1,0:T(8,128)S(1)}, f32[8,128]{1,0:T(8,128)S(1)}, u32[]{:S(2)}, u32[]{:S(2)}) collective-permute-start(f32[8,128]{1,0:T(8,128)S(1)} %add.15), channel_id=1, source_target_pairs={{0,7},{1,6},{2,5},{3,4},{4,3},{5,2},{6,1},{7,0},{8,15},{9,14},{10,... | collective-permute-start | bytes 12296 | tf_op jit(solution)/shard_map/ppermute | solution.py:36
  21.3 3.0 %collective-permute-start.8 = (f32[8,128]{1,0:T(8,128)S(1)}, f32[8,128]{1,0:T(8,128)S(1)}, u32[]{:S(2)}, u32[]{:S(2)}) collective-permute-start(f32[8,128]{1,0:T(8,128)S(1)} %add.15), channel_id=1, source_target_pairs={{0,5},{1,4},{2,7},{3,6},{4,1},{5,0},{6,3},{7,2},{8,13},{9,12},{10,... | collective-permute-start | bytes 12296 | tf_op jit(solution)/shard_map/ppermute | solution.py:36
  21.5 3.0 %collective-permute-start.7 = (f32[8,128]{1,0:T(8,128)S(1)}, f32[8,128]{1,0:T(8,128)S(1)}, u32[]{:S(2)}, u32[]{:S(2)}) collective-permute-start(f32[8,128]{1,0:T(8,128)S(1)} %add.15), channel_id=1, source_target_pairs={{0,3},{1,2},{2,1},{3,0},{4,7},{5,6},{6,5},{7,4},{8,11},{9,10},{10,... | collective-permute-start | bytes 12296 | tf_op jit(solution)/shard_map/ppermute | solution.py:36
  24.6 3.9 %collective-permute-start.10 = (f32[8,128]{1,0:T(8,128)S(1)}, f32[8,128]{1,0:T(8,128)S(1)}, u32[]{:S(2)}, u32[]{:S(2)}) collective-permute-start(f32[8,128]{1,0:T(8,128)S(1)} %add_add_fusion), channel_id=1, source_target_pairs={{0,9},{1,8},{2,11},{3,10},{4,13},{5,12},{6,15},{7,14},{8,1},{9,0},... | collective-permute-start | bytes 12296 | tf_op jit(solution)/shard_map/ppermute | solution.py:36

commit v13 on v12

--- a/solution.py
+++ b/solution.py
@@ -94,18 +94,19 @@
 
 
 def act_own_kernel(acts, factor, grad_factor, total, out, rows_held, grad_factor_held, factor_held, codes, sems):
-    copies = (
-        pltpu.make_async_copy(factor, factor_held, sems.at[0]),
-        pltpu.make_async_copy(acts, rows_held, sems.at[1]),
-        pltpu.make_async_copy(grad_factor, grad_factor_held, sems.at[2]),
-    )
-    for copy in copies:
-        copy.start()
-    copies[0].wait()
-    copies[1].wait()
+    copies = []
+    for source, held in ((factor, factor_held), (acts, rows_held), (grad_factor, grad_factor_held)):
+        size = source.shape[0] // 2
+        for index in range(2):
+            span = pl.ds(index * size, size)
+            copies.append(pltpu.make_async_copy(source.at[span, :], held.at[span, :], sems.at[len(copies)]))
+            copies[-1].start()
+    for copy in copies[:4]:
+        copy.wait()
     keep(dot(rows_held[...], factor_held[...]), total)
     encode(total, out, codes)
-    copies[2].wait()
+    for copy in copies[4:]:
+        copy.wait()
 
 
 def act_other_kernel(rows_held, factor, total, out, codes):
@@ -219,7 +220,7 @@
             pltpu.VMEM(grad_factors.shape, grad_factors.dtype),
         ),
         [IN_HBM] * 3,
-        [pltpu.VMEM(act_factors.shape, act_factors.dtype), codes_shape, pltpu.SemaphoreType.DMA((3,))],
+        [pltpu.VMEM(act_factors.shape, act_factors.dtype), codes_shape, pltpu.SemaphoreType.DMA((6,))],
         ACT_OWN_MIB, acts.shape[1],
     )(in_hbm(acts), in_hbm(act_factors), in_hbm(grad_factors))
     own_in = to_pair(own_out, 1 - GRAD_STEP)

time: 29.2 us -> 29.3 us (level)
  no operation moved by 1% of the time
where the time goes in v13:
time: 29.3 us; the launch traced here: 29.1 us
  starting transfers between devices  13.8 us (47%)
  Pallas kernels  8.17 us (28%)
  waiting for transfers between devices  6.48 us (22%)
  other arithmetic  0.6 us (2%)
    ppermute x4, starting transfers between devices, to_pair(): return in_vmem(lax.ppermute(out, both, pairs))  7.22 us
    ppermute x7, starting transfers between devices, from_partner(): return lax.ppermute(value, axis, pairs)  6.55 us
    ppermute x7, waiting for transfers between devices, from_partner(): return lax.ppermute(value, axis, pairs)  5.26 us
    pallas_call x1, Pallas kernels, on_device(): kernel(act_own_kernel, 'act_own_columns', (seqs_shape, message_shape, plt...  3.04 us
    pallas_call x1, Pallas kernels, on_device(): kernel(grad_own_kernel, 'grad_own_columns', (seqs_shape, message_shape),...  1.63 us
    pallas_call x1, Pallas kernels, on_device(): kernel(grad_other_kernel, 'grad_other_columns', (seqs_shape,), [IN_VMEM]...  1.58 us
    ppermute x4, waiting for transfers between devices, to_pair(): return in_vmem(lax.ppermute(out, both, pairs))  1.22 us
    pallas_call x1, Pallas kernels, on_device(): kernel(own_score_kernel, 'own_scores', (score_shape, seqs_shape), [IN_SME...  0.9 us
  transfers between devices with their start and end apart: 11, of which 6 were waited for; matrix products, arithmetic and copies ran while one was open for 0% of the time, Pallas kernels for 27%

profile of v13, /device:TPU:0, one launch (start us, length us, event | category | flops | bytes accessed | tf_op | source)
XLA Modules:
  0.0 29.1 jit_solution(7307379292292421616)
XLA Ops:
  0.0 0.5 %collective-permute-start = (bf16[2048,256]{1,0:T(8,128)(2,1)}, bf16[2048,256]{1,0:T(8,128)(2,1)S(1)}, u32[]{:S(2)}, u32[]{:S(2)}) collective-permute-start(bf16[2048,256]{1,0:T(8,128)(2,1)} %bitcast.10), channel_id=1, source_target_pairs={{0,1},{1,0},{2,3},{3,2},{4,5},{5,4},{6,7},{7,6},{8,9},{9,8},{10,11... | collective-permute-start | bytes 3145736 | tf_op jit(solution)/shard_map/ppermute | solution.py:36
  0.5 0.0 copy-start
  0.5 3.0 %act_own_columns.1 = (f32[4,96,256]{2,1,0:T(8,128)S(1)}, s16[49,16,128]{2,1,0:T(8,128)(2,1)S(1)}, bf16[384,2048]{1,0:T(8,128)(2,1)S(1)}, bf16[7168,256]{1,0:T(8,128)(2,1)S(1)}) custom-call(bf16[384,2048]{1,0:T(8,128)(2,1)} %bitcast.9, bf16[2048,256]{1,0:T(8,128)(2,1)} %bitcast.11, bf16[7168,256]{1,0:T(8,128)(2,1)} %bitcast.7), custom_call_target="tpu_custom_call" | custom-call | flops 402653184 | bytes 16777216 | tf_op jit(solution)/shard_map/act_own_columns/pallas_call | solution.py:216
  3.5 0.0 collective-permute-done.factor
  3.5 0.1 collective-permute-start.5
  3.6 0.6 %act_other_columns.1 = (f32[4,96,256]{2,1,0:T(8,128)S(1)}, s16[49,16,128]{2,1,0:T(8,128)(2,1)S(1)}) custom-call(bf16[384,2048]{1,0:T(8,128)(2,1)S(1)} %get-tuple-element.20.rows_held, bf16[2048,256]{1,0:T(8,128)(2,1)S(1)} %collective-permute-done.factor), custom_call_target="tpu_custom_call" | custom-call | flops 402653184 | bytes 8388608 | tf_op jit(solution)/shard_map/act_other_columns/pallas_call | solution.py:229
  4.3 3.0 %collective-permute-start.1 = (s16[49,16,128]{2,1,0:T(8,128)(2,1)S(1)}, s16[49,16,128]{2,1,0:T(8,128)(2,1)S(1)}, u32[]{:S(2)}, u32[]{:S(2)}) collective-permute-start(s16[49,16,128]{2,1,0:T(8,128)(2,1)S(1)} %get-tuple-element.24), channel_id=1, source_target_pairs={{0,2},{1,5},{2,0},{3,7},{4,6},{5,1},{6,4},{7,3},{8,10},{9,13},{10,... | collective-permute-start | bytes 602120 | tf_op jit(solution)/shard_map/ppermute | solution.py:213
  7.3 0.1 collective-permute-start.3
  7.4 0.0 copy-done
  7.4 1.6 %grad_own_columns.1 = (f32[4,96,256]{2,1,0:T(8,128)S(1)}, s16[49,16,128]{2,1,0:T(8,128)(2,1)S(1)}) custom-call(bf16[384,7168]{1,0:T(8,128)(2,1)S(1)} %bitcast.5, bf16[7168,256]{1,0:T(8,128)(2,1)S(1)} %get-tuple-element.25.factor), custom_call_target="tpu_custom_call" | custom-call | flops 1409286144 | bytes 16777216 | tf_op jit(solution)/shard_map/grad_own_columns/pallas_call | solution.py:234
  9.0 2.1 %collective-permute-start.4 = (s16[49,16,128]{2,1,0:T(8,128)(2,1)S(1)}, s16[49,16,128]{2,1,0:T(8,128)(2,1)S(1)}, u32[]{:S(2)}, u32[]{:S(2)}) collective-permute-start(s16[49,16,128]{2,1,0:T(8,128)(2,1)S(1)} %get-tuple-element.31), channel_id=1, source_target_pairs={{0,4},{1,3},{2,6},{3,1},{4,0},{5,7},{6,2},{7,5},{8,12},{9,11},{10,... | collective-permute-start | bytes 602120 | tf_op jit(solution)/shard_map/ppermute | solution.py:213
  11.1 0.0 collective-permute-done.1.message
  11.1 0.1 other_pair.1
  11.2 0.0 copy-start.1
  11.3 2.0 %collective-permute-start.2 = (s16[49,16,128]{2,1,0:T(8,128)(2,1)S(1)}, s16[49,16,128]{2,1,0:T(8,128)(2,1)S(1)}, u32[]{:S(2)}, u32[]{:S(2)}) collective-permute-start(s16[49,16,128]{2,1,0:T(8,128)(2,1)S(1)} %get-tuple-element.28), channel_id=1, source_target_pairs={{0,4},{1,3},{2,6},{3,1},{4,0},{5,7},{6,2},{7,5},{8,12},{9,11},{10,... | collective-permute-start | bytes 602120 | tf_op jit(solution)/shard_map/ppermute | solution.py:213
  13.3 0.0 collective-permute-done.5.factor
  13.3 1.6 %grad_other_columns.1.grad_other = f32[4,96,256]{2,1,0:T(8,128)S(1)} custom-call(bf16[384,7168]{1,0:T(8,128)(2,1)S(1)} %bitcast.6, bf16[7168,256]{1,0:T(8,128)(2,1)S(1)} %collective-permute-done.5.factor), custom_call_target="tpu_custom_call" | custom-call | flops 1409286144 | bytes 16777216 | tf_op jit(solution)/shard_map/grad_other_columns/pallas_call | solution.py:242
  14.9 0.0 collective-permute-done.3.act_message
  14.9 0.0 collective-permute-done.4.grad_message
  14.9 0.0 copy-done.1
  14.9 0.9 %own_scores.1 = (f32[8,128]{1,0:T(8,128)S(1)}, f32[4,96,256]{2,1,0:T(8,128)S(1)}) custom-call(s32[4]{0:T(128)S(1)} %copy-done.1, f32[4,96,256]{2,1,0:T(8,128)S(1)} %get-tuple-element.29.act_total, s16[49,16,128]{2,1,0:T(8,128)(2,1)S(1)} %collective-permute-done.3.act_message, f32[4,96,256]{2,1,0:T(8,128)S(1)} %get-tuple-element.26.refs_0_.grad_total, ...), custom_call_target="tpu_custom_call" | custom-call | bytes 8388608 | tf_op jit(solution)/shard_map/own_scores/pallas_call | solution.py:245
  15.8 1.2 %collective-permute-done.2.message = s16[49,16,128]{2,1,0:T(8,128)(2,1)S(1)} collective-permute-done((s16[49,16,128]{2,1,0:T(8,128)(2,1)S(1)}, s16[49,16,128]{2,1,0:T(8,128)(2,1)S(1)}, u32[]{:S(2)}, u32[]{:S(2)}) %collective-permute-start.2) | collective-permute-done | bytes 200736 | tf_op jit(solution)/shard_map/ppermute | solution.py:213
  17.0 0.2 other_scores.1
  17.3 0.2 collective-permute-start.6
  17.5 0.9 %collective-permute-done.6 = f32[8,128]{1,0:T(8,128)S(1)} collective-permute-done((f32[8,128]{1,0:T(8,128)S(1)}, f32[8,128]{1,0:T(8,128)S(1)}, u32[]{:S(2)}, u32[]{:S(2)}) %collective-permute-start.6) | collective-permute-done | bytes 4128 | tf_op jit(solution)/shard_map/ppermute | solution.py:36
  18.5 2.9 %collective-permute-start.9 = (f32[8,128]{1,0:T(8,128)S(1)}, f32[8,128]{1,0:T(8,128)S(1)}, u32[]{:S(2)}, u32[]{:S(2)}) collective-permute-start(f32[8,128]{1,0:T(8,128)S(1)} %add.15), channel_id=1, source_target_pairs={{0,7},{1,6},{2,5},{3,4},{4,3},{5,2},{6,1},{7,0},{8,15},{9,14},{10,... | collective-permute-start | bytes 12296 | tf_op jit(solution)/shard_map/ppermute | solution.py:36
  21.3 0.2 collective-permute-start.8
  21.6 0.1 collective-permute-start.7
  21.7 1.0 %collective-permute-done.9 = f32[8,128]{1,0:T(8,128)S(1)} collective-permute-done((f32[8,128]{1,0:T(8,128)S(1)}, f32[8,128]{1,0:T(8,128)S(1)}, u32[]{:S(2)}, u32[]{:S(2)}) %collective-permute-start.9) | collective-permute-done | bytes 4128 | tf_op jit(solution)/shard_map/ppermute | solution.py:36
  22.7 1.7 %collective-permute-done.8 = f32[8,128]{1,0:T(8,128)S(1)} collective-permute-done((f32[8,128]{1,0:T(8,128)S(1)}, f32[8,128]{1,0:T(8,128)S(1)}, u32[]{:S(2)}, u32[]{:S(2)}) %collective-permute-start.8) | collective-permute-done | bytes 4128 | tf_op jit(solution)/shard_map/ppermute | solution.py:36
  24.4 0.2 collective-permute-done.7
  24.6 2.5 %collective-permute-start.10 = (f32[8,128]{1,0:T(8,128)S(1)}, f32[8,128]{1,0:T(8,128)S(1)}, u32[]{:S(2)}, u32[]{:S(2)}) collective-permute-start(f32[8,128]{1,0:T(8,128)S(1)} %add_add_fusion), channel_id=1, source_target_pairs={{0,9},{1,8},{2,11},{3,10},{4,13},{5,12},{6,15},{7,14},{8,1},{9,0},... | collective-permute-start | bytes 12296 | tf_op jit(solution)/shard_map/ppermute | solution.py:36
  27.1 1.4 %collective-permute-done.10 = f32[8,128]{1,0:T(8,128)S(1)} collective-permute-done((f32[8,128]{1,0:T(8,128)S(1)}, f32[8,128]{1,0:T(8,128)S(1)}, u32[]{:S(2)}, u32[]{:S(2)}) %collective-permute-start.10) | collective-permute-done | bytes 4128 | tf_op jit(solution)/shard_map/ppermute | solution.py:36
  28.5 0.6 %add.19 = f32[8,128]{1,0:T(8,128)} add(f32[8,128]{1,0:T(8,128)S(1)} %add_add_fusion, f32[8,128]{1,0:T(8,128)S(1)} %collective-permute-done.10) | non-fusion elementwise | flops 1024 | bytes 12288 | tf_op jit(solution)/shard_map/add | solution.py:257
  (2 shorter events, 0.0 us)
Async XLA Ops:
  0.0 3.5 %collective-permute-start = (bf16[2048,256]{1,0:T(8,128)(2,1)}, bf16[2048,256]{1,0:T(8,128)(2,1)S(1)}, u32[]{:S(2)}, u32[]{:S(2)}) collective-permute-start(bf16[2048,256]{1,0:T(8,128)(2,1)} %bitcast.10), channel_id=1, source_target_pairs={{0,1},{1,0},{2,3},{3,2},{4,5},{5,4},{6,7},{7,6},{8,9},{9,8},{10,11... | collective-permute-start | bytes 3145736 | tf_op jit(solution)/shard_map/ppermute | solution.py:36
  0.5 6.9 %copy-start = (bf16[1,384,7168]{2,1,0:T(8,128)(2,1)S(1)}, bf16[1,384,7168]{2,1,0:T(8,128)(2,1)}, u32[]{:S(2)}) copy-start(bf16[1,384,7168]{2,1,0:T(8,128)(2,1)} %param.6) | copy-start | bytes 16515076
  3.5 9.8 %collective-permute-start.5 = (bf16[7168,256]{1,0:T(8,128)(2,1)}, bf16[7168,256]{1,0:T(8,128)(2,1)S(1)}, u32[]{:S(2)}, u32[]{:S(2)}) collective-permute-start(bf16[7168,256]{1,0:T(8,128)(2,1)} %bitcast.8), channel_id=1, source_target_pairs={{0,1},{1,0},{2,3},{3,2},{4,5},{5,4},{6,7},{7,6},{8,9},{9,8},{10,11... | collective-permute-start | bytes 11010056 | tf_op jit(solution)/shard_map/ppermute | solution.py:36
  4.3 6.8 %collective-permute-start.1 = (s16[49,16,128]{2,1,0:T(8,128)(2,1)S(1)}, s16[49,16,128]{2,1,0:T(8,128)(2,1)S(1)}, u32[]{:S(2)}, u32[]{:S(2)}) collective-permute-start(s16[49,16,128]{2,1,0:T(8,128)(2,1)S(1)} %get-tuple-element.24), channel_id=1, source_target_pairs={{0,2},{1,5},{2,0},{3,7},{4,6},{5,1},{6,4},{7,3},{8,10},{9,13},{10,... | collective-permute-start | bytes 602120 | tf_op jit(solution)/shard_map/ppermute | solution.py:213
  7.3 7.6 %collective-permute-start.3 = (s16[49,16,128]{2,1,0:T(8,128)(2,1)S(1)}, s16[49,16,128]{2,1,0:T(8,128)(2,1)S(1)}, u32[]{:S(2)}, u32[]{:S(2)}) collective-permute-start(s16[49,16,128]{2,1,0:T(8,128)(2,1)S(1)} %get-tuple-element.30), channel_id=1, source_target_pairs={{0,2},{1,5},{2,0},{3,7},{4,6},{5,1},{6,4},{7,3},{8,10},{9,13},{10,... | collective-permute-start | bytes 602120 | tf_op jit(solution)/shard_map/ppermute | solution.py:213
  9.0 5.9 %collective-permute-start.4 = (s16[49,16,128]{2,1,0:T(8,128)(2,1)S(1)}, s16[49,16,128]{2,1,0:T(8,128)(2,1)S(1)}, u32[]{:S(2)}, u32[]{:S(2)}) collective-permute-start(s16[49,16,128]{2,1,0:T(8,128)(2,1)S(1)} %get-tuple-element.31), channel_id=1, source_target_pairs={{0,4},{1,3},{2,6},{3,1},{4,0},{5,7},{6,2},{7,5},{8,12},{9,11},{10,... | collective-permute-start | bytes 602120 | tf_op jit(solution)/shard_map/ppermute | solution.py:213
  11.2 3.7 %copy-start.1 = (s32[4]{0:T(128)S(1)}, s32[4]{0:T(128)}, u32[]{:S(2)}) copy-start(s32[4]{0:T(128)} %lengths.1) | copy-start | bytes 52
  11.3 5.8 %collective-permute-start.2 = (s16[49,16,128]{2,1,0:T(8,128)(2,1)S(1)}, s16[49,16,128]{2,1,0:T(8,128)(2,1)S(1)}, u32[]{:S(2)}, u32[]{:S(2)}) collective-permute-start(s16[49,16,128]{2,1,0:T(8,128)(2,1)S(1)} %get-tuple-element.28), channel_id=1, source_target_pairs={{0,4},{1,3},{2,6},{3,1},{4,0},{5,7},{6,2},{7,5},{8,12},{9,11},{10,... | collective-permute-start | bytes 602120 | tf_op jit(solution)/shard_map/ppermute | solution.py:213
  17.3 1.2 %collective-permute-start.6 = (f32[8,128]{1,0:T(8,128)S(1)}, f32[8,128]{1,0:T(8,128)S(1)}, u32[]{:S(2)}, u32[]{:S(2)}) collective-permute-start(f32[8,128]{1,0:T(8,128)S(1)} %other_scores.1), channel_id=1, source_target_pairs={{0,1},{1,0},{2,3},{3,2},{4,5},{5,4},{6,7},{7,6},{8,9},{9,8},{10,11... | collective-permute-start | bytes 12296 | tf_op jit(solution)/shard_map/ppermute | solution.py:36
  18.5 4.2 %collective-permute-start.9 = (f32[8,128]{1,0:T(8,128)S(1)}, f32[8,128]{1,0:T(8,128)S(1)}, u32[]{:S(2)}, u32[]{:S(2)}) collective-permute-start(f32[8,128]{1,0:T(8,128)S(1)} %add.15), channel_id=1, source_target_pairs={{0,7},{1,6},{2,5},{3,4},{4,3},{5,2},{6,1},{7,0},{8,15},{9,14},{10,... | collective-permute-start | bytes 12296 | tf_op jit(solution)/shard_map/ppermute | solution.py:36
  21.3 3.0 %collective-permute-start.8 = (f32[8,128]{1,0:T(8,128)S(1)}, f32[8,128]{1,0:T(8,128)S(1)}, u32[]{:S(2)}, u32[]{:S(2)}) collective-permute-start(f32[8,128]{1,0:T(8,128)S(1)} %add.15), channel_id=1, source_target_pairs={{0,5},{1,4},{2,7},{3,6},{4,1},{5,0},{6,3},{7,2},{8,13},{9,12},{10,... | collective-permute-start | bytes 12296 | tf_op jit(solution)/shard_map/ppermute | solution.py:36
  21.6 3.0 %collective-permute-start.7 = (f32[8,128]{1,0:T(8,128)S(1)}, f32[8,128]{1,0:T(8,128)S(1)}, u32[]{:S(2)}, u32[]{:S(2)}) collective-permute-start(f32[8,128]{1,0:T(8,128)S(1)} %add.15), channel_id=1, source_target_pairs={{0,3},{1,2},{2,1},{3,0},{4,7},{5,6},{6,5},{7,4},{8,11},{9,10},{10,... | collective-permute-start | bytes 12296 | tf_op jit(solution)/shard_map/ppermute | solution.py:36
  24.6 3.9 %collective-permute-start.10 = (f32[8,128]{1,0:T(8,128)S(1)}, f32[8,128]{1,0:T(8,128)S(1)}, u32[]{:S(2)}, u32[]{:S(2)}) collective-permute-start(f32[8,128]{1,0:T(8,128)S(1)} %add_add_fusion), channel_id=1, source_target_pairs={{0,9},{1,8},{2,11},{3,10},{4,13},{5,12},{6,15},{7,14},{8,1},{9,0},... | collective-permute-start | bytes 12296 | tf_op jit(solution)/shard_map/ppermute | solution.py:36
